TPU v7x, 32 devices: a whole 2x2x4 slice. The times are simulated.
32 devices in a mesh: grp: 4 (over y, x), wide: 8 (over z, core).
Axes of the slice: x: 2, y: 2, z: 4, core: 2. Of those that a mesh axis runs over, the one named last changes fastest.
Arguments:
- tiles: bfloat16 [1536, 256, 256], P(('grp', 'wide')), may hold values from -0.59765625 to 0.59765625
- contraction: int32 [1536], P(('grp', 'wide')), may hold values from 0 to 15
- row_tile: int32 [1536], P(('grp', 'wide')), may hold values from 0 to 31, as said below
- owner_map: int32 [32], replicated, may hold values from 0 to 31, as said below
- panel: bfloat16 [4096, 768], P('grp'), may hold values from -0.5390625 to 0.5390625
Outputs:
- column_block: float32 [8192, 768], P('wide')
Inputs may be any that keep to these rules, and one draw needn't show every extreme that they name: `row_tile`: every row tile's owner is owner_map // 4; among the 48 contributions of one device at most 16 have row tiles of one owner, and on every device some owner gets exactly 16. `owner_map`: A permutation of the row tiles.
All inputs are finite; a program needn't handle non-finite values.
Results may differ from a plain program's by a relative error of at most 0.0003.
Values may be sent and summed in bfloat16 or wider, within the bound.
No kernel may reach another device: no remote copies, remote signals or barrier semaphores. Data moves between devices by JAX's collectives and lax.ppermute only.
A program may use at most 192 MiB of HBM per device.

v0:
```python
import functools
import math

import jax
import jax.numpy as jnp
from jax import lax
from jax.experimental import pallas as pl
from jax.experimental.pallas import tpu as pltpu
from jax.sharding import PartitionSpec as P

MIB = 1024 * 1024
CODE_ROWS = 16
CODE_STEPS = 256.0
TOP = 32000.0
CHUNK = 256
UNROLL = 8
LOG2 = math.log(2.0)


def place_slots(row_ids, owner_map, out_dev):
    table_ids = jnp.arange(owner_map.shape[0], dtype=jnp.int32)
    position = jnp.sum(jnp.where(row_ids[..., None] == table_ids, owner_map, 0), axis=-1)
    target = position // out_dev
    serial = jnp.arange(row_ids.shape[-1], dtype=jnp.int32)
    earlier = (target[..., :, None] == target[..., None, :]) & (serial[:, None] > serial[None, :])
    ranking = jnp.sum(earlier.astype(jnp.int32), axis=-1)
    return (position % out_dev, target, ranking)


def add_products(summed, arrived, slot_labels, panel_tiles):
    slot_count = arrived.shape[0]
    block_rows = math.gcd(slot_count, 32)
    out_dev = summed.shape[0]
    local_ids = jnp.arange(out_dev, dtype=jnp.int32)

    def one_block(which_block, running, source_tiles, source_labels):
        part_tiles = lax.dynamic_slice_in_dim(source_tiles, which_block * block_rows, block_rows, 0)
        part_labels = lax.dynamic_slice_in_dim(
            source_labels, which_block * block_rows, block_rows, 0
        )
        chosen = jnp.take(panel_tiles, part_labels[:, 1], axis=0)
        products = jnp.einsum(
            "sab,sbc->sac", part_tiles, chosen, preferred_element_type=jnp.float32
        )
        row_hits = (part_labels[:, 0][:, None] == local_ids[None, :]).astype(jnp.float32)
        return running + jnp.einsum(
            "sr,sac->rac", row_hits, products, precision=lax.Precision.HIGHEST
        )

    return lax.fori_loop(
        0,
        slot_count // block_rows,
        lambda which_block, running: one_block(which_block, running, arrived, slot_labels),
        summed,
    )


def slots_plan(tiles, contraction, row_tile, owner_map, panel):
    wide_count = lax.axis_size("wide")
    tile_dev = tiles.shape[0]
    tile_side = tiles.shape[1]
    out_dev = owner_map.shape[0] // wide_count
    most_slots = tile_dev * 8 // (3 * wide_count)
    slot_total = wide_count * most_slots
    local_row, target, ranking = place_slots(row_tile, owner_map, out_dev)
    slot_index = target * most_slots + ranking
    outgoing = jnp.zeros((slot_total, tile_side, tile_side), tiles.dtype).at[slot_index].set(tiles)
    all_rows, all_contraction = (
        lax.all_gather(row_tile, "wide", axis=0, tiled=True),
        lax.all_gather(contraction, "wide", axis=0, tiled=True),
    )
    all_rows = all_rows.reshape(wide_count, tile_dev)
    all_contraction = all_contraction.reshape(wide_count, tile_dev)
    source_local, source_target, source_rank = place_slots(all_rows, owner_map, out_dev)
    source_ids = jnp.arange(wide_count, dtype=jnp.int32)
    mine = source_target == lax.axis_index("wide")
    arrive_index = jnp.where(mine, source_ids[:, None] * most_slots + source_rank, slot_total)
    label_pairs = jnp.stack([source_local, all_contraction], axis=-1).reshape(
        wide_count * tile_dev, 2
    )
    vacant_label = jnp.stack(
        [jnp.full((slot_total,), out_dev, jnp.int32), jnp.zeros((slot_total,), jnp.int32)], axis=1
    )
    arrived_labels = vacant_label.at[arrive_index.reshape(-1)].set(label_pairs, mode="drop")
    gathered = lax.all_gather(panel, "grp", axis=0, tiled=True)
    panel_tiles = gathered.reshape(gathered.shape[0] // tile_side, tile_side, gathered.shape[1])
    summed = jnp.zeros((out_dev, tile_side, gathered.shape[1]), jnp.float32)
    arrived = lax.all_to_all(outgoing, "wide", split_axis=0, concat_axis=0, tiled=True)
    summed = add_products(summed, arrived, arrived_labels, panel_tiles)
    summed = lax.psum(summed, "grp")
    return summed.reshape(out_dev * tile_side, gathered.shape[1])


def encode(value):
    largest = jnp.max(jnp.abs(value), axis=0, keepdims=True)
    code = jnp.ceil(jnp.log(jnp.maximum(largest, 1e-30)) * (CODE_STEPS / LOG2))
    scale = jnp.exp(code * (-LOG2 / CODE_STEPS)) * TOP
    whole = jnp.round(value * scale).astype(jnp.int32).astype(jnp.int16)
    return whole, code.astype(jnp.int32)


def put_encoded(ref, value):
    side = value.shape[0]
    whole, code = encode(value)
    ref[pl.ds(0, side), :] = whole
    ref[pl.ds(side, CODE_ROWS), :] = jnp.broadcast_to(
        code, (CODE_ROWS, code.shape[1])
    ).astype(jnp.int16)


def get_decoded(ref, side):
    code = ref[pl.ds(side, CODE_ROWS), :].astype(jnp.int32).astype(jnp.float32)[:1]
    scale = jnp.exp(code * (LOG2 / CODE_STEPS)) * (1.0 / TOP)
    return ref[pl.ds(0, side), :].astype(jnp.int32).astype(jnp.float32) * scale


def here():
    g, w = lax.axis_index("grp"), lax.axis_index("wide")
    return g % 2, g // 2, (w // 2) % 2, w // 4


def hold_kernel(
    order, own_ref, sib_ref, own_tiles, sib_tiles,
    count_ref, plane_ref, line_ref, label_ref, out, sems,
):
    tile_dev = own_tiles.shape[0]
    sums = (own_ref.shape[0] - 2 * tile_dev) // 2
    shard, out_dev = 4, 4
    x, y, z_low, _ = here()
    g, core = lax.axis_index("grp"), lax.axis_index("wide") % 2

    def copy(tiles, which, at):
        return pltpu.make_async_copy(tiles.at[which], out.at[at], sems.at[at])

    def scan(tiles, index_ref, count):
        def one(i, count):
            position = own_ref[2 * tile_dev + index_ref[i]]
            k = index_ref[tile_dev + i]
            owner, local = lax.div(position, out_dev), lax.rem(position, out_dev)
            match = lax.rem(owner, 2) == core

            @pl.when(match)
            def _():
                copy(tiles, i, count).start()
                odd, to_z = lax.rem(lax.div(owner, 2), 2), lax.div(owner, 4)
                bit_x, bit_y = lax.rem(local, 2), lax.div(local, 2)
                first = jnp.where(odd == 1, bit_y == y, bit_x == x)
                second = jnp.where(odd == 1, bit_x, bit_y)
                plane_ref[count] = (
                    jnp.where(first, 0, sums // 2) + odd * (sums // 4) + 2 * to_z + second
                )
                line_ref[count] = (
                    jnp.where(odd == z_low, 0, sums // 2) + to_z * out_dev + local
                )
                apart, inner = lax.div(k, shard) ^ g, lax.rem(k, shard)
                half = shard // 2
                crossed = jnp.where(lax.div(inner, half) == core, 0, half) + lax.rem(inner, half)
                label_ref[count] = jnp.where(apart == 0, inner, apart * shard + crossed)

            return count + match.astype(jnp.int32)

        return lax.fori_loop(0, tile_dev, one, count)

    count = scan(own_tiles, own_ref, 0)
    count = scan(sib_tiles, sib_ref, count)
    count_ref[0] = count
    for i in range(UNROLL):
        plane_ref[count + i] = sums
        line_ref[count + i] = sums
        label_ref[count + i] = 0

    @pl.loop(0, count)
    def _(i):
        copy(own_tiles, 0, i).wait()


def join_kernel(order, *refs):
    *parts, out = refs
    rows = parts[0].shape[0]
    for i, part in enumerate(parts):
        out[pl.ds(i * rows, rows), :] = part[...]


def products_kernel(
    fill, chunk, order, count_ref, slot_ref, label_ref, tiles, own_panel, *refs
):
    parts = refs[: 1 + max(which for which, _, _ in fill)]
    *sends, sums, stack = refs[len(parts) :]
    side, width = stack.shape[1:]
    for t in range(own_panel.shape[0] // side):
        stack[t] = own_panel[pl.ds(t * side, side), pl.ds(chunk * width, width)]
    for which, t, at in fill:
        stack[at] = parts[which][pl.ds(t * side, side), :]

    @pl.loop(0, sums.shape[0])
    def _(i):
        sums[i] = jnp.zeros(sums.shape[1:], jnp.float32)

    @pl.loop(0, lax.div(count_ref[0] + UNROLL - 1, UNROLL))
    def _(i):
        found = [
            jnp.dot(
                tiles[i * UNROLL + u],
                stack[label_ref[i * UNROLL + u]],
                preferred_element_type=jnp.float32,
            )
            for u in range(UNROLL)
        ]
        for u in range(UNROLL):
            sums[slot_ref[i * UNROLL + u]] += found[u]

    sent = sums.shape[0] // 2
    for send in sends:

        @pl.loop(0, send.shape[0])
        def _(i, send=send, sent=sent):
            put_encoded(send.at[i], sums[sent + i])

        sent += send.shape[0]


def plane_kernel(order, recv_a, recv_b, kept, send_a, send_b, keep):
    side, half = kept.shape[1], send_a.shape[0]
    x, y, _, _ = here()
    for base, bit, recv, send in ((0, y, recv_a, send_a), (1, x, recv_b, send_b)):

        @pl.loop(0, half)
        def _(i, base=base, bit=bit, recv=recv, send=send):
            other, mine = 2 * i + 1 - bit, 2 * i + bit
            at = base * 2 * half
            put_encoded(send.at[i], kept[at + other] + get_decoded(recv.at[other], side))
            keep[base * half + i] = kept[at + mine] + get_decoded(recv.at[mine], side)


def owner_kernel(order, recv_a, recv_b, kept, send, keep):
    side, half = kept.shape[1], send.shape[0]
    odd = here()[2]

    @pl.loop(0, half)
    def _(i):
        value_a = kept[i] + get_decoded(recv_a.at[i], side)
        value_b = kept[half + i] + get_decoded(recv_b.at[i], side)
        put_encoded(send.at[i], jnp.where(odd == 1, value_a, value_b))
        keep[i] = jnp.where(odd == 1, value_b, value_a)


def rows_kernel(order, recv, kept, send_a, send_b):
    side, half = kept.shape[1], send_a.shape[0]
    for i in range(2 * half):
        put_encoded(
            (send_a, send_b)[i // half].at[i % half], kept[i] + get_decoded(recv.at[i], side)
        )


def swap_kernel(order, own_a, own_b, recv_a, recv_b, send_a, send_b):
    side = own_a.shape[1] - CODE_ROWS
    for own, recv, send in ((own_a, recv_a, send_a), (own_b, recv_b, send_b)):
        for i in range(own.shape[0]):
            put_encoded(send.at[i], get_decoded(own.at[i], side) + get_decoded(recv.at[i], side))


def line_kernel(order, recv, kept, send, keep):
    side, half = kept.shape[1], send.shape[0]
    bit = here()[3]

    @pl.loop(0, half)
    def _(i):
        other, mine = (1 - bit) * half + i, bit * half + i
        put_encoded(send.at[i], kept[other] + get_decoded(recv.at[other], side))
        keep[i] = kept[mine] + get_decoded(recv.at[mine], side)


def finish_kernel(order, recv, kept, out):
    put_encoded(out, kept[0] + get_decoded(recv.at[0], kept.shape[1]))


def spread_kernel(chunk, order, *refs):
    blocks, (out, rows, sems) = refs[:4], refs[-3:]
    side, width = rows.shape[1:]
    x, y, _, _ = here()
    halves = len(blocks[0].shape) == 3
    copies = []
    for i in range(4):
        if halves:
            own, recv = blocks[i // 2].at[i % 2], blocks[2 + i // 2].at[i % 2]
            rows[i] = get_decoded(own, side) + get_decoded(recv, side)
            at = i * side
        else:
            rows[i] = get_decoded(blocks[i], side)
            at = pl.multiple_of(((2 * y + x) ^ i) * side, side)
        copies.append(
            pltpu.make_async_copy(
                rows.at[i], out.at[pl.ds(at, side), pl.ds(chunk * width, width)], sems.at[i]
            )
        )
        copies[-1].start()
    for copy in copies:
        copy.wait()


def in_vmem(count):
    return [pl.BlockSpec(memory_space=pltpu.VMEM)] * count


def in_smem(count):
    return [pl.BlockSpec(memory_space=pltpu.SMEM)] * count


def in_any(count):
    return [pl.BlockSpec(memory_space=pl.ANY)] * count


def shape(dims, kind):
    return jax.ShapeDtypeStruct(dims, kind)


def params(mib):
    return pltpu.CompilerParams(vmem_limit_bytes=mib * MIB)


def cost(flops, moved):
    return pl.CostEstimate(flops=flops, bytes_accessed=moved, transcendentals=0)


def sums_plan(tiles, contraction, row_tile, owner_map, panel):
    wide_count = lax.axis_size("wide")
    tile_dev, side = tiles.shape[0], tiles.shape[1]
    out_dev = owner_map.shape[0] // wide_count
    rows, columns = panel.shape
    shard = rows // side
    chunks = columns // CHUNK
    sums = owner_map.shape[0] // 2
    core = lax.axis_index("wide") % 2

    def to_core(v):
        return lax.ppermute(v, "wide", [(i, i ^ 1) for i in range(wide_count)])

    def to_grp(v, d):
        return lax.ppermute(v, "grp", [(i, i ^ d) for i in range(4)])

    def to_line(v, b):
        return lax.ppermute(v, "wide", [(i, i ^ (2 << b)) for i in range(wide_count)])


    own_index = jnp.concatenate([row_tile, contraction, owner_map])
    sib_index = to_core(own_index)
    sib_tiles = to_core(tiles)

    def own_half(source, j):
        return lax.dynamic_slice(source, (core * (rows // 2), j * CHUNK), (rows // 2, CHUNK))

    mines = [own_half(panel, j) for j in range(chunks)]
    ways = [None, (1, 2), (2, 1)]
    firsts = [None] + [to_grp(mines[j], ways[j][0]) for j in range(1, chunks)]
    mine, sib_index = lax.optimization_barrier((mines[0], sib_index))
    near = [to_grp(mine, 1), to_grp(mine, 2), to_grp(mines[0], 3)]

    half, quarter = sums // 2, sums // 4
    coded = shape((side + CODE_ROWS, CHUNK), jnp.int16)
    plain = shape((side, CHUNK), jnp.float32)

    def stack_of(count, one):
        return shape((count, *one.shape), one.dtype)

    order = jnp.zeros((1,), jnp.int32)
    last = None

    def in_order():
        return order if last is None else lax.optimization_barrier((order, last))[0]

    def call(body, name, outs, *args, smem=0, mib=16, extra=(), **more):
        nonlocal last
        done = pl.pallas_call(
            body,
            in_specs=more.pop("in_specs", in_any(1) + in_smem(smem) + in_vmem(len(args) - smem)),
            out_specs=more.pop("out_specs", in_vmem(len(outs))),
            out_shape=outs,
            scratch_shapes=list(extra),
            compiler_params=params(mib),
            cost_estimate=cost(0, sum(math.prod(a.shape) * a.dtype.itemsize for a in args)),
            name=name,
            **more,
        )(in_order(), *args)
        last = done[0]
        return done

    def places(operand, tiles_of, first):
        return [
            (operand, t, d * shard + first + i % part)
            for i, (t, d) in enumerate((t, d) for d, ts in tiles_of for t in ts)
        ]

    part = shard // 2

    def join(j):
        (joined,) = call(join_kernel, "join", [shape((3 * rows // 2, CHUNK), panel.dtype)], *near)
        tiles_of = [(d, range((d - 1) * part, d * part)) for d in (1, 2, 3)]
        fill = places(0, tiles_of, 0) + places(1, tiles_of, part)
        return fill, [joined, to_core(joined)]

    def pair(j):
        way, other = ways[j]
        (joined,) = call(
            join_kernel, "join", [shape((rows, CHUNK), panel.dtype)], mines[j], firsts[j]
        )
        second = to_grp(joined, other)
        in_first = [(way, range(part, 2 * part))]
        in_second = [(other, range(part)), (way ^ other, range(part, 2 * part))]
        fill = (
            places(0, in_first, 0)
            + places(1, in_first, part)
            + places(2, in_second, 0)
            + places(3, in_second, part)
        )
        return fill, [joined, to_core(joined), second, to_core(second)]

    def products(j, slot, sends, fill, parts):
        *sends, kept = call(
            functools.partial(products_kernel, tuple(fill), j),
            "products",
            [*sends, stack_of(sums + 1, plain)],
            counts,
            slot,
            label,
            held,
            panel,
            *parts,
            smem=3,
            extra=[pltpu.VMEM((4 * shard, side, CHUNK), panel.dtype)],
            mib=24,
        )
        return *sends, kept

    def gathered(done):
        return [done] + [to_grp(done, d) for d in (1, 2, 3)]

    def spread(j, blocks, result):
        earlier = [] if result is None else [result]
        return call(
            functools.partial(spread_kernel, j),
            "spread",
            [shape((out_dev * side, columns), jnp.float32)],
            *blocks,
            *earlier,
            in_specs=in_any(1) + in_vmem(4) + in_any(len(earlier)),
            out_specs=in_any(1),
            input_output_aliases={5: 0} if earlier else {},
            extra=[pltpu.VMEM((4, side, CHUNK), jnp.float32), pltpu.SemaphoreType.DMA((4,))],
        )[0]

    eighth = quarter // 2
    entries = shape((2 * tile_dev + UNROLL,), jnp.int32)
    counts, in_plane, in_line, label, held = call(
        hold_kernel,
        "hold",
        [shape((1,), jnp.int32)]
        + [entries] * 3
        + [pltpu.VMEM((2 * tile_dev + UNROLL, side, side), tiles.dtype)],
        own_index,
        sib_index,
        *[pltpu.with_memory_space_constraint(v, pltpu.HBM) for v in (tiles, sib_tiles)],
        in_specs=in_any(1) + in_smem(2) + in_any(2),
        out_specs=in_smem(4) + in_vmem(1),
        extra=[pltpu.SemaphoreType.DMA((2 * tile_dev,))],
        mib=8,
    )
    last = held
    pairs = {j: pair(j) for j in (1, 2)}

    send, keep_0 = products(0, in_line, [stack_of(half, coded)], *join(0))
    sent_0 = send
    sent, keep = {}, {}
    for j in (1, 2):
        send_a, send_b, keep[j] = products(j, in_plane, [stack_of(quarter, coded)] * 2, *pairs[j])
        sent[j] = send_a, send_b

    sent_0, keep_0 = call(
        line_kernel,
        "line",
        [stack_of(quarter, coded), stack_of(quarter, plain)],
        to_line(sent_0, 0),
        keep_0,
    )

    def plane(j):
        return call(
            plane_kernel,
            "plane",
            [stack_of(eighth, coded)] * 2 + [stack_of(quarter, plain)],
            to_grp(sent[j][0], 1),
            to_grp(sent[j][1], 2),
            keep[j],
        )

    def owner(j):
        return call(
            owner_kernel,
            "owner",
            [stack_of(eighth, coded), stack_of(eighth, plain)],
            to_grp(sent[j][0], 2),
            to_grp(sent[j][1], 1),
            keep[j],
        )

    *sent[1], keep[1] = plane(1)
    *sent[2], keep[2] = plane(2)
    sent[1], keep[1] = owner(1)
    pair_of = [stack_of(2, coded)] * 2
    own_a, own_b = call(rows_kernel, "rows", pair_of, to_line(sent_0, 1), keep_0)
    sent[2], keep[2] = owner(2)

    def line(j):
        return call(
            line_kernel,
            "line",
            [stack_of(1, coded), stack_of(1, plain)],
            to_line(sent[j], 0),
            keep[j],
        )

    def finish(j):
        return call(finish_kernel, "finish", [coded], to_line(sent[j], 1), keep[j])[0]

    sent[1], keep[1] = line(1)
    own_a, own_b = call(
        swap_kernel, "swap", pair_of, own_a, own_b, to_grp(own_a, 1), to_grp(own_b, 2)
    )
    done_1 = finish(1)
    sent[2], keep[2] = line(2)
    result = spread(0, [own_a, own_b, to_grp(own_a, 2), to_grp(own_b, 1)], None)
    done_2 = finish(2)
    result = spread(1, gathered(done_1), result)
    return spread(2, gathered(done_2), result)


def per_device(tiles, contraction, row_tile, owner_map, panel):
    dense = owner_map.shape[0] <= tiles.shape[0]
    wide_count = lax.axis_size("wide")
    fits = lax.axis_size("grp") == 4 and wide_count >= 4 and wide_count & (wide_count - 1) == 0
    out_dev = owner_map.shape[0] // wide_count
    if dense and fits and wide_count == 8 and out_dev == 4 and panel.shape[1] == 3 * CHUNK:
        return sums_plan(tiles, contraction, row_tile, owner_map, panel)
    return slots_plan(tiles, contraction, row_tile, owner_map, panel)


def solution(mesh):
    return jax.shard_map(
        per_device,
        mesh=mesh,
        in_specs=(
            P(("grp", "wide"), None, None),
            P(("grp", "wide")),
            P(("grp", "wide")),
            P(),
            P("grp", None),
        ),
        out_specs=P("wide", None),
        check_vma=False,
    )
```

profile of v0, /device:TPU:0, one launch (start us, length us, event | category | flops | bytes accessed | tf_op | source)
XLA Modules:
  0.0 122.8 jit_solution(5569825506922005990)
XLA Ops:
  2.4 3.0 %collective-permute-start.2 = (bf16[512,256]{1,0:T(8,128)(2,1)S(1)}, bf16[512,256]{1,0:T(8,128)(2,1)S(1)}, u32[]{:S(2)}, u32[]{:S(2)}) collective-permute-start(bf16[512,256]{1,0:T(8,128)(2,1)S(1)} %get-tuple-element.116.refs_0_), channel_id=1, source_target_pairs={{0,8},{8,0},{16,24},{24,16},{1,9},{9,1},{17,25},{25,17},{2,10},{10... | collective-permute-start | bytes 786440 | tf_op jit(solution)/shard_map/ppermute | solution.py:339
  7.0 3.1 %collective-permute-done.sib_ref = s32[128]{0:T(128)S(1)} collective-permute-done((s32[128]{0:T(128)S(1)}, s32[128]{0:T(128)S(1)}, u32[]{:S(2)}, u32[]{:S(2)}) %collective-permute-start) | collective-permute-done | bytes 544 | tf_op jit(solution)/shard_map/ppermute | solution.py:336
  10.1 2.6 %collective-permute-start.5 = (bf16[512,256]{1,0:T(8,128)(2,1)S(1)}, bf16[512,256]{1,0:T(8,128)(2,1)S(1)}, u32[]{:S(2)}, u32[]{:S(2)}) collective-permute-start(bf16[512,256]{1,0:T(8,128)(2,1)S(1)} %get-tuple-element.65), channel_id=1, source_target_pairs={{0,16},{8,24},{16,0},{24,8},{1,17},{9,25},{17,1},{25,9},{2,18},{10... | collective-permute-start | bytes 786440 | tf_op jit(solution)/shard_map/ppermute | solution.py:339
  14.3 6.4 %hold.1 = (s32[1]{0:T(128)}, s32[104]{0:T(128)S(1)}, s32[104]{0:T(128)S(1)}, s32[104]{0:T(128)S(1)}, bf16[104,256,256]{2,1,0:T(8,128)(2,1)S(1)}) custom-call(s32[1]{0:T(128)} %constant.8.clone.1.order, s32[128]{0:T(128)S(1)} %pad_add_fusion.own_ref, s32[128]{0:T(128)S(1)} %collective-permute-done.sib_ref, bf16[48,256,256]{2,1,0:T(8,128)(2,1)} %own_tiles.1, ...), custom_call_target="tpu_custom_call" | custom-call | bytes 12583936 | tf_op jit(solution)/shard_map/hold/pallas_call | solution.py:373
  20.8 3.9 %collective-permute-done.5.refs_1_ = bf16[512,256]{1,0:T(8,128)(2,1)S(1)} collective-permute-done((bf16[512,256]{1,0:T(8,128)(2,1)S(1)}, bf16[512,256]{1,0:T(8,128)(2,1)S(1)}, u32[]{:S(2)}, u32[]{:S(2)}) %collective-permute-start.5) | collective-permute-done | bytes 262176 | tf_op jit(solution)/shard_map/ppermute | solution.py:339
  27.1 4.5 %products.3 = (s16[8,272,256]{2,1,0:T(8,128)(2,1)S(1)}, f32[17,256,256]{2,1,0:T(8,128)S(1)}) custom-call(s32[1]{0:T(128)} %constant.8.clone.1.order, s32[1]{0:T(128)} %get-tuple-element.67.count_ref, s32[104]{0:T(128)S(1)} %get-tuple-element.68.slot_ref, s32[104]{0:T(128)S(1)} %get-tuple-element.69.label_ref, ...), custom_call_target="tpu_custom_call" | custom-call | bytes 16778052 | tf_op jit(solution)/shard_map/products/pallas_call | solution.py:373
  32.3 3.2 %collective-permute-start.8 = (bf16[1024,256]{1,0:T(8,128)(2,1)S(1)}, bf16[1024,256]{1,0:T(8,128)(2,1)S(1)}, u32[]{:S(2)}, u32[]{:S(2)}) collective-permute-start(bf16[1024,256]{1,0:T(8,128)(2,1)S(1)} %join.3.refs_0_), channel_id=1, source_target_pairs={{0,1},{1,0},{2,3},{3,2},{4,5},{5,4},{6,7},{7,6},{8,9},{9,8},{10,11... | collective-permute-start | bytes 1572872 | tf_op jit(solution)/shard_map/ppermute | solution.py:336
  35.4 3.7 %collective-permute-done.9.refs_2_ = bf16[1024,256]{1,0:T(8,128)(2,1)S(1)} collective-permute-done((bf16[1024,256]{1,0:T(8,128)(2,1)S(1)}, bf16[1024,256]{1,0:T(8,128)(2,1)S(1)}, u32[]{:S(2)}, u32[]{:S(2)}) %collective-permute-start.9) | collective-permute-done | bytes 524320 | tf_op jit(solution)/shard_map/ppermute | solution.py:339
  41.0 4.5 %products.4 = (s16[4,272,256]{2,1,0:T(8,128)(2,1)S(1)}, s16[4,272,256]{2,1,0:T(8,128)(2,1)S(1)}, f32[17,256,256]{2,1,0:T(8,128)S(1)}) custom-call(s32[1]{0:T(128)} %constant.8.clone.1.order, s32[1]{0:T(128)} %get-tuple-element.67.count_ref, s32[104]{0:T(128)S(1)} %get-tuple-element.72.slot_ref, s32[104]{0:T(128)S(1)} %get-tuple-element.69.label_ref, ...), custom_call_target="tpu_custom_call" | custom-call | bytes 17302340 | tf_op jit(solution)/shard_map/products/pallas_call | solution.py:373
  45.5 2.1 %collective-permute-start.16 = (s16[4,272,256]{2,1,0:T(8,128)(2,1)S(1)}, s16[4,272,256]{2,1,0:T(8,128)(2,1)S(1)}, u32[]{:S(2)}, u32[]{:S(2)}) collective-permute-start(s16[4,272,256]{2,1,0:T(8,128)(2,1)S(1)} %get-tuple-element.80), channel_id=1, source_target_pairs={{0,16},{8,24},{16,0},{24,8},{1,17},{9,25},{17,1},{25,9},{2,18},{10... | collective-permute-start | bytes 1671176 | tf_op jit(solution)/shard_map/ppermute | solution.py:339
  48.1 4.5 %products.5 = (s16[4,272,256]{2,1,0:T(8,128)(2,1)S(1)}, s16[4,272,256]{2,1,0:T(8,128)(2,1)S(1)}, f32[17,256,256]{2,1,0:T(8,128)S(1)}) custom-call(s32[1]{0:T(128)} %constant.8.clone.1.order, s32[1]{0:T(128)} %get-tuple-element.67.count_ref, s32[104]{0:T(128)S(1)} %get-tuple-element.72.slot_ref, s32[104]{0:T(128)S(1)} %get-tuple-element.69.label_ref, ...), custom_call_target="tpu_custom_call" | custom-call | bytes 17302340 | tf_op jit(solution)/shard_map/products/pallas_call | solution.py:373
  54.8 2.9 %collective-permute-done.14.recv = s16[8,272,256]{2,1,0:T(8,128)(2,1)S(1)} collective-permute-done((s16[8,272,256]{2,1,0:T(8,128)(2,1)S(1)}, s16[8,272,256]{2,1,0:T(8,128)(2,1)S(1)}, u32[]{:S(2)}, u32[]{:S(2)}) %collective-permute-start.14) | collective-permute-done | bytes 1114144 | tf_op jit(solution)/shard_map/ppermute | solution.py:342
  58.3 2.7 %collective-permute-start.21 = (s16[4,272,256]{2,1,0:T(8,128)(2,1)S(1)}, s16[4,272,256]{2,1,0:T(8,128)(2,1)S(1)}, u32[]{:S(2)}, u32[]{:S(2)}) collective-permute-start(s16[4,272,256]{2,1,0:T(8,128)(2,1)S(1)} %get-tuple-element.78), channel_id=1, source_target_pairs={{0,4},{1,5},{2,6},{3,7},{4,0},{5,1},{6,2},{7,3},{8,12},{9,13},{10,... | collective-permute-start | bytes 1671176 | tf_op jit(solution)/shard_map/ppermute | solution.py:342
  60.9 2.1 %collective-permute-done.15.recv_a = s16[4,272,256]{2,1,0:T(8,128)(2,1)S(1)} collective-permute-done((s16[4,272,256]{2,1,0:T(8,128)(2,1)S(1)}, s16[4,272,256]{2,1,0:T(8,128)(2,1)S(1)}, u32[]{:S(2)}, u32[]{:S(2)}) %collective-permute-start.15) | collective-permute-done | bytes 557088 | tf_op jit(solution)/shard_map/ppermute | solution.py:339
  64.7 7.8 %collective-permute-done.18.recv_b = s16[4,272,256]{2,1,0:T(8,128)(2,1)S(1)} collective-permute-done((s16[4,272,256]{2,1,0:T(8,128)(2,1)S(1)}, s16[4,272,256]{2,1,0:T(8,128)(2,1)S(1)}, u32[]{:S(2)}, u32[]{:S(2)}) %collective-permute-start.18) | collective-permute-done | bytes 557088 | tf_op jit(solution)/shard_map/ppermute | solution.py:339
  72.5 2.4 %collective-permute-done.17.recv_a = s16[4,272,256]{2,1,0:T(8,128)(2,1)S(1)} collective-permute-done((s16[4,272,256]{2,1,0:T(8,128)(2,1)S(1)}, s16[4,272,256]{2,1,0:T(8,128)(2,1)S(1)}, u32[]{:S(2)}, u32[]{:S(2)}) %collective-permute-start.17) | collective-permute-done | bytes 557088 | tf_op jit(solution)/shard_map/ppermute | solution.py:339
  76.7 4.3 %collective-permute-done.20.recv_b = s16[2,272,256]{2,1,0:T(8,128)(2,1)S(1)} collective-permute-done((s16[2,272,256]{2,1,0:T(8,128)(2,1)S(1)}, s16[2,272,256]{2,1,0:T(8,128)(2,1)S(1)}, u32[]{:S(2)}, u32[]{:S(2)}) %collective-permute-start.20) | collective-permute-done | bytes 278560 | tf_op jit(solution)/shard_map/ppermute | solution.py:339
  82.9 3.4 %collective-permute-done.21.recv = s16[4,272,256]{2,1,0:T(8,128)(2,1)S(1)} collective-permute-done((s16[4,272,256]{2,1,0:T(8,128)(2,1)S(1)}, s16[4,272,256]{2,1,0:T(8,128)(2,1)S(1)}, u32[]{:S(2)}, u32[]{:S(2)}) %collective-permute-start.21) | collective-permute-done | bytes 557088 | tf_op jit(solution)/shard_map/ppermute | solution.py:342
  86.6 3.1 %collective-permute-start.26 = (s16[2,272,256]{2,1,0:T(8,128)(2,1)S(1)}, s16[2,272,256]{2,1,0:T(8,128)(2,1)S(1)}, u32[]{:S(2)}, u32[]{:S(2)}) collective-permute-start(s16[2,272,256]{2,1,0:T(8,128)(2,1)S(1)} %get-tuple-element.102.own_b), channel_id=1, source_target_pairs={{0,16},{8,24},{16,0},{24,8},{1,17},{9,25},{17,1},{25,9},{2,18},{10... | collective-permute-start | bytes 835592 | tf_op jit(solution)/shard_map/ppermute | solution.py:339
  90.5 2.2 %collective-permute-done.24.recv = s16[2,272,256]{2,1,0:T(8,128)(2,1)S(1)} collective-permute-done((s16[2,272,256]{2,1,0:T(8,128)(2,1)S(1)}, s16[2,272,256]{2,1,0:T(8,128)(2,1)S(1)}, u32[]{:S(2)}, u32[]{:S(2)}) %collective-permute-start.24) | collective-permute-done | bytes 278560 | tf_op jit(solution)/shard_map/ppermute | solution.py:342
  99.8 2.6 %collective-permute-done.27.recv = s16[1,272,256]{2,1,0:T(8,128)(2,1)S(1)} collective-permute-done((s16[1,272,256]{2,1,0:T(8,128)(2,1)S(1)}, s16[1,272,256]{2,1,0:T(8,128)(2,1)S(1)}, u32[]{:S(2)}, u32[]{:S(2)}) %collective-permute-start.27) | collective-permute-done | bytes 139296 | tf_op jit(solution)/shard_map/ppermute | solution.py:342
  102.7 2.5 %collective-permute-start.34 = (s16[272,256]{1,0:T(8,128)(2,1)S(1)}, s16[272,256]{1,0:T(8,128)(2,1)S(1)}, u32[]{:S(2)}, u32[]{:S(2)}) collective-permute-start(s16[272,256]{1,0:T(8,128)(2,1)S(1)} %finish.2.refs_0_), channel_id=1, source_target_pairs={{0,24},{8,16},{16,8},{24,0},{1,25},{9,17},{17,9},{25,1},{2,26},{10... | collective-permute-start | bytes 417800 | tf_op jit(solution)/shard_map/ppermute | solution.py:339
  107.9 3.0 %collective-permute-done.31.recv = s16[1,272,256]{2,1,0:T(8,128)(2,1)S(1)} collective-permute-done((s16[1,272,256]{2,1,0:T(8,128)(2,1)S(1)}, s16[1,272,256]{2,1,0:T(8,128)(2,1)S(1)}, u32[]{:S(2)}, u32[]{:S(2)}) %collective-permute-start.31) | collective-permute-done | bytes 139296 | tf_op jit(solution)/shard_map/ppermute | solution.py:342
  117.1 2.7 %collective-permute-done.36.refs_2_ = s16[272,256]{1,0:T(8,128)(2,1)S(1)} collective-permute-done((s16[272,256]{1,0:T(8,128)(2,1)S(1)}, s16[272,256]{1,0:T(8,128)(2,1)S(1)}, u32[]{:S(2)}, u32[]{:S(2)}) %collective-permute-start.36) | collective-permute-done | bytes 139296 | tf_op jit(solution)/shard_map/ppermute | solution.py:339
  (77 shorter events, 39.4 us)
Async XLA Ops:
  0.0 12.8 %collective-permute-start.1 = (bf16[48,256,256]{2,1,0:T(8,128)(2,1)}, bf16[48,256,256]{2,1,0:T(8,128)(2,1)}, u32[]{:S(2)}, u32[]{:S(2)}) collective-permute-start(bf16[48,256,256]{2,1,0:T(8,128)(2,1)} %own_tiles.1), channel_id=1, source_target_pairs={{0,1},{1,0},{2,3},{3,2},{4,5},{5,4},{6,7},{7,6},{8,9},{9,8},{10,11... | collective-permute-start | bytes 18874376 | tf_op jit(solution)/shard_map/ppermute | solution.py:336
  2.4 18.2 %collective-permute-start.2 = (bf16[512,256]{1,0:T(8,128)(2,1)S(1)}, bf16[512,256]{1,0:T(8,128)(2,1)S(1)}, u32[]{:S(2)}, u32[]{:S(2)}) collective-permute-start(bf16[512,256]{1,0:T(8,128)(2,1)S(1)} %get-tuple-element.116.refs_0_), channel_id=1, source_target_pairs={{0,8},{8,0},{16,24},{24,16},{1,9},{9,1},{17,25},{25,17},{2,10},{10... | collective-permute-start | bytes 786440 | tf_op jit(solution)/shard_map/ppermute | solution.py:339
  5.5 15.3 %collective-permute-start.3 = (bf16[512,256]{1,0:T(8,128)(2,1)S(1)}, bf16[512,256]{1,0:T(8,128)(2,1)S(1)}, u32[]{:S(2)}, u32[]{:S(2)}) collective-permute-start(bf16[512,256]{1,0:T(8,128)(2,1)S(1)} %get-tuple-element.115.refs_0_), channel_id=1, source_target_pairs={{0,16},{8,24},{16,0},{24,8},{1,17},{9,25},{17,1},{25,9},{2,18},{10... | collective-permute-start | bytes 786440 | tf_op jit(solution)/shard_map/ppermute | solution.py:339
  7.0 13.8 %collective-permute-start.6 = (bf16[512,256]{1,0:T(8,128)(2,1)S(1)}, bf16[512,256]{1,0:T(8,128)(2,1)S(1)}, u32[]{:S(2)}, u32[]{:S(2)}) collective-permute-start(bf16[512,256]{1,0:T(8,128)(2,1)S(1)} %get-tuple-element.65), channel_id=1, source_target_pairs={{0,24},{8,16},{16,8},{24,0},{1,25},{9,17},{17,9},{25,1},{2,26},{10... | collective-permute-start | bytes 786440 | tf_op jit(solution)/shard_map/ppermute | solution.py:339
  10.1 14.5 %collective-permute-start.5 = (bf16[512,256]{1,0:T(8,128)(2,1)S(1)}, bf16[512,256]{1,0:T(8,128)(2,1)S(1)}, u32[]{:S(2)}, u32[]{:S(2)}) collective-permute-start(bf16[512,256]{1,0:T(8,128)(2,1)S(1)} %get-tuple-element.65), channel_id=1, source_target_pairs={{0,16},{8,24},{16,0},{24,8},{1,17},{9,25},{17,1},{25,9},{2,18},{10... | collective-permute-start | bytes 786440 | tf_op jit(solution)/shard_map/ppermute | solution.py:339
  12.8 11.9 %collective-permute-start.4 = (bf16[512,256]{1,0:T(8,128)(2,1)S(1)}, bf16[512,256]{1,0:T(8,128)(2,1)S(1)}, u32[]{:S(2)}, u32[]{:S(2)}) collective-permute-start(bf16[512,256]{1,0:T(8,128)(2,1)S(1)} %get-tuple-element.65), channel_id=1, source_target_pairs={{0,8},{8,0},{16,24},{24,16},{1,9},{9,1},{17,25},{25,17},{2,10},{10... | collective-permute-start | bytes 786440 | tf_op jit(solution)/shard_map/ppermute | solution.py:339
  24.8 14.3 %collective-permute-start.9 = (bf16[1024,256]{1,0:T(8,128)(2,1)S(1)}, bf16[1024,256]{1,0:T(8,128)(2,1)S(1)}, u32[]{:S(2)}, u32[]{:S(2)}) collective-permute-start(bf16[1024,256]{1,0:T(8,128)(2,1)S(1)} %join.3.refs_0_), channel_id=1, source_target_pairs={{0,16},{8,24},{16,0},{24,8},{1,17},{9,25},{17,1},{25,9},{2,18},{10... | collective-permute-start | bytes 1572872 | tf_op jit(solution)/shard_map/ppermute | solution.py:339
  26.4 14.0 %collective-permute-start.12 = (bf16[1024,256]{1,0:T(8,128)(2,1)S(1)}, bf16[1024,256]{1,0:T(8,128)(2,1)S(1)}, u32[]{:S(2)}, u32[]{:S(2)}) collective-permute-start(bf16[1024,256]{1,0:T(8,128)(2,1)S(1)} %join.4.refs_0_), channel_id=1, source_target_pairs={{0,8},{8,0},{16,24},{24,16},{1,9},{9,1},{17,25},{25,17},{2,10},{10... | collective-permute-start | bytes 1572872 | tf_op jit(solution)/shard_map/ppermute | solution.py:339
  31.6 26.1 %collective-permute-start.14 = (s16[8,272,256]{2,1,0:T(8,128)(2,1)S(1)}, s16[8,272,256]{2,1,0:T(8,128)(2,1)S(1)}, u32[]{:S(2)}, u32[]{:S(2)}) collective-permute-start(s16[8,272,256]{2,1,0:T(8,128)(2,1)S(1)} %get-tuple-element.70), channel_id=1, source_target_pairs={{0,2},{1,3},{2,0},{3,1},{4,6},{5,7},{6,4},{7,5},{8,10},{9,11},{10,... | collective-permute-start | bytes 3342344 | tf_op jit(solution)/shard_map/ppermute | solution.py:342
  45.5 15.4 %collective-permute-start.16 = (s16[4,272,256]{2,1,0:T(8,128)(2,1)S(1)}, s16[4,272,256]{2,1,0:T(8,128)(2,1)S(1)}, u32[]{:S(2)}, u32[]{:S(2)}) collective-permute-start(s16[4,272,256]{2,1,0:T(8,128)(2,1)S(1)} %get-tuple-element.80), channel_id=1, source_target_pairs={{0,16},{8,24},{16,0},{24,8},{1,17},{9,25},{17,1},{25,9},{2,18},{10... | collective-permute-start | bytes 1671176 | tf_op jit(solution)/shard_map/ppermute | solution.py:339
  47.6 15.4 %collective-permute-start.15 = (s16[4,272,256]{2,1,0:T(8,128)(2,1)S(1)}, s16[4,272,256]{2,1,0:T(8,128)(2,1)S(1)}, u32[]{:S(2)}, u32[]{:S(2)}) collective-permute-start(s16[4,272,256]{2,1,0:T(8,128)(2,1)S(1)} %get-tuple-element.73), channel_id=1, source_target_pairs={{0,8},{8,0},{16,24},{24,16},{1,9},{9,1},{17,25},{25,17},{2,10},{10... | collective-permute-start | bytes 1671176 | tf_op jit(solution)/shard_map/ppermute | solution.py:339
  52.7 19.9 %collective-permute-start.18 = (s16[4,272,256]{2,1,0:T(8,128)(2,1)S(1)}, s16[4,272,256]{2,1,0:T(8,128)(2,1)S(1)}, u32[]{:S(2)}, u32[]{:S(2)}) collective-permute-start(s16[4,272,256]{2,1,0:T(8,128)(2,1)S(1)} %get-tuple-element.84), channel_id=1, source_target_pairs={{0,16},{8,24},{16,0},{24,8},{1,17},{9,25},{17,1},{25,9},{2,18},{10... | collective-permute-start | bytes 1671176 | tf_op jit(solution)/shard_map/ppermute | solution.py:339
  53.9 21.1 %collective-permute-start.17 = (s16[4,272,256]{2,1,0:T(8,128)(2,1)S(1)}, s16[4,272,256]{2,1,0:T(8,128)(2,1)S(1)}, u32[]{:S(2)}, u32[]{:S(2)}) collective-permute-start(s16[4,272,256]{2,1,0:T(8,128)(2,1)S(1)} %get-tuple-element.75), channel_id=1, source_target_pairs={{0,8},{8,0},{16,24},{24,16},{1,9},{9,1},{17,25},{25,17},{2,10},{10... | collective-permute-start | bytes 1671176 | tf_op jit(solution)/shard_map/ppermute | solution.py:339
  58.3 28.0 %collective-permute-start.21 = (s16[4,272,256]{2,1,0:T(8,128)(2,1)S(1)}, s16[4,272,256]{2,1,0:T(8,128)(2,1)S(1)}, u32[]{:S(2)}, u32[]{:S(2)}) collective-permute-start(s16[4,272,256]{2,1,0:T(8,128)(2,1)S(1)} %get-tuple-element.78), channel_id=1, source_target_pairs={{0,4},{1,5},{2,6},{3,7},{4,0},{5,1},{6,2},{7,3},{8,12},{9,13},{10,... | collective-permute-start | bytes 1671176 | tf_op jit(solution)/shard_map/ppermute | solution.py:342
  63.6 17.3 %collective-permute-start.20 = (s16[2,272,256]{2,1,0:T(8,128)(2,1)S(1)}, s16[2,272,256]{2,1,0:T(8,128)(2,1)S(1)}, u32[]{:S(2)}, u32[]{:S(2)}) collective-permute-start(s16[2,272,256]{2,1,0:T(8,128)(2,1)S(1)} %get-tuple-element.88), channel_id=1, source_target_pairs={{0,8},{8,0},{16,24},{24,16},{1,9},{9,1},{17,25},{25,17},{2,10},{10... | collective-permute-start | bytes 835592 | tf_op jit(solution)/shard_map/ppermute | solution.py:339
  64.2 16.7 %collective-permute-start.19 = (s16[2,272,256]{2,1,0:T(8,128)(2,1)S(1)}, s16[2,272,256]{2,1,0:T(8,128)(2,1)S(1)}, u32[]{:S(2)}, u32[]{:S(2)}) collective-permute-start(s16[2,272,256]{2,1,0:T(8,128)(2,1)S(1)} %get-tuple-element.82), channel_id=1, source_target_pairs={{0,16},{8,24},{16,0},{24,8},{1,17},{9,25},{17,1},{25,9},{2,18},{10... | collective-permute-start | bytes 835592 | tf_op jit(solution)/shard_map/ppermute | solution.py:339
  75.6 14.5 %collective-permute-start.23 = (s16[2,272,256]{2,1,0:T(8,128)(2,1)S(1)}, s16[2,272,256]{2,1,0:T(8,128)(2,1)S(1)}, u32[]{:S(2)}, u32[]{:S(2)}) collective-permute-start(s16[2,272,256]{2,1,0:T(8,128)(2,1)S(1)} %get-tuple-element.95), channel_id=1, source_target_pairs={{0,8},{8,0},{16,24},{24,16},{1,9},{9,1},{17,25},{25,17},{2,10},{10... | collective-permute-start | bytes 835592 | tf_op jit(solution)/shard_map/ppermute | solution.py:339
  76.2 13.9 %collective-permute-start.22 = (s16[2,272,256]{2,1,0:T(8,128)(2,1)S(1)}, s16[2,272,256]{2,1,0:T(8,128)(2,1)S(1)}, u32[]{:S(2)}, u32[]{:S(2)}) collective-permute-start(s16[2,272,256]{2,1,0:T(8,128)(2,1)S(1)} %get-tuple-element.86), channel_id=1, source_target_pairs={{0,16},{8,24},{16,0},{24,8},{1,17},{9,25},{17,1},{25,9},{2,18},{10... | collective-permute-start | bytes 835592 | tf_op jit(solution)/shard_map/ppermute | solution.py:339
  81.3 11.5 %collective-permute-start.24 = (s16[2,272,256]{2,1,0:T(8,128)(2,1)S(1)}, s16[2,272,256]{2,1,0:T(8,128)(2,1)S(1)}, u32[]{:S(2)}, u32[]{:S(2)}) collective-permute-start(s16[2,272,256]{2,1,0:T(8,128)(2,1)S(1)} %get-tuple-element.90), channel_id=1, source_target_pairs={{0,2},{1,3},{2,0},{3,1},{4,6},{5,7},{6,4},{7,5},{8,10},{9,11},{10,... | collective-permute-start | bytes 835592 | tf_op jit(solution)/shard_map/ppermute | solution.py:342
  86.6 9.5 %collective-permute-start.26 = (s16[2,272,256]{2,1,0:T(8,128)(2,1)S(1)}, s16[2,272,256]{2,1,0:T(8,128)(2,1)S(1)}, u32[]{:S(2)}, u32[]{:S(2)}) collective-permute-start(s16[2,272,256]{2,1,0:T(8,128)(2,1)S(1)} %get-tuple-element.102.own_b), channel_id=1, source_target_pairs={{0,16},{8,24},{16,0},{24,8},{1,17},{9,25},{17,1},{25,9},{2,18},{10... | collective-permute-start | bytes 835592 | tf_op jit(solution)/shard_map/ppermute | solution.py:339
  90.4 12.1 %collective-permute-start.28 = (s16[2,272,256]{2,1,0:T(8,128)(2,1)S(1)}, s16[2,272,256]{2,1,0:T(8,128)(2,1)S(1)}, u32[]{:S(2)}, u32[]{:S(2)}) collective-permute-start(s16[2,272,256]{2,1,0:T(8,128)(2,1)S(1)} %get-tuple-element.97), channel_id=1, source_target_pairs={{0,2},{1,3},{2,0},{3,1},{4,6},{5,7},{6,4},{7,5},{8,10},{9,11},{10,... | collective-permute-start | bytes 835592 | tf_op jit(solution)/shard_map/ppermute | solution.py:342
  92.9 9.5 %collective-permute-start.27 = (s16[1,272,256]{2,1,0:T(8,128)(2,1)S(1)}, s16[1,272,256]{2,1,0:T(8,128)(2,1)S(1)}, u32[]{:S(2)}, u32[]{:S(2)}) collective-permute-start(s16[1,272,256]{2,1,0:T(8,128)(2,1)S(1)} %get-tuple-element.100), channel_id=1, source_target_pairs={{0,4},{1,5},{2,6},{3,7},{4,0},{5,1},{6,2},{7,3},{8,12},{9,13},{10,... | collective-permute-start | bytes 417800 | tf_op jit(solution)/shard_map/ppermute | solution.py:342
  102.7 11.3 %collective-permute-start.34 = (s16[272,256]{1,0:T(8,128)(2,1)S(1)}, s16[272,256]{1,0:T(8,128)(2,1)S(1)}, u32[]{:S(2)}, u32[]{:S(2)}) collective-permute-start(s16[272,256]{1,0:T(8,128)(2,1)S(1)} %finish.2.refs_0_), channel_id=1, source_target_pairs={{0,24},{8,16},{16,8},{24,0},{1,25},{9,17},{17,9},{25,1},{2,26},{10... | collective-permute-start | bytes 417800 | tf_op jit(solution)/shard_map/ppermute | solution.py:339
  105.3 9.9 %collective-permute-start.33 = (s16[272,256]{1,0:T(8,128)(2,1)S(1)}, s16[272,256]{1,0:T(8,128)(2,1)S(1)}, u32[]{:S(2)}, u32[]{:S(2)}) collective-permute-start(s16[272,256]{1,0:T(8,128)(2,1)S(1)} %finish.2.refs_0_), channel_id=1, source_target_pairs={{0,16},{8,24},{16,0},{24,8},{1,17},{9,25},{17,1},{25,9},{2,18},{10... | collective-permute-start | bytes 417800 | tf_op jit(solution)/shard_map/ppermute | solution.py:339
  (15 other events, 107.1 us)
where the time goes:
time: 123 us
  waiting for transfers between devices  51.8 us (42%)
  starting transfers between devices  42.1 us (34%)
  Pallas kernels  26.7 us (22%)
    ppermute x25, waiting for transfers between devices, to_grp(): return lax.ppermute(v, 'grp', [(i, i ^ d) for i in range(4)])  33.7 us
    ppermute x25, starting transfers between devices, to_grp(): return lax.ppermute(v, 'grp', [(i, i ^ d) for i in range(4)])  31.3 us
    pallas_call x21, Pallas kernels, call(): pl.pallas_call(body, in_specs=more.pop('in_specs', in_any(1) + in_smem(sm...  26.7 us
    ppermute x6, waiting for transfers between devices, to_line(): return lax.ppermute(v, 'wide', [(i, i ^ 2 << b) for i in range(wide_count)])  14.1 us
    ppermute x6, starting transfers between devices, to_line(): return lax.ppermute(v, 'wide', [(i, i ^ 2 << b) for i in range(wide_count)])  6.55 us
    ppermute x7, starting transfers between devices, to_core(): return lax.ppermute(v, 'wide', [(i, i ^ 1) for i in range(wide_count)])  4.25 us
    ppermute x7, waiting for transfers between devices, to_core(): return lax.ppermute(v, 'wide', [(i, i ^ 1) for i in range(wide_count)])  3.95 us
  transfers between devices with their start and end apart: 38, of which 20 were waited for; matrix products, arithmetic and copies ran while one was open for 2% of the time, Pallas kernels for 21%

commit v1 on v0

--- a/solution.py
+++ b/solution.py
@@ -99,19 +99,35 @@
     return whole, code.astype(jnp.int32)
 
 
-def put_encoded(ref, value):
-    side = value.shape[0]
-    whole, code = encode(value)
-    ref[pl.ds(0, side), :] = whole
-    ref[pl.ds(side, CODE_ROWS), :] = jnp.broadcast_to(
-        code, (CODE_ROWS, code.shape[1])
-    ).astype(jnp.int16)
-
-
-def get_decoded(ref, side):
-    code = ref[pl.ds(side, CODE_ROWS), :].astype(jnp.int32).astype(jnp.float32)[:1]
-    scale = jnp.exp(code * (LOG2 / CODE_STEPS)) * (1.0 / TOP)
-    return ref[pl.ds(0, side), :].astype(jnp.int32).astype(jnp.float32) * scale
+def put_coded(ref, values):
+    codes = []
+    for value in values:
+        side = value.shape[0]
+        whole, code = encode(value)
+        ref[pl.ds(len(codes) * side, side), :] = whole
+        codes.append(code)
+    end = len(codes) * side
+    codes += [jnp.zeros_like(codes[0])] * (CODE_ROWS - len(codes))
+    ref[pl.ds(end, CODE_ROWS), :] = jnp.concatenate(codes, axis=0).astype(jnp.int16)
+
+
+class Decoded:
+    def __init__(self, ref, side):
+        self.ref, self.side = ref, side
+        self.count = (ref.shape[0] - CODE_ROWS) // side
+        code = ref[pl.ds(self.count * side, CODE_ROWS), :].astype(jnp.int32)
+        self.scales = jnp.exp(code.astype(jnp.float32) * (LOG2 / CODE_STEPS)) * (1.0 / TOP)
+
+    def tile(self, i):
+        return self.part(i * self.side, self.scales[i : i + 1])
+
+    def either(self, bit, zero, one):
+        at = pl.multiple_of(jnp.where(bit == 1, one, zero) * self.side, self.side)
+        scales = self.scales
+        return self.part(at, jnp.where(bit == 1, scales[one : one + 1], scales[zero : zero + 1]))
+
+    def part(self, at, scale):
+        return self.ref[pl.ds(at, self.side), :].astype(jnp.int32).astype(jnp.float32) * scale
 
 
 def here():
@@ -211,82 +227,83 @@
 
     sent = sums.shape[0] // 2
     for send in sends:
-
-        @pl.loop(0, send.shape[0])
-        def _(i, send=send, sent=sent):
-            put_encoded(send.at[i], sums[sent + i])
-
-        sent += send.shape[0]
+        count = (send.shape[0] - CODE_ROWS) // side
+        put_coded(send, (sums[sent + i] for i in range(count)))
+        sent += count
 
 
 def plane_kernel(order, recv_a, recv_b, kept, send_a, send_b, keep):
-    side, half = kept.shape[1], send_a.shape[0]
+    side, half = kept.shape[1], keep.shape[0] // 2
     x, y, _, _ = here()
     for base, bit, recv, send in ((0, y, recv_a, send_a), (1, x, recv_b, send_b)):
-
-        @pl.loop(0, half)
-        def _(i, base=base, bit=bit, recv=recv, send=send):
-            other, mine = 2 * i + 1 - bit, 2 * i + bit
-            at = base * 2 * half
-            put_encoded(send.at[i], kept[at + other] + get_decoded(recv.at[other], side))
-            keep[base * half + i] = kept[at + mine] + get_decoded(recv.at[mine], side)
+        came = Decoded(recv, side)
+
+        def total(i, which, base=base, came=came):
+            return kept[2 * half * base + 2 * i + which] + came.either(which, 2 * i, 2 * i + 1)
+
+        put_coded(send, (total(i, 1 - bit) for i in range(half)))
+        for i in range(half):
+            keep[base * half + i] = total(i, bit)
 
 
 def owner_kernel(order, recv_a, recv_b, kept, send, keep):
-    side, half = kept.shape[1], send.shape[0]
+    side, half = kept.shape[1], keep.shape[0]
     odd = here()[2]
-
-    @pl.loop(0, half)
-    def _(i):
-        value_a = kept[i] + get_decoded(recv_a.at[i], side)
-        value_b = kept[half + i] + get_decoded(recv_b.at[i], side)
-        put_encoded(send.at[i], jnp.where(odd == 1, value_a, value_b))
-        keep[i] = jnp.where(odd == 1, value_b, value_a)
+    came_a, came_b = Decoded(recv_a, side), Decoded(recv_b, side)
+
+    def to_send():
+        for i in range(half):
+            value_a = kept[i] + came_a.tile(i)
+            value_b = kept[half + i] + came_b.tile(i)
+            keep[i] = jnp.where(odd == 1, value_b, value_a)
+            yield jnp.where(odd == 1, value_a, value_b)
+
+    put_coded(send, to_send())
+
+
+def line_kernel(order, recv, kept, send, keep):
+    side, half = kept.shape[1], keep.shape[0]
+    bit = here()[3]
+    came = Decoded(recv, side)
+
+    def total(i, which):
+        return kept[which * half + i] + came.either(which, i, half + i)
+
+    put_coded(send, (total(i, 1 - bit) for i in range(half)))
+    for i in range(half):
+        keep[i] = total(i, bit)
 
 
 def rows_kernel(order, recv, kept, send_a, send_b):
-    side, half = kept.shape[1], send_a.shape[0]
-    for i in range(2 * half):
-        put_encoded(
-            (send_a, send_b)[i // half].at[i % half], kept[i] + get_decoded(recv.at[i], side)
-        )
+    came = Decoded(recv, kept.shape[1])
+    half = came.count // 2
+    put_coded(send_a, (kept[i] + came.tile(i) for i in range(half)))
+    put_coded(send_b, (kept[half + i] + came.tile(half + i) for i in range(half)))
 
 
 def swap_kernel(order, own_a, own_b, recv_a, recv_b, send_a, send_b):
-    side = own_a.shape[1] - CODE_ROWS
+    side = (own_a.shape[0] - CODE_ROWS) // 2
     for own, recv, send in ((own_a, recv_a, send_a), (own_b, recv_b, send_b)):
-        for i in range(own.shape[0]):
-            put_encoded(send.at[i], get_decoded(own.at[i], side) + get_decoded(recv.at[i], side))
-
-
-def line_kernel(order, recv, kept, send, keep):
-    side, half = kept.shape[1], send.shape[0]
-    bit = here()[3]
-
-    @pl.loop(0, half)
-    def _(i):
-        other, mine = (1 - bit) * half + i, bit * half + i
-        put_encoded(send.at[i], kept[other] + get_decoded(recv.at[other], side))
-        keep[i] = kept[mine] + get_decoded(recv.at[mine], side)
+        here_, there = Decoded(own, side), Decoded(recv, side)
+        put_coded(send, (here_.tile(i) + there.tile(i) for i in range(2)))
 
 
 def finish_kernel(order, recv, kept, out):
-    put_encoded(out, kept[0] + get_decoded(recv.at[0], kept.shape[1]))
+    put_coded(out, [kept[0] + Decoded(recv, kept.shape[1]).tile(0)])
 
 
 def spread_kernel(chunk, order, *refs):
     blocks, (out, rows, sems) = refs[:4], refs[-3:]
     side, width = rows.shape[1:]
     x, y, _, _ = here()
-    halves = len(blocks[0].shape) == 3
+    blocks = [Decoded(block, side) for block in blocks]
     copies = []
     for i in range(4):
-        if halves:
-            own, recv = blocks[i // 2].at[i % 2], blocks[2 + i // 2].at[i % 2]
-            rows[i] = get_decoded(own, side) + get_decoded(recv, side)
+        if blocks[0].count == 2:
+            rows[i] = blocks[i // 2].tile(i % 2) + blocks[2 + i // 2].tile(i % 2)
             at = i * side
         else:
-            rows[i] = get_decoded(blocks[i], side)
+            rows[i] = blocks[i].tile(0)
             at = pl.multiple_of(((2 * y + x) ^ i) * side, side)
         copies.append(
             pltpu.make_async_copy(
@@ -356,11 +373,13 @@
     near = [to_grp(mine, 1), to_grp(mine, 2), to_grp(mines[0], 3)]
 
     half, quarter = sums // 2, sums // 4
-    coded = shape((side + CODE_ROWS, CHUNK), jnp.int16)
     plain = shape((side, CHUNK), jnp.float32)
 
     def stack_of(count, one):
         return shape((count, *one.shape), one.dtype)
+
+    def coded(count):
+        return shape((count * side + CODE_ROWS, CHUNK), jnp.int16)
 
     order = jnp.zeros((1,), jnp.int32)
     last = None
@@ -467,17 +486,17 @@
     last = held
     pairs = {j: pair(j) for j in (1, 2)}
 
-    send, keep_0 = products(0, in_line, [stack_of(half, coded)], *join(0))
+    send, keep_0 = products(0, in_line, [coded(half)], *join(0))
     sent_0 = send
     sent, keep = {}, {}
     for j in (1, 2):
-        send_a, send_b, keep[j] = products(j, in_plane, [stack_of(quarter, coded)] * 2, *pairs[j])
+        send_a, send_b, keep[j] = products(j, in_plane, [coded(quarter)] * 2, *pairs[j])
         sent[j] = send_a, send_b
 
     sent_0, keep_0 = call(
         line_kernel,
         "line",
-        [stack_of(quarter, coded), stack_of(quarter, plain)],
+        [coded(quarter), stack_of(quarter, plain)],
         to_line(sent_0, 0),
         keep_0,
     )
@@ -486,7 +505,7 @@
         return call(
             plane_kernel,
             "plane",
-            [stack_of(eighth, coded)] * 2 + [stack_of(quarter, plain)],
+            [coded(eighth)] * 2 + [stack_of(quarter, plain)],
             to_grp(sent[j][0], 1),
             to_grp(sent[j][1], 2),
             keep[j],
@@ -496,7 +515,7 @@
         return call(
             owner_kernel,
             "owner",
-            [stack_of(eighth, coded), stack_of(eighth, plain)],
+            [coded(eighth), stack_of(eighth, plain)],
             to_grp(sent[j][0], 2),
             to_grp(sent[j][1], 1),
             keep[j],
@@ -505,7 +524,7 @@
     *sent[1], keep[1] = plane(1)
     *sent[2], keep[2] = plane(2)
     sent[1], keep[1] = owner(1)
-    pair_of = [stack_of(2, coded)] * 2
+    pair_of = [coded(2)] * 2
     own_a, own_b = call(rows_kernel, "rows", pair_of, to_line(sent_0, 1), keep_0)
     sent[2], keep[2] = owner(2)
 
@@ -513,13 +532,13 @@
         return call(
             line_kernel,
             "line",
-            [stack_of(1, coded), stack_of(1, plain)],
+            [coded(1), stack_of(1, plain)],
             to_line(sent[j], 0),
             keep[j],
         )
 
     def finish(j):
-        return call(finish_kernel, "finish", [coded], to_line(sent[j], 1), keep[j])[0]
+        return call(finish_kernel, "finish", [coded(1)], to_line(sent[j], 1), keep[j])[0]
 
     sent[1], keep[1] = line(1)
     own_a, own_b = call(

time: 123 us -> 121 us (0.984)
  waiting for transfers between devices: 51.8 us -> 45.2 us
  Pallas kernels: 26.7 us -> 30.2 us
    ppermute x25, waiting for transfers between devices: 33.7 us -> 28.3 us  [to_grp(): return lax.ppermute(v, 'grp', [(i, i ^ d) for i in range(4)])]
    pallas_call x21, Pallas kernels: 26.7 us -> 30.2 us  [call(): pl.pallas_call(body, in_specs=more.pop('in_specs', in_any(1) + in_smem(sm...]
    ppermute x25, starting transfers between devices: 31.3 us -> 33.3 us  [to_grp(): return lax.ppermute(v, 'grp', [(i, i ^ d) for i in range(4)])]
    ppermute x7, starting transfers between devices: 4.25 us -> 2.37 us  [to_core(): return lax.ppermute(v, 'wide', [(i, i ^ 1) for i in range(wide_count)])]
  transfers between devices with their start and end apart: 38 -> 38, of which waited for: 20 -> 19; matrix products, arithmetic and copies ran while one was open for 2% -> 2% of each run, Pallas kernels for 21% -> 24%
where the time goes in v1:
time: 121 us; the launch traced here: 120 us
  waiting for transfers between devices  45.2 us (37%)
  starting transfers between devices  42.7 us (35%)
  Pallas kernels  30.2 us (25%)
    ppermute x25, starting transfers between devices, to_grp(): return lax.ppermute(v, 'grp', [(i, i ^ d) for i in range(4)])  33.3 us
    pallas_call x21, Pallas kernels, call(): pl.pallas_call(body, in_specs=more.pop('in_specs', in_any(1) + in_smem(sm...  30.2 us
    ppermute x25, waiting for transfers between devices, to_grp(): return lax.ppermute(v, 'grp', [(i, i ^ d) for i in range(4)])  28.3 us
    ppermute x6, waiting for transfers between devices, to_line(): return lax.ppermute(v, 'wide', [(i, i ^ 2 << b) for i in range(wide_count)])  13 us
    ppermute x6, starting transfers between devices, to_line(): return lax.ppermute(v, 'wide', [(i, i ^ 2 << b) for i in range(wide_count)])  7.05 us
    ppermute x7, waiting for transfers between devices, to_core(): return lax.ppermute(v, 'wide', [(i, i ^ 1) for i in range(wide_count)])  3.95 us
  transfers between devices with their start and end apart: 38, of which 19 were waited for; matrix products, arithmetic and copies ran while one was open for 2% of the time, Pallas kernels for 24%

profile of v1, /device:TPU:0, one launch (start us, length us, event | category | flops | bytes accessed | tf_op | source)
XLA Modules:
  0.0 120.2 jit_solution(8337741578213524797)
XLA Ops:
  2.4 3.0 %collective-permute-start.2 = (bf16[512,256]{1,0:T(8,128)(2,1)S(1)}, bf16[512,256]{1,0:T(8,128)(2,1)S(1)}, u32[]{:S(2)}, u32[]{:S(2)}) collective-permute-start(bf16[512,256]{1,0:T(8,128)(2,1)S(1)} %get-tuple-element.116.refs_0_), channel_id=1, source_target_pairs={{0,8},{8,0},{16,24},{24,16},{1,9},{9,1},{17,25},{25,17},{2,10},{10... | collective-permute-start | bytes 786440 | tf_op jit(solution)/shard_map/ppermute | solution.py:356
  7.0 3.1 %collective-permute-done.sib_ref = s32[128]{0:T(128)S(1)} collective-permute-done((s32[128]{0:T(128)S(1)}, s32[128]{0:T(128)S(1)}, u32[]{:S(2)}, u32[]{:S(2)}) %collective-permute-start) | collective-permute-done | bytes 544 | tf_op jit(solution)/shard_map/ppermute | solution.py:353
  10.1 2.6 %collective-permute-start.5 = (bf16[512,256]{1,0:T(8,128)(2,1)S(1)}, bf16[512,256]{1,0:T(8,128)(2,1)S(1)}, u32[]{:S(2)}, u32[]{:S(2)}) collective-permute-start(bf16[512,256]{1,0:T(8,128)(2,1)S(1)} %get-tuple-element.65), channel_id=1, source_target_pairs={{0,16},{8,24},{16,0},{24,8},{1,17},{9,25},{17,1},{25,9},{2,18},{10... | collective-permute-start | bytes 786440 | tf_op jit(solution)/shard_map/ppermute | solution.py:356
  14.3 6.4 %hold.1 = (s32[1]{0:T(128)}, s32[104]{0:T(128)S(1)}, s32[104]{0:T(128)S(1)}, s32[104]{0:T(128)S(1)}, bf16[104,256,256]{2,1,0:T(8,128)(2,1)S(1)}) custom-call(s32[1]{0:T(128)} %constant.8.clone.1.order, s32[128]{0:T(128)S(1)} %pad_add_fusion.own_ref, s32[128]{0:T(128)S(1)} %collective-permute-done.sib_ref, bf16[48,256,256]{2,1,0:T(8,128)(2,1)} %own_tiles.1, ...), custom_call_target="tpu_custom_call" | custom-call | bytes 12583936 | tf_op jit(solution)/shard_map/hold/pallas_call | solution.py:392
  20.8 3.9 %collective-permute-done.5.refs_1_ = bf16[512,256]{1,0:T(8,128)(2,1)S(1)} collective-permute-done((bf16[512,256]{1,0:T(8,128)(2,1)S(1)}, bf16[512,256]{1,0:T(8,128)(2,1)S(1)}, u32[]{:S(2)}, u32[]{:S(2)}) %collective-permute-start.5) | collective-permute-done | bytes 262176 | tf_op jit(solution)/shard_map/ppermute | solution.py:356
  27.1 5.7 %products.3 = (s16[2064,256]{1,0:T(8,128)(2,1)S(1)}, f32[17,256,256]{2,1,0:T(8,128)S(1)}) custom-call(s32[1]{0:T(128)} %constant.8.clone.1.order, s32[1]{0:T(128)} %get-tuple-element.67.count_ref, s32[104]{0:T(128)S(1)} %get-tuple-element.68.slot_ref, s32[104]{0:T(128)S(1)} %get-tuple-element.69.label_ref, ...), custom_call_target="tpu_custom_call" | custom-call | bytes 16778052 | tf_op jit(solution)/shard_map/products/pallas_call | solution.py:392
  34.3 4.8 %collective-permute-done.9.refs_2_ = bf16[1024,256]{1,0:T(8,128)(2,1)S(1)} collective-permute-done((bf16[1024,256]{1,0:T(8,128)(2,1)S(1)}, bf16[1024,256]{1,0:T(8,128)(2,1)S(1)}, u32[]{:S(2)}, u32[]{:S(2)}) %collective-permute-start.9) | collective-permute-done | bytes 524320 | tf_op jit(solution)/shard_map/ppermute | solution.py:356
  41.0 5.7 %products.4 = (s16[1040,256]{1,0:T(8,128)(2,1)S(1)}, s16[1040,256]{1,0:T(8,128)(2,1)S(1)}, f32[17,256,256]{2,1,0:T(8,128)S(1)}) custom-call(s32[1]{0:T(128)} %constant.8.clone.1.order, s32[1]{0:T(128)} %get-tuple-element.67.count_ref, s32[104]{0:T(128)S(1)} %get-tuple-element.72.slot_ref, s32[104]{0:T(128)S(1)} %get-tuple-element.69.label_ref, ...), custom_call_target="tpu_custom_call" | custom-call | bytes 17302340 | tf_op jit(solution)/shard_map/products/pallas_call | solution.py:392
  48.4 5.7 %products.5 = (s16[1040,256]{1,0:T(8,128)(2,1)S(1)}, s16[1040,256]{1,0:T(8,128)(2,1)S(1)}, f32[17,256,256]{2,1,0:T(8,128)S(1)}) custom-call(s32[1]{0:T(128)} %constant.8.clone.1.order, s32[1]{0:T(128)} %get-tuple-element.67.count_ref, s32[104]{0:T(128)S(1)} %get-tuple-element.72.slot_ref, s32[104]{0:T(128)S(1)} %get-tuple-element.69.label_ref, ...), custom_call_target="tpu_custom_call" | custom-call | bytes 17302340 | tf_op jit(solution)/shard_map/products/pallas_call | solution.py:392
  54.5 1.7 %collective-permute-start.17 = (s16[1040,256]{1,0:T(8,128)(2,1)S(1)}, s16[1040,256]{1,0:T(8,128)(2,1)S(1)}, u32[]{:S(2)}, u32[]{:S(2)}) collective-permute-start(s16[1040,256]{1,0:T(8,128)(2,1)S(1)} %get-tuple-element.75), channel_id=1, source_target_pairs={{0,8},{8,0},{16,24},{24,16},{1,9},{9,1},{17,25},{25,17},{2,10},{10... | collective-permute-start | bytes 1597448 | tf_op jit(solution)/shard_map/ppermute | solution.py:356
  56.3 1.8 %collective-permute-done.14.recv = s16[2064,256]{1,0:T(8,128)(2,1)S(1)} collective-permute-done((s16[2064,256]{1,0:T(8,128)(2,1)S(1)}, s16[2064,256]{1,0:T(8,128)(2,1)S(1)}, u32[]{:S(2)}, u32[]{:S(2)}) %collective-permute-start.14) | collective-permute-done | bytes 1056800 | tf_op jit(solution)/shard_map/ppermute | solution.py:359
  58.6 2.2 %collective-permute-start.21 = (s16[1040,256]{1,0:T(8,128)(2,1)S(1)}, s16[1040,256]{1,0:T(8,128)(2,1)S(1)}, u32[]{:S(2)}, u32[]{:S(2)}) collective-permute-start(s16[1040,256]{1,0:T(8,128)(2,1)S(1)} %get-tuple-element.78), channel_id=1, source_target_pairs={{0,4},{1,5},{2,6},{3,7},{4,0},{5,1},{6,2},{7,3},{8,12},{9,13},{10,... | collective-permute-start | bytes 1597448 | tf_op jit(solution)/shard_map/ppermute | solution.py:359
  64.0 1.8 %collective-permute-start.19 = (s16[528,256]{1,0:T(8,128)(2,1)S(1)}, s16[528,256]{1,0:T(8,128)(2,1)S(1)}, u32[]{:S(2)}, u32[]{:S(2)}) collective-permute-start(s16[528,256]{1,0:T(8,128)(2,1)S(1)} %get-tuple-element.82), channel_id=1, source_target_pairs={{0,16},{8,24},{16,0},{24,8},{1,17},{9,25},{17,1},{25,9},{2,18},{10... | collective-permute-start | bytes 811016 | tf_op jit(solution)/shard_map/ppermute | solution.py:356
  65.8 7.5 %collective-permute-done.18.recv_b = s16[1040,256]{1,0:T(8,128)(2,1)S(1)} collective-permute-done((s16[1040,256]{1,0:T(8,128)(2,1)S(1)}, s16[1040,256]{1,0:T(8,128)(2,1)S(1)}, u32[]{:S(2)}, u32[]{:S(2)}) %collective-permute-start.18) | collective-permute-done | bytes 532512 | tf_op jit(solution)/shard_map/ppermute | solution.py:356
  75.4 1.8 %collective-permute-start.22 = (s16[528,256]{1,0:T(8,128)(2,1)S(1)}, s16[528,256]{1,0:T(8,128)(2,1)S(1)}, u32[]{:S(2)}, u32[]{:S(2)}) collective-permute-start(s16[528,256]{1,0:T(8,128)(2,1)S(1)} %get-tuple-element.86), channel_id=1, source_target_pairs={{0,16},{8,24},{16,0},{24,8},{1,17},{9,25},{17,1},{25,9},{2,18},{10... | collective-permute-start | bytes 811016 | tf_op jit(solution)/shard_map/ppermute | solution.py:356
  79.1 3.4 %collective-permute-start.24 = (s16[528,256]{1,0:T(8,128)(2,1)S(1)}, s16[528,256]{1,0:T(8,128)(2,1)S(1)}, u32[]{:S(2)}, u32[]{:S(2)}) collective-permute-start(s16[528,256]{1,0:T(8,128)(2,1)S(1)} %get-tuple-element.90), channel_id=1, source_target_pairs={{0,2},{1,3},{2,0},{3,1},{4,6},{5,7},{6,4},{7,5},{8,10},{9,11},{10,... | collective-permute-start | bytes 811016 | tf_op jit(solution)/shard_map/ppermute | solution.py:359
  82.5 1.7 %collective-permute-done.21.recv = s16[1040,256]{1,0:T(8,128)(2,1)S(1)} collective-permute-done((s16[1040,256]{1,0:T(8,128)(2,1)S(1)}, s16[1040,256]{1,0:T(8,128)(2,1)S(1)}, u32[]{:S(2)}, u32[]{:S(2)}) %collective-permute-start.21) | collective-permute-done | bytes 532512 | tf_op jit(solution)/shard_map/ppermute | solution.py:359
  84.5 2.4 %collective-permute-start.26 = (s16[528,256]{1,0:T(8,128)(2,1)S(1)}, s16[528,256]{1,0:T(8,128)(2,1)S(1)}, u32[]{:S(2)}, u32[]{:S(2)}) collective-permute-start(s16[528,256]{1,0:T(8,128)(2,1)S(1)} %get-tuple-element.102.own_b), channel_id=1, source_target_pairs={{0,16},{8,24},{16,0},{24,8},{1,17},{9,25},{17,1},{25,9},{2,18},{10... | collective-permute-start | bytes 811016 | tf_op jit(solution)/shard_map/ppermute | solution.py:356
  87.3 2.7 %collective-permute-done.24.recv = s16[528,256]{1,0:T(8,128)(2,1)S(1)} collective-permute-done((s16[528,256]{1,0:T(8,128)(2,1)S(1)}, s16[528,256]{1,0:T(8,128)(2,1)S(1)}, u32[]{:S(2)}, u32[]{:S(2)}) %collective-permute-start.24) | collective-permute-done | bytes 270368 | tf_op jit(solution)/shard_map/ppermute | solution.py:359
  95.4 4.2 %collective-permute-done.27.recv = s16[272,256]{1,0:T(8,128)(2,1)S(1)} collective-permute-done((s16[272,256]{1,0:T(8,128)(2,1)S(1)}, s16[272,256]{1,0:T(8,128)(2,1)S(1)}, u32[]{:S(2)}, u32[]{:S(2)}) %collective-permute-start.27) | collective-permute-done | bytes 139296 | tf_op jit(solution)/shard_map/ppermute | solution.py:359
  105.0 2.6 %collective-permute-done.31.recv = s16[272,256]{1,0:T(8,128)(2,1)S(1)} collective-permute-done((s16[272,256]{1,0:T(8,128)(2,1)S(1)}, s16[272,256]{1,0:T(8,128)(2,1)S(1)}, u32[]{:S(2)}, u32[]{:S(2)}) %collective-permute-start.31) | collective-permute-done | bytes 139296 | tf_op jit(solution)/shard_map/ppermute | solution.py:359
  108.5 2.7 %collective-permute-start.36 = (s16[272,256]{1,0:T(8,128)(2,1)S(1)}, s16[272,256]{1,0:T(8,128)(2,1)S(1)}, u32[]{:S(2)}, u32[]{:S(2)}) collective-permute-start(s16[272,256]{1,0:T(8,128)(2,1)S(1)} %finish.3.refs_0_), channel_id=1, source_target_pairs={{0,16},{8,24},{16,0},{24,8},{1,17},{9,25},{17,1},{25,9},{2,18},{10... | collective-permute-start | bytes 417800 | tf_op jit(solution)/shard_map/ppermute | solution.py:356
  113.7 3.6 %collective-permute-done.36.refs_2_ = s16[272,256]{1,0:T(8,128)(2,1)S(1)} collective-permute-done((s16[272,256]{1,0:T(8,128)(2,1)S(1)}, s16[272,256]{1,0:T(8,128)(2,1)S(1)}, u32[]{:S(2)}, u32[]{:S(2)}) %collective-permute-start.36) | collective-permute-done | bytes 139296 | tf_op jit(solution)/shard_map/ppermute | solution.py:356
  117.3 1.9 %collective-permute-done.35.refs_1_ = s16[272,256]{1,0:T(8,128)(2,1)S(1)} collective-permute-done((s16[272,256]{1,0:T(8,128)(2,1)S(1)}, s16[272,256]{1,0:T(8,128)(2,1)S(1)}, u32[]{:S(2)}, u32[]{:S(2)}) %collective-permute-start.35) | collective-permute-done | bytes 139296 | tf_op jit(solution)/shard_map/ppermute | solution.py:356
  (77 shorter events, 37.0 us)
Async XLA Ops:
  0.0 12.8 %collective-permute-start.1 = (bf16[48,256,256]{2,1,0:T(8,128)(2,1)}, bf16[48,256,256]{2,1,0:T(8,128)(2,1)}, u32[]{:S(2)}, u32[]{:S(2)}) collective-permute-start(bf16[48,256,256]{2,1,0:T(8,128)(2,1)} %own_tiles.1), channel_id=1, source_target_pairs={{0,1},{1,0},{2,3},{3,2},{4,5},{5,4},{6,7},{7,6},{8,9},{9,8},{10,11... | collective-permute-start | bytes 18874376 | tf_op jit(solution)/shard_map/ppermute | solution.py:353
  2.4 18.2 %collective-permute-start.2 = (bf16[512,256]{1,0:T(8,128)(2,1)S(1)}, bf16[512,256]{1,0:T(8,128)(2,1)S(1)}, u32[]{:S(2)}, u32[]{:S(2)}) collective-permute-start(bf16[512,256]{1,0:T(8,128)(2,1)S(1)} %get-tuple-element.116.refs_0_), channel_id=1, source_target_pairs={{0,8},{8,0},{16,24},{24,16},{1,9},{9,1},{17,25},{25,17},{2,10},{10... | collective-permute-start | bytes 786440 | tf_op jit(solution)/shard_map/ppermute | solution.py:356
  5.5 15.3 %collective-permute-start.3 = (bf16[512,256]{1,0:T(8,128)(2,1)S(1)}, bf16[512,256]{1,0:T(8,128)(2,1)S(1)}, u32[]{:S(2)}, u32[]{:S(2)}) collective-permute-start(bf16[512,256]{1,0:T(8,128)(2,1)S(1)} %get-tuple-element.115.refs_0_), channel_id=1, source_target_pairs={{0,16},{8,24},{16,0},{24,8},{1,17},{9,25},{17,1},{25,9},{2,18},{10... | collective-permute-start | bytes 786440 | tf_op jit(solution)/shard_map/ppermute | solution.py:356
  7.0 13.8 %collective-permute-start.6 = (bf16[512,256]{1,0:T(8,128)(2,1)S(1)}, bf16[512,256]{1,0:T(8,128)(2,1)S(1)}, u32[]{:S(2)}, u32[]{:S(2)}) collective-permute-start(bf16[512,256]{1,0:T(8,128)(2,1)S(1)} %get-tuple-element.65), channel_id=1, source_target_pairs={{0,24},{8,16},{16,8},{24,0},{1,25},{9,17},{17,9},{25,1},{2,26},{10... | collective-permute-start | bytes 786440 | tf_op jit(solution)/shard_map/ppermute | solution.py:356
  10.1 14.5 %collective-permute-start.5 = (bf16[512,256]{1,0:T(8,128)(2,1)S(1)}, bf16[512,256]{1,0:T(8,128)(2,1)S(1)}, u32[]{:S(2)}, u32[]{:S(2)}) collective-permute-start(bf16[512,256]{1,0:T(8,128)(2,1)S(1)} %get-tuple-element.65), channel_id=1, source_target_pairs={{0,16},{8,24},{16,0},{24,8},{1,17},{9,25},{17,1},{25,9},{2,18},{10... | collective-permute-start | bytes 786440 | tf_op jit(solution)/shard_map/ppermute | solution.py:356
  12.8 11.9 %collective-permute-start.4 = (bf16[512,256]{1,0:T(8,128)(2,1)S(1)}, bf16[512,256]{1,0:T(8,128)(2,1)S(1)}, u32[]{:S(2)}, u32[]{:S(2)}) collective-permute-start(bf16[512,256]{1,0:T(8,128)(2,1)S(1)} %get-tuple-element.65), channel_id=1, source_target_pairs={{0,8},{8,0},{16,24},{24,16},{1,9},{9,1},{17,25},{25,17},{2,10},{10... | collective-permute-start | bytes 786440 | tf_op jit(solution)/shard_map/ppermute | solution.py:356
  24.8 14.3 %collective-permute-start.9 = (bf16[1024,256]{1,0:T(8,128)(2,1)S(1)}, bf16[1024,256]{1,0:T(8,128)(2,1)S(1)}, u32[]{:S(2)}, u32[]{:S(2)}) collective-permute-start(bf16[1024,256]{1,0:T(8,128)(2,1)S(1)} %join.3.refs_0_), channel_id=1, source_target_pairs={{0,16},{8,24},{16,0},{24,8},{1,17},{9,25},{17,1},{25,9},{2,18},{10... | collective-permute-start | bytes 1572872 | tf_op jit(solution)/shard_map/ppermute | solution.py:356
  26.4 14.0 %collective-permute-start.12 = (bf16[1024,256]{1,0:T(8,128)(2,1)S(1)}, bf16[1024,256]{1,0:T(8,128)(2,1)S(1)}, u32[]{:S(2)}, u32[]{:S(2)}) collective-permute-start(bf16[1024,256]{1,0:T(8,128)(2,1)S(1)} %join.4.refs_0_), channel_id=1, source_target_pairs={{0,8},{8,0},{16,24},{24,16},{1,9},{9,1},{17,25},{25,17},{2,10},{10... | collective-permute-start | bytes 1572872 | tf_op jit(solution)/shard_map/ppermute | solution.py:356
  32.8 25.3 %collective-permute-start.14 = (s16[2064,256]{1,0:T(8,128)(2,1)S(1)}, s16[2064,256]{1,0:T(8,128)(2,1)S(1)}, u32[]{:S(2)}, u32[]{:S(2)}) collective-permute-start(s16[2064,256]{1,0:T(8,128)(2,1)S(1)} %get-tuple-element.70), channel_id=1, source_target_pairs={{0,2},{1,3},{2,0},{3,1},{4,6},{5,7},{6,4},{7,5},{8,10},{9,11},{10,... | collective-permute-start | bytes 3170312 | tf_op jit(solution)/shard_map/ppermute | solution.py:359
  46.8 15.0 %collective-permute-start.16 = (s16[1040,256]{1,0:T(8,128)(2,1)S(1)}, s16[1040,256]{1,0:T(8,128)(2,1)S(1)}, u32[]{:S(2)}, u32[]{:S(2)}) collective-permute-start(s16[1040,256]{1,0:T(8,128)(2,1)S(1)} %get-tuple-element.80), channel_id=1, source_target_pairs={{0,16},{8,24},{16,0},{24,8},{1,17},{9,25},{17,1},{25,9},{2,18},{10... | collective-permute-start | bytes 1597448 | tf_op jit(solution)/shard_map/ppermute | solution.py:356
  47.0 14.9 %collective-permute-start.15 = (s16[1040,256]{1,0:T(8,128)(2,1)S(1)}, s16[1040,256]{1,0:T(8,128)(2,1)S(1)}, u32[]{:S(2)}, u32[]{:S(2)}) collective-permute-start(s16[1040,256]{1,0:T(8,128)(2,1)S(1)} %get-tuple-element.73), channel_id=1, source_target_pairs={{0,8},{8,0},{16,24},{24,16},{1,9},{9,1},{17,25},{25,17},{2,10},{10... | collective-permute-start | bytes 1597448 | tf_op jit(solution)/shard_map/ppermute | solution.py:356
  54.2 19.0 %collective-permute-start.18 = (s16[1040,256]{1,0:T(8,128)(2,1)S(1)}, s16[1040,256]{1,0:T(8,128)(2,1)S(1)}, u32[]{:S(2)}, u32[]{:S(2)}) collective-permute-start(s16[1040,256]{1,0:T(8,128)(2,1)S(1)} %get-tuple-element.84), channel_id=1, source_target_pairs={{0,16},{8,24},{16,0},{24,8},{1,17},{9,25},{17,1},{25,9},{2,18},{10... | collective-permute-start | bytes 1597448 | tf_op jit(solution)/shard_map/ppermute | solution.py:356
  54.5 18.7 %collective-permute-start.17 = (s16[1040,256]{1,0:T(8,128)(2,1)S(1)}, s16[1040,256]{1,0:T(8,128)(2,1)S(1)}, u32[]{:S(2)}, u32[]{:S(2)}) collective-permute-start(s16[1040,256]{1,0:T(8,128)(2,1)S(1)} %get-tuple-element.75), channel_id=1, source_target_pairs={{0,8},{8,0},{16,24},{24,16},{1,9},{9,1},{17,25},{25,17},{2,10},{10... | collective-permute-start | bytes 1597448 | tf_op jit(solution)/shard_map/ppermute | solution.py:356
  58.6 25.6 %collective-permute-start.21 = (s16[1040,256]{1,0:T(8,128)(2,1)S(1)}, s16[1040,256]{1,0:T(8,128)(2,1)S(1)}, u32[]{:S(2)}, u32[]{:S(2)}) collective-permute-start(s16[1040,256]{1,0:T(8,128)(2,1)S(1)} %get-tuple-element.78), channel_id=1, source_target_pairs={{0,4},{1,5},{2,6},{3,7},{4,0},{5,1},{6,2},{7,3},{8,12},{9,13},{10,... | collective-permute-start | bytes 1597448 | tf_op jit(solution)/shard_map/ppermute | solution.py:359
  62.4 16.5 %collective-permute-start.20 = (s16[528,256]{1,0:T(8,128)(2,1)S(1)}, s16[528,256]{1,0:T(8,128)(2,1)S(1)}, u32[]{:S(2)}, u32[]{:S(2)}) collective-permute-start(s16[528,256]{1,0:T(8,128)(2,1)S(1)} %get-tuple-element.88), channel_id=1, source_target_pairs={{0,8},{8,0},{16,24},{24,16},{1,9},{9,1},{17,25},{25,17},{2,10},{10... | collective-permute-start | bytes 811016 | tf_op jit(solution)/shard_map/ppermute | solution.py:356
  64.0 14.8 %collective-permute-start.19 = (s16[528,256]{1,0:T(8,128)(2,1)S(1)}, s16[528,256]{1,0:T(8,128)(2,1)S(1)}, u32[]{:S(2)}, u32[]{:S(2)}) collective-permute-start(s16[528,256]{1,0:T(8,128)(2,1)S(1)} %get-tuple-element.82), channel_id=1, source_target_pairs={{0,16},{8,24},{16,0},{24,8},{1,17},{9,25},{17,1},{25,9},{2,18},{10... | collective-permute-start | bytes 811016 | tf_op jit(solution)/shard_map/ppermute | solution.py:356
  73.8 13.2 %collective-permute-start.23 = (s16[528,256]{1,0:T(8,128)(2,1)S(1)}, s16[528,256]{1,0:T(8,128)(2,1)S(1)}, u32[]{:S(2)}, u32[]{:S(2)}) collective-permute-start(s16[528,256]{1,0:T(8,128)(2,1)S(1)} %get-tuple-element.95), channel_id=1, source_target_pairs={{0,8},{8,0},{16,24},{24,16},{1,9},{9,1},{17,25},{25,17},{2,10},{10... | collective-permute-start | bytes 811016 | tf_op jit(solution)/shard_map/ppermute | solution.py:356
  75.4 11.6 %collective-permute-start.22 = (s16[528,256]{1,0:T(8,128)(2,1)S(1)}, s16[528,256]{1,0:T(8,128)(2,1)S(1)}, u32[]{:S(2)}, u32[]{:S(2)}) collective-permute-start(s16[528,256]{1,0:T(8,128)(2,1)S(1)} %get-tuple-element.86), channel_id=1, source_target_pairs={{0,16},{8,24},{16,0},{24,8},{1,17},{9,25},{17,1},{25,9},{2,18},{10... | collective-permute-start | bytes 811016 | tf_op jit(solution)/shard_map/ppermute | solution.py:356
  79.1 10.9 %collective-permute-start.24 = (s16[528,256]{1,0:T(8,128)(2,1)S(1)}, s16[528,256]{1,0:T(8,128)(2,1)S(1)}, u32[]{:S(2)}, u32[]{:S(2)}) collective-permute-start(s16[528,256]{1,0:T(8,128)(2,1)S(1)} %get-tuple-element.90), channel_id=1, source_target_pairs={{0,2},{1,3},{2,0},{3,1},{4,6},{5,7},{6,4},{7,5},{8,10},{9,11},{10,... | collective-permute-start | bytes 811016 | tf_op jit(solution)/shard_map/ppermute | solution.py:359
  87.2 12.5 %collective-permute-start.28 = (s16[528,256]{1,0:T(8,128)(2,1)S(1)}, s16[528,256]{1,0:T(8,128)(2,1)S(1)}, u32[]{:S(2)}, u32[]{:S(2)}) collective-permute-start(s16[528,256]{1,0:T(8,128)(2,1)S(1)} %get-tuple-element.97), channel_id=1, source_target_pairs={{0,2},{1,3},{2,0},{3,1},{4,6},{5,7},{6,4},{7,5},{8,10},{9,11},{10,... | collective-permute-start | bytes 811016 | tf_op jit(solution)/shard_map/ppermute | solution.py:359
  90.2 9.5 %collective-permute-start.27 = (s16[272,256]{1,0:T(8,128)(2,1)S(1)}, s16[272,256]{1,0:T(8,128)(2,1)S(1)}, u32[]{:S(2)}, u32[]{:S(2)}) collective-permute-start(s16[272,256]{1,0:T(8,128)(2,1)S(1)} %get-tuple-element.100), channel_id=1, source_target_pairs={{0,4},{1,5},{2,6},{3,7},{4,0},{5,1},{6,2},{7,3},{8,12},{9,13},{10,... | collective-permute-start | bytes 417800 | tf_op jit(solution)/shard_map/ppermute | solution.py:359
  100.0 11.2 %collective-permute-start.34 = (s16[272,256]{1,0:T(8,128)(2,1)S(1)}, s16[272,256]{1,0:T(8,128)(2,1)S(1)}, u32[]{:S(2)}, u32[]{:S(2)}) collective-permute-start(s16[272,256]{1,0:T(8,128)(2,1)S(1)} %finish.2.refs_0_), channel_id=1, source_target_pairs={{0,24},{8,16},{16,8},{24,0},{1,25},{9,17},{17,9},{25,1},{2,26},{10... | collective-permute-start | bytes 417800 | tf_op jit(solution)/shard_map/ppermute | solution.py:356
  101.1 11.5 %collective-permute-start.33 = (s16[272,256]{1,0:T(8,128)(2,1)S(1)}, s16[272,256]{1,0:T(8,128)(2,1)S(1)}, u32[]{:S(2)}, u32[]{:S(2)}) collective-permute-start(s16[272,256]{1,0:T(8,128)(2,1)S(1)} %finish.2.refs_0_), channel_id=1, source_target_pairs={{0,16},{8,24},{16,0},{24,8},{1,17},{9,25},{17,1},{25,9},{2,18},{10... | collective-permute-start | bytes 417800 | tf_op jit(solution)/shard_map/ppermute | solution.py:356
  102.8 9.8 %collective-permute-start.32 = (s16[272,256]{1,0:T(8,128)(2,1)S(1)}, s16[272,256]{1,0:T(8,128)(2,1)S(1)}, u32[]{:S(2)}, u32[]{:S(2)}) collective-permute-start(s16[272,256]{1,0:T(8,128)(2,1)S(1)} %finish.2.refs_0_), channel_id=1, source_target_pairs={{0,8},{8,0},{16,24},{24,16},{1,9},{9,1},{17,25},{25,17},{2,10},{10... | collective-permute-start | bytes 417800 | tf_op jit(solution)/shard_map/ppermute | solution.py:356
  (15 other events, 107.3 us)

commit v2 on v1

--- a/solution.py
+++ b/solution.py
@@ -525,8 +525,8 @@
     *sent[2], keep[2] = plane(2)
     sent[1], keep[1] = owner(1)
     pair_of = [coded(2)] * 2
+    sent[2], keep[2] = owner(2)
     own_a, own_b = call(rows_kernel, "rows", pair_of, to_line(sent_0, 1), keep_0)
-    sent[2], keep[2] = owner(2)
 
     def line(j):
         return call(
@@ -541,11 +541,11 @@
         return call(finish_kernel, "finish", [coded(1)], to_line(sent[j], 1), keep[j])[0]
 
     sent[1], keep[1] = line(1)
+    sent[2], keep[2] = line(2)
     own_a, own_b = call(
         swap_kernel, "swap", pair_of, own_a, own_b, to_grp(own_a, 1), to_grp(own_b, 2)
     )
     done_1 = finish(1)
-    sent[2], keep[2] = line(2)
     result = spread(0, [own_a, own_b, to_grp(own_a, 2), to_grp(own_b, 1)], None)
     done_2 = finish(2)
     result = spread(1, gathered(done_1), result)

time: 121 us -> 122 us (level)
  waiting for transfers between devices: 45.2 us -> 52.1 us
  starting transfers between devices: 42.7 us -> 37.4 us
    ppermute x25, waiting for transfers between devices: 28.3 us -> 38.2 us  [to_grp(): return lax.ppermute(v, 'grp', [(i, i ^ d) for i in range(4)])]
    ppermute x25, starting transfers between devices: 33.3 us -> 26.3 us  [to_grp(): return lax.ppermute(v, 'grp', [(i, i ^ d) for i in range(4)])]
    ppermute x6, waiting for transfers between devices: 13 us -> 9.88 us  [to_line(): return lax.ppermute(v, 'wide', [(i, i ^ 2 << b) for i in range(wide_count)])]
    ppermute x6, starting transfers between devices: 7.05 us -> 10.1 us  [to_line(): return lax.ppermute(v, 'wide', [(i, i ^ 2 << b) for i in range(wide_count)])]
    ppermute x7, starting transfers between devices: 2.37 us -> 1.1 us  [to_core(): return lax.ppermute(v, 'wide', [(i, i ^ 1) for i in range(wide_count)])]
  transfers between devices with their start and end apart: 38 -> 38, of which waited for: 19 -> 20; matrix products, arithmetic and copies ran while one was open for 2% -> 2% of each run, Pallas kernels for 24% -> 24%
where the time goes in v2:
time: 122 us
  waiting for transfers between devices  52.1 us (43%)
  starting transfers between devices  37.4 us (31%)
  Pallas kernels  30.1 us (25%)
    ppermute x25, waiting for transfers between devices, to_grp(): return lax.ppermute(v, 'grp', [(i, i ^ d) for i in range(4)])  38.2 us
    pallas_call x21, Pallas kernels, call(): pl.pallas_call(body, in_specs=more.pop('in_specs', in_any(1) + in_smem(sm...  30.1 us
    ppermute x25, starting transfers between devices, to_grp(): return lax.ppermute(v, 'grp', [(i, i ^ d) for i in range(4)])  26.3 us
    ppermute x6, starting transfers between devices, to_line(): return lax.ppermute(v, 'wide', [(i, i ^ 2 << b) for i in range(wide_count)])  10.1 us
    ppermute x6, waiting for transfers between devices, to_line(): return lax.ppermute(v, 'wide', [(i, i ^ 2 << b) for i in range(wide_count)])  9.88 us
    ppermute x7, waiting for transfers between devices, to_core(): return lax.ppermute(v, 'wide', [(i, i ^ 1) for i in range(wide_count)])  3.95 us
  transfers between devices with their start and end apart: 38, of which 20 were waited for; matrix products, arithmetic and copies ran while one was open for 2% of the time, Pallas kernels for 24%

profile of v2, /device:TPU:0, one launch (start us, length us, event | category | flops | bytes accessed | tf_op | source)
XLA Modules:
  0.0 121.8 jit_solution(18092538036388255166)
XLA Ops:
  2.4 3.0 %collective-permute-start.2 = (bf16[512,256]{1,0:T(8,128)(2,1)S(1)}, bf16[512,256]{1,0:T(8,128)(2,1)S(1)}, u32[]{:S(2)}, u32[]{:S(2)}) collective-permute-start(bf16[512,256]{1,0:T(8,128)(2,1)S(1)} %get-tuple-element.116.refs_0_), channel_id=1, source_target_pairs={{0,8},{8,0},{16,24},{24,16},{1,9},{9,1},{17,25},{25,17},{2,10},{10... | collective-permute-start | bytes 786440 | tf_op jit(solution)/shard_map/ppermute | solution.py:356
  7.0 3.1 %collective-permute-done.sib_ref = s32[128]{0:T(128)S(1)} collective-permute-done((s32[128]{0:T(128)S(1)}, s32[128]{0:T(128)S(1)}, u32[]{:S(2)}, u32[]{:S(2)}) %collective-permute-start) | collective-permute-done | bytes 544 | tf_op jit(solution)/shard_map/ppermute | solution.py:353
  10.1 2.6 %collective-permute-start.5 = (bf16[512,256]{1,0:T(8,128)(2,1)S(1)}, bf16[512,256]{1,0:T(8,128)(2,1)S(1)}, u32[]{:S(2)}, u32[]{:S(2)}) collective-permute-start(bf16[512,256]{1,0:T(8,128)(2,1)S(1)} %get-tuple-element.65), channel_id=1, source_target_pairs={{0,16},{8,24},{16,0},{24,8},{1,17},{9,25},{17,1},{25,9},{2,18},{10... | collective-permute-start | bytes 786440 | tf_op jit(solution)/shard_map/ppermute | solution.py:356
  14.3 6.4 %hold.1 = (s32[1]{0:T(128)}, s32[104]{0:T(128)S(1)}, s32[104]{0:T(128)S(1)}, s32[104]{0:T(128)S(1)}, bf16[104,256,256]{2,1,0:T(8,128)(2,1)S(1)}) custom-call(s32[1]{0:T(128)} %constant.8.clone.1.order, s32[128]{0:T(128)S(1)} %pad_add_fusion.own_ref, s32[128]{0:T(128)S(1)} %collective-permute-done.sib_ref, bf16[48,256,256]{2,1,0:T(8,128)(2,1)} %own_tiles.1, ...), custom_call_target="tpu_custom_call" | custom-call | bytes 12583936 | tf_op jit(solution)/shard_map/hold/pallas_call | solution.py:392
  20.8 3.9 %collective-permute-done.5.refs_1_ = bf16[512,256]{1,0:T(8,128)(2,1)S(1)} collective-permute-done((bf16[512,256]{1,0:T(8,128)(2,1)S(1)}, bf16[512,256]{1,0:T(8,128)(2,1)S(1)}, u32[]{:S(2)}, u32[]{:S(2)}) %collective-permute-start.5) | collective-permute-done | bytes 262176 | tf_op jit(solution)/shard_map/ppermute | solution.py:356
  27.1 5.7 %products.3 = (s16[2064,256]{1,0:T(8,128)(2,1)S(1)}, f32[17,256,256]{2,1,0:T(8,128)S(1)}) custom-call(s32[1]{0:T(128)} %constant.8.clone.1.order, s32[1]{0:T(128)} %get-tuple-element.67.count_ref, s32[104]{0:T(128)S(1)} %get-tuple-element.68.slot_ref, s32[104]{0:T(128)S(1)} %get-tuple-element.69.label_ref, ...), custom_call_target="tpu_custom_call" | custom-call | bytes 16778052 | tf_op jit(solution)/shard_map/products/pallas_call | solution.py:392
  32.8 1.6 %collective-permute-start.14 = (s16[2064,256]{1,0:T(8,128)(2,1)S(1)}, s16[2064,256]{1,0:T(8,128)(2,1)S(1)}, u32[]{:S(2)}, u32[]{:S(2)}) collective-permute-start(s16[2064,256]{1,0:T(8,128)(2,1)S(1)} %get-tuple-element.70), channel_id=1, source_target_pairs={{0,2},{1,3},{2,0},{3,1},{4,6},{5,7},{6,4},{7,5},{8,10},{9,11},{10,... | collective-permute-start | bytes 3170312 | tf_op jit(solution)/shard_map/ppermute | solution.py:359
  34.5 4.7 %collective-permute-done.9.refs_2_ = bf16[1024,256]{1,0:T(8,128)(2,1)S(1)} collective-permute-done((bf16[1024,256]{1,0:T(8,128)(2,1)S(1)}, bf16[1024,256]{1,0:T(8,128)(2,1)S(1)}, u32[]{:S(2)}, u32[]{:S(2)}) %collective-permute-start.9) | collective-permute-done | bytes 524320 | tf_op jit(solution)/shard_map/ppermute | solution.py:356
  41.0 5.7 %products.4 = (s16[1040,256]{1,0:T(8,128)(2,1)S(1)}, s16[1040,256]{1,0:T(8,128)(2,1)S(1)}, f32[17,256,256]{2,1,0:T(8,128)S(1)}) custom-call(s32[1]{0:T(128)} %constant.8.clone.1.order, s32[1]{0:T(128)} %get-tuple-element.67.count_ref, s32[104]{0:T(128)S(1)} %get-tuple-element.72.slot_ref, s32[104]{0:T(128)S(1)} %get-tuple-element.69.label_ref, ...), custom_call_target="tpu_custom_call" | custom-call | bytes 17302340 | tf_op jit(solution)/shard_map/products/pallas_call | solution.py:392
  47.9 5.7 %products.5 = (s16[1040,256]{1,0:T(8,128)(2,1)S(1)}, s16[1040,256]{1,0:T(8,128)(2,1)S(1)}, f32[17,256,256]{2,1,0:T(8,128)S(1)}) custom-call(s32[1]{0:T(128)} %constant.8.clone.1.order, s32[1]{0:T(128)} %get-tuple-element.67.count_ref, s32[104]{0:T(128)S(1)} %get-tuple-element.72.slot_ref, s32[104]{0:T(128)S(1)} %get-tuple-element.69.label_ref, ...), custom_call_target="tpu_custom_call" | custom-call | bytes 17302340 | tf_op jit(solution)/shard_map/products/pallas_call | solution.py:392
  57.4 3.6 %collective-permute-start.23 = (s16[1040,256]{1,0:T(8,128)(2,1)S(1)}, s16[1040,256]{1,0:T(8,128)(2,1)S(1)}, u32[]{:S(2)}, u32[]{:S(2)}) collective-permute-start(s16[1040,256]{1,0:T(8,128)(2,1)S(1)} %get-tuple-element.78), channel_id=1, source_target_pairs={{0,4},{1,5},{2,6},{3,7},{4,0},{5,1},{6,2},{7,3},{8,12},{9,13},{10,... | collective-permute-start | bytes 1597448 | tf_op jit(solution)/shard_map/ppermute | solution.py:359
  64.6 8.7 %collective-permute-done.18.recv_b = s16[1040,256]{1,0:T(8,128)(2,1)S(1)} collective-permute-done((s16[1040,256]{1,0:T(8,128)(2,1)S(1)}, s16[1040,256]{1,0:T(8,128)(2,1)S(1)}, u32[]{:S(2)}, u32[]{:S(2)}) %collective-permute-start.18) | collective-permute-done | bytes 532512 | tf_op jit(solution)/shard_map/ppermute | solution.py:356
  76.0 4.1 %collective-permute-done.20.recv_b = s16[528,256]{1,0:T(8,128)(2,1)S(1)} collective-permute-done((s16[528,256]{1,0:T(8,128)(2,1)S(1)}, s16[528,256]{1,0:T(8,128)(2,1)S(1)}, u32[]{:S(2)}, u32[]{:S(2)}) %collective-permute-start.20) | collective-permute-done | bytes 270368 | tf_op jit(solution)/shard_map/ppermute | solution.py:356
  80.4 1.6 %collective-permute-start.24 = (s16[528,256]{1,0:T(8,128)(2,1)S(1)}, s16[528,256]{1,0:T(8,128)(2,1)S(1)}, u32[]{:S(2)}, u32[]{:S(2)}) collective-permute-start(s16[528,256]{1,0:T(8,128)(2,1)S(1)} %get-tuple-element.90), channel_id=1, source_target_pairs={{0,2},{1,3},{2,0},{3,1},{4,6},{5,7},{6,4},{7,5},{8,10},{9,11},{10,... | collective-permute-start | bytes 811016 | tf_op jit(solution)/shard_map/ppermute | solution.py:359
  82.0 2.2 %collective-permute-done.22.recv_b = s16[528,256]{1,0:T(8,128)(2,1)S(1)} collective-permute-done((s16[528,256]{1,0:T(8,128)(2,1)S(1)}, s16[528,256]{1,0:T(8,128)(2,1)S(1)}, u32[]{:S(2)}, u32[]{:S(2)}) %collective-permute-start.22) | collective-permute-done | bytes 270368 | tf_op jit(solution)/shard_map/ppermute | solution.py:356
  84.6 1.6 %collective-permute-start.25 = (s16[528,256]{1,0:T(8,128)(2,1)S(1)}, s16[528,256]{1,0:T(8,128)(2,1)S(1)}, u32[]{:S(2)}, u32[]{:S(2)}) collective-permute-start(s16[528,256]{1,0:T(8,128)(2,1)S(1)} %get-tuple-element.94), channel_id=1, source_target_pairs={{0,2},{1,3},{2,0},{3,1},{4,6},{5,7},{6,4},{7,5},{8,10},{9,11},{10,... | collective-permute-start | bytes 811016 | tf_op jit(solution)/shard_map/ppermute | solution.py:359
  91.1 6.8 %collective-permute-done.25.recv = s16[528,256]{1,0:T(8,128)(2,1)S(1)} collective-permute-done((s16[528,256]{1,0:T(8,128)(2,1)S(1)}, s16[528,256]{1,0:T(8,128)(2,1)S(1)}, u32[]{:S(2)}, u32[]{:S(2)}) %collective-permute-start.25) | collective-permute-done | bytes 270368 | tf_op jit(solution)/shard_map/ppermute | solution.py:359
  98.7 1.6 %collective-permute-start.29 = (s16[528,256]{1,0:T(8,128)(2,1)S(1)}, s16[528,256]{1,0:T(8,128)(2,1)S(1)}, u32[]{:S(2)}, u32[]{:S(2)}) collective-permute-start(s16[528,256]{1,0:T(8,128)(2,1)S(1)} %get-tuple-element.106.refs_0_), channel_id=1, source_target_pairs={{0,16},{8,24},{16,0},{24,8},{1,17},{9,25},{17,1},{25,9},{2,18},{10... | collective-permute-start | bytes 811016 | tf_op jit(solution)/shard_map/ppermute | solution.py:356
  100.9 1.6 %collective-permute-start.34 = (s16[272,256]{1,0:T(8,128)(2,1)S(1)}, s16[272,256]{1,0:T(8,128)(2,1)S(1)}, u32[]{:S(2)}, u32[]{:S(2)}) collective-permute-start(s16[272,256]{1,0:T(8,128)(2,1)S(1)} %finish.2.refs_0_), channel_id=1, source_target_pairs={{0,24},{8,16},{16,8},{24,0},{1,25},{9,17},{17,9},{25,1},{2,26},{10... | collective-permute-start | bytes 417800 | tf_op jit(solution)/shard_map/ppermute | solution.py:356
  102.5 1.7 %collective-permute-start.33 = (s16[272,256]{1,0:T(8,128)(2,1)S(1)}, s16[272,256]{1,0:T(8,128)(2,1)S(1)}, u32[]{:S(2)}, u32[]{:S(2)}) collective-permute-start(s16[272,256]{1,0:T(8,128)(2,1)S(1)} %finish.2.refs_0_), channel_id=1, source_target_pairs={{0,16},{8,24},{16,0},{24,8},{1,17},{9,25},{17,1},{25,9},{2,18},{10... | collective-permute-start | bytes 417800 | tf_op jit(solution)/shard_map/ppermute | solution.py:356
  104.1 3.9 %collective-permute-done.30.refs_3_ = s16[528,256]{1,0:T(8,128)(2,1)S(1)} collective-permute-done((s16[528,256]{1,0:T(8,128)(2,1)S(1)}, s16[528,256]{1,0:T(8,128)(2,1)S(1)}, u32[]{:S(2)}, u32[]{:S(2)}) %collective-permute-start.30) | collective-permute-done | bytes 270368 | tf_op jit(solution)/shard_map/ppermute | solution.py:356
  108.1 3.0 %collective-permute-done.29.refs_2_ = s16[528,256]{1,0:T(8,128)(2,1)S(1)} collective-permute-done((s16[528,256]{1,0:T(8,128)(2,1)S(1)}, s16[528,256]{1,0:T(8,128)(2,1)S(1)}, u32[]{:S(2)}, u32[]{:S(2)}) %collective-permute-start.29) | collective-permute-done | bytes 270368 | tf_op jit(solution)/shard_map/ppermute | solution.py:356
  112.3 1.6 %collective-permute-start.37 = (s16[272,256]{1,0:T(8,128)(2,1)S(1)}, s16[272,256]{1,0:T(8,128)(2,1)S(1)}, u32[]{:S(2)}, u32[]{:S(2)}) collective-permute-start(s16[272,256]{1,0:T(8,128)(2,1)S(1)} %finish.3.refs_0_), channel_id=1, source_target_pairs={{0,24},{8,16},{16,8},{24,0},{1,25},{9,17},{17,9},{25,1},{2,26},{10... | collective-permute-start | bytes 417800 | tf_op jit(solution)/shard_map/ppermute | solution.py:356
  113.9 1.8 %collective-permute-start.36 = (s16[272,256]{1,0:T(8,128)(2,1)S(1)}, s16[272,256]{1,0:T(8,128)(2,1)S(1)}, u32[]{:S(2)}, u32[]{:S(2)}) collective-permute-start(s16[272,256]{1,0:T(8,128)(2,1)S(1)} %finish.3.refs_0_), channel_id=1, source_target_pairs={{0,16},{8,24},{16,0},{24,8},{1,17},{9,25},{17,1},{25,9},{2,18},{10... | collective-permute-start | bytes 417800 | tf_op jit(solution)/shard_map/ppermute | solution.py:356
  (77 shorter events, 35.0 us)
Async XLA Ops:
  0.0 12.8 %collective-permute-start.1 = (bf16[48,256,256]{2,1,0:T(8,128)(2,1)}, bf16[48,256,256]{2,1,0:T(8,128)(2,1)}, u32[]{:S(2)}, u32[]{:S(2)}) collective-permute-start(bf16[48,256,256]{2,1,0:T(8,128)(2,1)} %own_tiles.1), channel_id=1, source_target_pairs={{0,1},{1,0},{2,3},{3,2},{4,5},{5,4},{6,7},{7,6},{8,9},{9,8},{10,11... | collective-permute-start | bytes 18874376 | tf_op jit(solution)/shard_map/ppermute | solution.py:353
  2.4 18.2 %collective-permute-start.2 = (bf16[512,256]{1,0:T(8,128)(2,1)S(1)}, bf16[512,256]{1,0:T(8,128)(2,1)S(1)}, u32[]{:S(2)}, u32[]{:S(2)}) collective-permute-start(bf16[512,256]{1,0:T(8,128)(2,1)S(1)} %get-tuple-element.116.refs_0_), channel_id=1, source_target_pairs={{0,8},{8,0},{16,24},{24,16},{1,9},{9,1},{17,25},{25,17},{2,10},{10... | collective-permute-start | bytes 786440 | tf_op jit(solution)/shard_map/ppermute | solution.py:356
  5.5 15.3 %collective-permute-start.3 = (bf16[512,256]{1,0:T(8,128)(2,1)S(1)}, bf16[512,256]{1,0:T(8,128)(2,1)S(1)}, u32[]{:S(2)}, u32[]{:S(2)}) collective-permute-start(bf16[512,256]{1,0:T(8,128)(2,1)S(1)} %get-tuple-element.115.refs_0_), channel_id=1, source_target_pairs={{0,16},{8,24},{16,0},{24,8},{1,17},{9,25},{17,1},{25,9},{2,18},{10... | collective-permute-start | bytes 786440 | tf_op jit(solution)/shard_map/ppermute | solution.py:356
  7.0 13.8 %collective-permute-start.6 = (bf16[512,256]{1,0:T(8,128)(2,1)S(1)}, bf16[512,256]{1,0:T(8,128)(2,1)S(1)}, u32[]{:S(2)}, u32[]{:S(2)}) collective-permute-start(bf16[512,256]{1,0:T(8,128)(2,1)S(1)} %get-tuple-element.65), channel_id=1, source_target_pairs={{0,24},{8,16},{16,8},{24,0},{1,25},{9,17},{17,9},{25,1},{2,26},{10... | collective-permute-start | bytes 786440 | tf_op jit(solution)/shard_map/ppermute | solution.py:356
  10.1 14.5 %collective-permute-start.5 = (bf16[512,256]{1,0:T(8,128)(2,1)S(1)}, bf16[512,256]{1,0:T(8,128)(2,1)S(1)}, u32[]{:S(2)}, u32[]{:S(2)}) collective-permute-start(bf16[512,256]{1,0:T(8,128)(2,1)S(1)} %get-tuple-element.65), channel_id=1, source_target_pairs={{0,16},{8,24},{16,0},{24,8},{1,17},{9,25},{17,1},{25,9},{2,18},{10... | collective-permute-start | bytes 786440 | tf_op jit(solution)/shard_map/ppermute | solution.py:356
  12.8 11.9 %collective-permute-start.4 = (bf16[512,256]{1,0:T(8,128)(2,1)S(1)}, bf16[512,256]{1,0:T(8,128)(2,1)S(1)}, u32[]{:S(2)}, u32[]{:S(2)}) collective-permute-start(bf16[512,256]{1,0:T(8,128)(2,1)S(1)} %get-tuple-element.65), channel_id=1, source_target_pairs={{0,8},{8,0},{16,24},{24,16},{1,9},{9,1},{17,25},{25,17},{2,10},{10... | collective-permute-start | bytes 786440 | tf_op jit(solution)/shard_map/ppermute | solution.py:356
  24.8 14.3 %collective-permute-start.9 = (bf16[1024,256]{1,0:T(8,128)(2,1)S(1)}, bf16[1024,256]{1,0:T(8,128)(2,1)S(1)}, u32[]{:S(2)}, u32[]{:S(2)}) collective-permute-start(bf16[1024,256]{1,0:T(8,128)(2,1)S(1)} %join.3.refs_0_), channel_id=1, source_target_pairs={{0,16},{8,24},{16,0},{24,8},{1,17},{9,25},{17,1},{25,9},{2,18},{10... | collective-permute-start | bytes 1572872 | tf_op jit(solution)/shard_map/ppermute | solution.py:356
  26.4 14.0 %collective-permute-start.12 = (bf16[1024,256]{1,0:T(8,128)(2,1)S(1)}, bf16[1024,256]{1,0:T(8,128)(2,1)S(1)}, u32[]{:S(2)}, u32[]{:S(2)}) collective-permute-start(bf16[1024,256]{1,0:T(8,128)(2,1)S(1)} %join.4.refs_0_), channel_id=1, source_target_pairs={{0,8},{8,0},{16,24},{24,16},{1,9},{9,1},{17,25},{25,17},{2,10},{10... | collective-permute-start | bytes 1572872 | tf_op jit(solution)/shard_map/ppermute | solution.py:356
  32.8 24.0 %collective-permute-start.14 = (s16[2064,256]{1,0:T(8,128)(2,1)S(1)}, s16[2064,256]{1,0:T(8,128)(2,1)S(1)}, u32[]{:S(2)}, u32[]{:S(2)}) collective-permute-start(s16[2064,256]{1,0:T(8,128)(2,1)S(1)} %get-tuple-element.70), channel_id=1, source_target_pairs={{0,2},{1,3},{2,0},{3,1},{4,6},{5,7},{6,4},{7,5},{8,10},{9,11},{10,... | collective-permute-start | bytes 3170312 | tf_op jit(solution)/shard_map/ppermute | solution.py:359
  46.8 15.1 %collective-permute-start.16 = (s16[1040,256]{1,0:T(8,128)(2,1)S(1)}, s16[1040,256]{1,0:T(8,128)(2,1)S(1)}, u32[]{:S(2)}, u32[]{:S(2)}) collective-permute-start(s16[1040,256]{1,0:T(8,128)(2,1)S(1)} %get-tuple-element.80), channel_id=1, source_target_pairs={{0,16},{8,24},{16,0},{24,8},{1,17},{9,25},{17,1},{25,9},{2,18},{10... | collective-permute-start | bytes 1597448 | tf_op jit(solution)/shard_map/ppermute | solution.py:356
  47.9 15.0 %collective-permute-start.15 = (s16[1040,256]{1,0:T(8,128)(2,1)S(1)}, s16[1040,256]{1,0:T(8,128)(2,1)S(1)}, u32[]{:S(2)}, u32[]{:S(2)}) collective-permute-start(s16[1040,256]{1,0:T(8,128)(2,1)S(1)} %get-tuple-element.73), channel_id=1, source_target_pairs={{0,8},{8,0},{16,24},{24,16},{1,9},{9,1},{17,25},{25,17},{2,10},{10... | collective-permute-start | bytes 1597448 | tf_op jit(solution)/shard_map/ppermute | solution.py:356
  53.7 19.6 %collective-permute-start.18 = (s16[1040,256]{1,0:T(8,128)(2,1)S(1)}, s16[1040,256]{1,0:T(8,128)(2,1)S(1)}, u32[]{:S(2)}, u32[]{:S(2)}) collective-permute-start(s16[1040,256]{1,0:T(8,128)(2,1)S(1)} %get-tuple-element.84), channel_id=1, source_target_pairs={{0,16},{8,24},{16,0},{24,8},{1,17},{9,25},{17,1},{25,9},{2,18},{10... | collective-permute-start | bytes 1597448 | tf_op jit(solution)/shard_map/ppermute | solution.py:356
  54.2 20.1 %collective-permute-start.17 = (s16[1040,256]{1,0:T(8,128)(2,1)S(1)}, s16[1040,256]{1,0:T(8,128)(2,1)S(1)}, u32[]{:S(2)}, u32[]{:S(2)}) collective-permute-start(s16[1040,256]{1,0:T(8,128)(2,1)S(1)} %get-tuple-element.75), channel_id=1, source_target_pairs={{0,8},{8,0},{16,24},{24,16},{1,9},{9,1},{17,25},{25,17},{2,10},{10... | collective-permute-start | bytes 1597448 | tf_op jit(solution)/shard_map/ppermute | solution.py:356
  57.4 28.9 %collective-permute-start.23 = (s16[1040,256]{1,0:T(8,128)(2,1)S(1)}, s16[1040,256]{1,0:T(8,128)(2,1)S(1)}, u32[]{:S(2)}, u32[]{:S(2)}) collective-permute-start(s16[1040,256]{1,0:T(8,128)(2,1)S(1)} %get-tuple-element.78), channel_id=1, source_target_pairs={{0,4},{1,5},{2,6},{3,7},{4,0},{5,1},{6,2},{7,3},{8,12},{9,13},{10,... | collective-permute-start | bytes 1597448 | tf_op jit(solution)/shard_map/ppermute | solution.py:359
  63.5 16.7 %collective-permute-start.20 = (s16[528,256]{1,0:T(8,128)(2,1)S(1)}, s16[528,256]{1,0:T(8,128)(2,1)S(1)}, u32[]{:S(2)}, u32[]{:S(2)}) collective-permute-start(s16[528,256]{1,0:T(8,128)(2,1)S(1)} %get-tuple-element.88), channel_id=1, source_target_pairs={{0,8},{8,0},{16,24},{24,16},{1,9},{9,1},{17,25},{25,17},{2,10},{10... | collective-permute-start | bytes 811016 | tf_op jit(solution)/shard_map/ppermute | solution.py:356
  63.6 16.6 %collective-permute-start.19 = (s16[528,256]{1,0:T(8,128)(2,1)S(1)}, s16[528,256]{1,0:T(8,128)(2,1)S(1)}, u32[]{:S(2)}, u32[]{:S(2)}) collective-permute-start(s16[528,256]{1,0:T(8,128)(2,1)S(1)} %get-tuple-element.82), channel_id=1, source_target_pairs={{0,16},{8,24},{16,0},{24,8},{1,17},{9,25},{17,1},{25,9},{2,18},{10... | collective-permute-start | bytes 811016 | tf_op jit(solution)/shard_map/ppermute | solution.py:356
  84.6 13.4 %collective-permute-start.25 = (s16[528,256]{1,0:T(8,128)(2,1)S(1)}, s16[528,256]{1,0:T(8,128)(2,1)S(1)}, u32[]{:S(2)}, u32[]{:S(2)}) collective-permute-start(s16[528,256]{1,0:T(8,128)(2,1)S(1)} %get-tuple-element.94), channel_id=1, source_target_pairs={{0,2},{1,3},{2,0},{3,1},{4,6},{5,7},{6,4},{7,5},{8,10},{9,11},{10,... | collective-permute-start | bytes 811016 | tf_op jit(solution)/shard_map/ppermute | solution.py:359
  86.5 11.6 %collective-permute-start.27 = (s16[528,256]{1,0:T(8,128)(2,1)S(1)}, s16[528,256]{1,0:T(8,128)(2,1)S(1)}, u32[]{:S(2)}, u32[]{:S(2)}) collective-permute-start(s16[528,256]{1,0:T(8,128)(2,1)S(1)} %get-tuple-element.105.own_b), channel_id=1, source_target_pairs={{0,16},{8,24},{16,0},{24,8},{1,17},{9,25},{17,1},{25,9},{2,18},{10... | collective-permute-start | bytes 811016 | tf_op jit(solution)/shard_map/ppermute | solution.py:356
  86.9 11.2 %collective-permute-start.26 = (s16[528,256]{1,0:T(8,128)(2,1)S(1)}, s16[528,256]{1,0:T(8,128)(2,1)S(1)}, u32[]{:S(2)}, u32[]{:S(2)}) collective-permute-start(s16[528,256]{1,0:T(8,128)(2,1)S(1)} %get-tuple-element.97.own_a), channel_id=1, source_target_pairs={{0,8},{8,0},{16,24},{24,16},{1,9},{9,1},{17,25},{25,17},{2,10},{10... | collective-permute-start | bytes 811016 | tf_op jit(solution)/shard_map/ppermute | solution.py:356
  90.0 10.8 %collective-permute-start.28 = (s16[272,256]{1,0:T(8,128)(2,1)S(1)}, s16[272,256]{1,0:T(8,128)(2,1)S(1)}, u32[]{:S(2)}, u32[]{:S(2)}) collective-permute-start(s16[272,256]{1,0:T(8,128)(2,1)S(1)} %get-tuple-element.100), channel_id=1, source_target_pairs={{0,4},{1,5},{2,6},{3,7},{4,0},{5,1},{6,2},{7,3},{8,12},{9,13},{10,... | collective-permute-start | bytes 417800 | tf_op jit(solution)/shard_map/ppermute | solution.py:359
  98.7 12.3 %collective-permute-start.29 = (s16[528,256]{1,0:T(8,128)(2,1)S(1)}, s16[528,256]{1,0:T(8,128)(2,1)S(1)}, u32[]{:S(2)}, u32[]{:S(2)}) collective-permute-start(s16[528,256]{1,0:T(8,128)(2,1)S(1)} %get-tuple-element.106.refs_0_), channel_id=1, source_target_pairs={{0,16},{8,24},{16,0},{24,8},{1,17},{9,25},{17,1},{25,9},{2,18},{10... | collective-permute-start | bytes 811016 | tf_op jit(solution)/shard_map/ppermute | solution.py:356
  100.3 11.8 %collective-permute-start.31 = (s16[272,256]{1,0:T(8,128)(2,1)S(1)}, s16[272,256]{1,0:T(8,128)(2,1)S(1)}, u32[]{:S(2)}, u32[]{:S(2)}) collective-permute-start(s16[272,256]{1,0:T(8,128)(2,1)S(1)} %get-tuple-element.103), channel_id=1, source_target_pairs={{0,4},{1,5},{2,6},{3,7},{4,0},{5,1},{6,2},{7,3},{8,12},{9,13},{10,... | collective-permute-start | bytes 417800 | tf_op jit(solution)/shard_map/ppermute | solution.py:359
  100.9 14.9 %collective-permute-start.34 = (s16[272,256]{1,0:T(8,128)(2,1)S(1)}, s16[272,256]{1,0:T(8,128)(2,1)S(1)}, u32[]{:S(2)}, u32[]{:S(2)}) collective-permute-start(s16[272,256]{1,0:T(8,128)(2,1)S(1)} %finish.2.refs_0_), channel_id=1, source_target_pairs={{0,24},{8,16},{16,8},{24,0},{1,25},{9,17},{17,9},{25,1},{2,26},{10... | collective-permute-start | bytes 417800 | tf_op jit(solution)/shard_map/ppermute | solution.py:356
  102.5 13.4 %collective-permute-start.33 = (s16[272,256]{1,0:T(8,128)(2,1)S(1)}, s16[272,256]{1,0:T(8,128)(2,1)S(1)}, u32[]{:S(2)}, u32[]{:S(2)}) collective-permute-start(s16[272,256]{1,0:T(8,128)(2,1)S(1)} %finish.2.refs_0_), channel_id=1, source_target_pairs={{0,16},{8,24},{16,0},{24,8},{1,17},{9,25},{17,1},{25,9},{2,18},{10... | collective-permute-start | bytes 417800 | tf_op jit(solution)/shard_map/ppermute | solution.py:356
  (15 other events, 104.2 us)

commit v3 on v1

--- a/solution.py
+++ b/solution.py
@@ -27,7 +27,7 @@
     return (position % out_dev, target, ranking)
 
 
-def add_products(summed, arrived, slot_labels, panel_tiles):
+def add_slot_products(summed, arrived, slot_labels, panel_tiles):
     slot_count = arrived.shape[0]
     block_rows = math.gcd(slot_count, 32)
     out_dev = summed.shape[0]
@@ -86,7 +86,7 @@
     panel_tiles = gathered.reshape(gathered.shape[0] // tile_side, tile_side, gathered.shape[1])
     summed = jnp.zeros((out_dev, tile_side, gathered.shape[1]), jnp.float32)
     arrived = lax.all_to_all(outgoing, "wide", split_axis=0, concat_axis=0, tiled=True)
-    summed = add_products(summed, arrived, arrived_labels, panel_tiles)
+    summed = add_slot_products(summed, arrived, arrived_labels, panel_tiles)
     summed = lax.psum(summed, "grp")
     return summed.reshape(out_dev * tile_side, gathered.shape[1])
 
@@ -137,53 +137,66 @@
 
 def hold_kernel(
     order, own_ref, sib_ref, own_tiles, sib_tiles,
-    count_ref, plane_ref, line_ref, label_ref, out, sems,
+    count_ref, plane_ref, line_ref, label_ref, plane_order, line_order, out, sems,
 ):
     tile_dev = own_tiles.shape[0]
     sums = (own_ref.shape[0] - 2 * tile_dev) // 2
     shard, out_dev = 4, 4
+    room = 2 * tile_dev + UNROLL
     x, y, z_low, _ = here()
     g, core = lax.axis_index("grp"), lax.axis_index("wide") % 2
 
     def copy(tiles, which, at):
         return pltpu.make_async_copy(tiles.at[which], out.at[at], sems.at[at])
 
-    def scan(tiles, index_ref, count):
-        def one(i, count):
+    def scan(tiles, index_ref, counts):
+        def one(i, counts):
             position = own_ref[2 * tile_dev + index_ref[i]]
             k = index_ref[tile_dev + i]
             owner, local = lax.div(position, out_dev), lax.rem(position, out_dev)
             match = lax.rem(owner, 2) == core
 
+            odd, to_z = lax.rem(lax.div(owner, 2), 2), lax.div(owner, 4)
+            bit_x, bit_y = lax.rem(local, 2), lax.div(local, 2)
+            kept = [
+                jnp.where(odd == 1, bit_y == y, bit_x == x),
+                odd == z_low,
+            ]
+
             @pl.when(match)
             def _():
-                copy(tiles, i, count).start()
-                odd, to_z = lax.rem(lax.div(owner, 2), 2), lax.div(owner, 4)
-                bit_x, bit_y = lax.rem(local, 2), lax.div(local, 2)
-                first = jnp.where(odd == 1, bit_y == y, bit_x == x)
+                copy(tiles, i, counts[0]).start()
                 second = jnp.where(odd == 1, bit_x, bit_y)
-                plane_ref[count] = (
-                    jnp.where(first, 0, sums // 2) + odd * (sums // 4) + 2 * to_z + second
-                )
-                line_ref[count] = (
-                    jnp.where(odd == z_low, 0, sums // 2) + to_z * out_dev + local
-                )
+                places = [odd * (sums // 4) + 2 * to_z + second, to_z * out_dev + local]
+                for ref, order_ref, keep, place, sent in (
+                    (plane_ref, plane_order, kept[0], places[0], counts[1]),
+                    (line_ref, line_order, kept[1], places[1], counts[2]),
+                ):
+                    ref[counts[0]] = place
+                    order_ref[jnp.where(keep, room + counts[0] - sent, sent)] = counts[0]
                 apart, inner = lax.div(k, shard) ^ g, lax.rem(k, shard)
                 half = shard // 2
                 crossed = jnp.where(lax.div(inner, half) == core, 0, half) + lax.rem(inner, half)
-                label_ref[count] = jnp.where(apart == 0, inner, apart * shard + crossed)
-
-            return count + match.astype(jnp.int32)
-
-        return lax.fori_loop(0, tile_dev, one, count)
-
-    count = scan(own_tiles, own_ref, 0)
-    count = scan(sib_tiles, sib_ref, count)
-    count_ref[0] = count
-    for i in range(UNROLL):
-        plane_ref[count + i] = sums
-        line_ref[count + i] = sums
-        label_ref[count + i] = 0
+                label_ref[counts[0]] = jnp.where(apart == 0, inner, apart * shard + crossed)
+
+            more = [match, match & ~kept[0], match & ~kept[1]]
+            return tuple(c + m.astype(jnp.int32) for c, m in zip(counts, more))
+
+        return lax.fori_loop(0, tile_dev, one, counts)
+
+    counts = scan(own_tiles, own_ref, (0, 0, 0))
+    counts = scan(sib_tiles, sib_ref, counts)
+    count = counts[0]
+    for i in range(3):
+        count_ref[i] = counts[i]
+    spare = 2 * tile_dev
+    plane_ref[spare] = sums // 2
+    line_ref[spare] = sums // 2
+    label_ref[spare] = 0
+    for order_ref, sent in ((plane_order, counts[1]), (line_order, counts[2])):
+        for i in range(UNROLL):
+            order_ref[sent + i] = spare
+            order_ref[room + count - sent + i] = spare
 
     @pl.loop(0, count)
     def _(i):
@@ -197,39 +210,45 @@
         out[pl.ds(i * rows, rows), :] = part[...]
 
 
-def products_kernel(
-    fill, chunk, order, count_ref, slot_ref, label_ref, tiles, own_panel, *refs
+def add_products(count, first, order_ref, slot_ref, label_ref, tiles, stack, sums):
+    @pl.loop(0, sums.shape[0])
+    def _(i):
+        sums[i] = jnp.zeros(sums.shape[1:], jnp.float32)
+
+    @pl.loop(0, lax.div(count + UNROLL - 1, UNROLL))
+    def _(i):
+        entries = [order_ref[first + i * UNROLL + u] for u in range(UNROLL)]
+        found = [
+            jnp.dot(tiles[e], stack[label_ref[e]], preferred_element_type=jnp.float32)
+            for e in entries
+        ]
+        for e, product in zip(entries, found):
+            sums[slot_ref[e]] += product
+
+
+def sent_kernel(
+    fill, chunk, which, order, count_ref, order_ref, slot_ref, label_ref,
+    tiles, own_panel, *refs
 ):
-    parts = refs[: 1 + max(which for which, _, _ in fill)]
-    *sends, sums, stack = refs[len(parts) :]
+    parts = refs[: 1 + max(part for part, _, _ in fill)]
+    *sends, stack, sums = refs[len(parts) :]
     side, width = stack.shape[1:]
     for t in range(own_panel.shape[0] // side):
         stack[t] = own_panel[pl.ds(t * side, side), pl.ds(chunk * width, width)]
-    for which, t, at in fill:
-        stack[at] = parts[which][pl.ds(t * side, side), :]
-
-    @pl.loop(0, sums.shape[0])
-    def _(i):
-        sums[i] = jnp.zeros(sums.shape[1:], jnp.float32)
-
-    @pl.loop(0, lax.div(count_ref[0] + UNROLL - 1, UNROLL))
-    def _(i):
-        found = [
-            jnp.dot(
-                tiles[i * UNROLL + u],
-                stack[label_ref[i * UNROLL + u]],
-                preferred_element_type=jnp.float32,
-            )
-            for u in range(UNROLL)
-        ]
-        for u in range(UNROLL):
-            sums[slot_ref[i * UNROLL + u]] += found[u]
-
-    sent = sums.shape[0] // 2
+    for part, t, at in fill:
+        stack[at] = parts[part][pl.ds(t * side, side), :]
+    add_products(count_ref[which], 0, order_ref, slot_ref, label_ref, tiles, stack, sums)
+    sent = 0
     for send in sends:
         count = (send.shape[0] - CODE_ROWS) // side
         put_coded(send, (sums[sent + i] for i in range(count)))
         sent += count
+
+
+def kept_kernel(which, order, count_ref, order_ref, slot_ref, label_ref, tiles, stack, sums):
+    count = count_ref[0] - count_ref[which]
+    room = tiles.shape[0]
+    add_products(count, room, order_ref, slot_ref, label_ref, tiles, stack, sums)
 
 
 def plane_kernel(order, recv_a, recv_b, kept, send_a, send_b, keep):
@@ -431,21 +450,30 @@
             + places(2, in_second, 0)
             + places(3, in_second, part)
         )
-        return fill, [joined, to_core(joined), second, to_core(second)]
-
-    def products(j, slot, sends, fill, parts):
-        *sends, kept = call(
-            functools.partial(products_kernel, tuple(fill), j),
-            "products",
-            [*sends, stack_of(sums + 1, plain)],
-            counts,
-            slot,
-            label,
+        return fill, [joined, to_core(joined), second]
+
+    def products(j, which, sends, fill, parts):
+        lists = counts, orders[which], slots[which], label
+        *sends, stacked = call(
+            functools.partial(sent_kernel, tuple(fill), j, which),
+            "products_sent",
+            [*sends, shape((4 * shard, side, CHUNK), panel.dtype)],
+            *lists,
             held,
             panel,
             *parts,
-            smem=3,
-            extra=[pltpu.VMEM((4 * shard, side, CHUNK), panel.dtype)],
+            smem=4,
+            extra=[pltpu.VMEM((half + 1, side, CHUNK), jnp.float32)],
+            mib=24,
+        )
+        (kept,) = call(
+            functools.partial(kept_kernel, which),
+            "products_kept",
+            [stack_of(half + 1, plain)],
+            *lists,
+            held,
+            stacked,
+            smem=4,
             mib=24,
         )
         return *sends, kept
@@ -469,28 +497,34 @@
 
     eighth = quarter // 2
     entries = shape((2 * tile_dev + UNROLL,), jnp.int32)
-    counts, in_plane, in_line, label, held = call(
+    twice = shape((2 * entries.shape[0],), jnp.int32)
+    counts, in_plane, in_line, label, plane_order, line_order, held = call(
         hold_kernel,
         "hold",
-        [shape((1,), jnp.int32)]
+        [shape((3,), jnp.int32)]
         + [entries] * 3
+        + [twice] * 2
         + [pltpu.VMEM((2 * tile_dev + UNROLL, side, side), tiles.dtype)],
         own_index,
         sib_index,
         *[pltpu.with_memory_space_constraint(v, pltpu.HBM) for v in (tiles, sib_tiles)],
         in_specs=in_any(1) + in_smem(2) + in_any(2),
-        out_specs=in_smem(4) + in_vmem(1),
+        out_specs=in_smem(6) + in_vmem(1),
         extra=[pltpu.SemaphoreType.DMA((2 * tile_dev,))],
         mib=8,
     )
     last = held
+    slots, orders = {1: in_plane, 2: in_line}, {1: plane_order, 2: line_order}
     pairs = {j: pair(j) for j in (1, 2)}
 
-    send, keep_0 = products(0, in_line, [coded(half)], *join(0))
+    send, keep_0 = products(0, 2, [coded(half)], *join(0))
     sent_0 = send
     sent, keep = {}, {}
     for j in (1, 2):
-        send_a, send_b, keep[j] = products(j, in_plane, [coded(quarter)] * 2, *pairs[j])
+        fill, (*parts, second) = pairs[j]
+        second = lax.optimization_barrier((second, keep_0))[0]
+        parts += [second, to_core(second)]
+        send_a, send_b, keep[j] = products(j, 1, [coded(quarter)] * 2, fill, parts)
         sent[j] = send_a, send_b
 
     sent_0, keep_0 = call(

time: 121 us -> 119 us (0.983)
  starting transfers between devices: 42.7 us -> 39.7 us
    ppermute x25, waiting for transfers between devices: 28.3 us -> 30.7 us  [to_grp(): return lax.ppermute(v, 'grp', [(i, i ^ d) for i in range(4)])]
    ppermute x25, starting transfers between devices: 33.3 us -> 31.5 us  [to_grp(): return lax.ppermute(v, 'grp', [(i, i ^ d) for i in range(4)])]
    ppermute x6, waiting for transfers between devices: 13 us -> 11.6 us  [to_line(): return lax.ppermute(v, 'wide', [(i, i ^ 2 << b) for i in range(wide_count)])]
    ppermute x7, starting transfers between devices: 2.37 us -> 1.1 us  [to_core(): return lax.ppermute(v, 'wide', [(i, i ^ 1) for i in range(wide_count)])]
    pallas_call x21 -> x24, Pallas kernels: 30.2 us -> 29.8 us  [call(): pl.pallas_call(body, in_specs=more.pop('in_specs', in_any(1) + in_smem(sm...]
  transfers between devices with their start and end apart: 38 -> 38, of which waited for: 19 -> 17; matrix products, arithmetic and copies ran while one was open for 2% -> 2% of each run, Pallas kernels for 24% -> 24%
where the time goes in v3:
time: 119 us; the launch traced here: 118 us
  waiting for transfers between devices  46.2 us (39%)
  starting transfers between devices  39.7 us (33%)
  Pallas kernels  29.8 us (25%)
    ppermute x25, starting transfers between devices, to_grp(): return lax.ppermute(v, 'grp', [(i, i ^ d) for i in range(4)])  31.5 us
    ppermute x25, waiting for transfers between devices, to_grp(): return lax.ppermute(v, 'grp', [(i, i ^ d) for i in range(4)])  30.7 us
    pallas_call x24, Pallas kernels, call(): pl.pallas_call(body, in_specs=more.pop('in_specs', in_any(1) + in_smem(sm...  29.8 us
    ppermute x6, waiting for transfers between devices, to_line(): return lax.ppermute(v, 'wide', [(i, i ^ 2 << b) for i in range(wide_count)])  11.6 us
    ppermute x6, starting transfers between devices, to_line(): return lax.ppermute(v, 'wide', [(i, i ^ 2 << b) for i in range(wide_count)])  7.07 us
    ppermute x7, waiting for transfers between devices, to_core(): return lax.ppermute(v, 'wide', [(i, i ^ 1) for i in range(wide_count)])  3.95 us
  transfers between devices with their start and end apart: 38, of which 17 were waited for; matrix products, arithmetic and copies ran while one was open for 2% of the time, Pallas kernels for 24%

profile of v3, /device:TPU:0, one launch (start us, length us, event | category | flops | bytes accessed | tf_op | source)
XLA Modules:
  0.0 118.1 jit_solution(12342724158241772982)
XLA Ops:
  2.4 3.0 %collective-permute-start.2 = (bf16[512,256]{1,0:T(8,128)(2,1)S(1)}, bf16[512,256]{1,0:T(8,128)(2,1)S(1)}, u32[]{:S(2)}, u32[]{:S(2)}) collective-permute-start(bf16[512,256]{1,0:T(8,128)(2,1)S(1)} %get-tuple-element.130.refs_0_), channel_id=1, source_target_pairs={{0,8},{8,0},{16,24},{24,16},{1,9},{9,1},{17,25},{25,17},{2,10},{10... | collective-permute-start | bytes 786440 | tf_op jit(solution)/shard_map/ppermute | solution.py:375
  7.0 3.1 %collective-permute-done.sib_ref = s32[128]{0:T(128)S(1)} collective-permute-done((s32[128]{0:T(128)S(1)}, s32[128]{0:T(128)S(1)}, u32[]{:S(2)}, u32[]{:S(2)}) %collective-permute-start) | collective-permute-done | bytes 544 | tf_op jit(solution)/shard_map/ppermute | solution.py:372
  10.1 2.6 %collective-permute-start.5 = (bf16[512,256]{1,0:T(8,128)(2,1)S(1)}, bf16[512,256]{1,0:T(8,128)(2,1)S(1)}, u32[]{:S(2)}, u32[]{:S(2)}) collective-permute-start(bf16[512,256]{1,0:T(8,128)(2,1)S(1)} %get-tuple-element.72), channel_id=1, source_target_pairs={{0,16},{8,24},{16,0},{24,8},{1,17},{9,25},{17,1},{25,9},{2,18},{10... | collective-permute-start | bytes 786440 | tf_op jit(solution)/shard_map/ppermute | solution.py:375
  14.3 6.7 %hold.1 = (s32[3]{0:T(128)S(1)}, s32[104]{0:T(128)S(1)}, s32[104]{0:T(128)S(1)}, s32[104]{0:T(128)S(1)}, s32[208]{0:T(256)S(1)}, /*index=5*/s32[208]{0:T(256)S(1)}, bf16[104,256,256]{2,1,0:T(8,128)(2,1)S(1)}) custom-call(s32[1]{0:T(128)} %constant.8.clone.1.order, s32[128]{0:T(128)S(1)} %pad_add_fusion.own_ref, s32[128]{0:T(128)S(1)} %collective-permute-done.sib_ref, ...), custom_call_target="tpu_custom_call" | custom-call | bytes 12583936 | tf_op jit(solution)/shard_map/hold/pallas_call | solution.py:411
  21.1 3.5 %collective-permute-done.5.refs_1_ = bf16[512,256]{1,0:T(8,128)(2,1)S(1)} collective-permute-done((bf16[512,256]{1,0:T(8,128)(2,1)S(1)}, bf16[512,256]{1,0:T(8,128)(2,1)S(1)}, u32[]{:S(2)}, u32[]{:S(2)}) %collective-permute-start.5) | collective-permute-done | bytes 262176 | tf_op jit(solution)/shard_map/ppermute | solution.py:375
  27.1 3.7 %products_sent.3 = (s16[2064,256]{1,0:T(8,128)(2,1)S(1)}, bf16[16,256,256]{2,1,0:T(8,128)(2,1)S(1)}) custom-call(s32[1]{0:T(128)} %constant.8.clone.1.order, s32[3]{0:T(128)S(1)} %get-tuple-element.74.count_ref, s32[208]{0:T(256)S(1)} %get-tuple-element.75.order_ref, s32[104]{0:T(128)S(1)} %get-tuple-element.76.slot_ref, ...), custom_call_target="tpu_custom_call" | custom-call | bytes 16778892 | tf_op jit(solution)/shard_map/products_sent/pallas_call | solution.py:411
  33.2 6.0 %collective-permute-done.9.refs_2_ = bf16[1024,256]{1,0:T(8,128)(2,1)S(1)} collective-permute-done((bf16[1024,256]{1,0:T(8,128)(2,1)S(1)}, bf16[1024,256]{1,0:T(8,128)(2,1)S(1)}, u32[]{:S(2)}, u32[]{:S(2)}) %collective-permute-start.9) | collective-permute-done | bytes 524320 | tf_op jit(solution)/shard_map/ppermute | solution.py:375
  41.0 3.2 %products_sent.4 = (s16[1040,256]{1,0:T(8,128)(2,1)S(1)}, s16[1040,256]{1,0:T(8,128)(2,1)S(1)}, bf16[16,256,256]{2,1,0:T(8,128)(2,1)S(1)}) custom-call(s32[1]{0:T(128)} %constant.8.clone.1.order, s32[3]{0:T(128)S(1)} %get-tuple-element.74.count_ref, s32[208]{0:T(256)S(1)} %get-tuple-element.82.order_ref, s32[104]{0:T(128)S(1)} %get-tuple-element.83.slot_ref, ...), custom_call_target="tpu_custom_call" | custom-call | bytes 17303180 | tf_op jit(solution)/shard_map/products_sent/pallas_call | solution.py:411
  45.9 2.2 %products_kept.4.kept = f32[9,256,256]{2,1,0:T(8,128)S(1)} custom-call(s32[1]{0:T(128)} %constant.8.clone.1.order, s32[3]{0:T(128)S(1)} %get-tuple-element.74.count_ref, s32[208]{0:T(256)S(1)} %get-tuple-element.82.order_ref, s32[104]{0:T(128)S(1)} %get-tuple-element.83.slot_ref, s32[104]{0:T(128)S(1)} %get-tuple-element.77.label_ref, ...), custom_call_target="tpu_custom_call" | custom-call | bytes 15730316 | tf_op jit(solution)/shard_map/products_kept/pallas_call | solution.py:411
  48.1 3.1 %products_sent.5 = (s16[1040,256]{1,0:T(8,128)(2,1)S(1)}, s16[1040,256]{1,0:T(8,128)(2,1)S(1)}, bf16[16,256,256]{2,1,0:T(8,128)(2,1)S(1)}) custom-call(s32[1]{0:T(128)} %constant.8.clone.1.order, s32[3]{0:T(128)S(1)} %get-tuple-element.74.count_ref, s32[208]{0:T(256)S(1)} %get-tuple-element.82.order_ref, s32[104]{0:T(128)S(1)} %get-tuple-element.83.slot_ref, ...), custom_call_target="tpu_custom_call" | custom-call | bytes 17303180 | tf_op jit(solution)/shard_map/products_sent/pallas_call | solution.py:411
  52.0 2.3 %collective-permute-start.17 = (s16[1040,256]{1,0:T(8,128)(2,1)S(1)}, s16[1040,256]{1,0:T(8,128)(2,1)S(1)}, u32[]{:S(2)}, u32[]{:S(2)}) collective-permute-start(s16[1040,256]{1,0:T(8,128)(2,1)S(1)} %get-tuple-element.90), channel_id=1, source_target_pairs={{0,8},{8,0},{16,24},{24,16},{1,9},{9,1},{17,25},{25,17},{2,10},{10... | collective-permute-start | bytes 1597448 | tf_op jit(solution)/shard_map/ppermute | solution.py:375
  54.3 2.4 %products_kept.5.kept = f32[9,256,256]{2,1,0:T(8,128)S(1)} custom-call(s32[1]{0:T(128)} %constant.8.clone.1.order, s32[3]{0:T(128)S(1)} %get-tuple-element.74.count_ref, s32[208]{0:T(256)S(1)} %get-tuple-element.82.order_ref, s32[104]{0:T(128)S(1)} %get-tuple-element.83.slot_ref, s32[104]{0:T(128)S(1)} %get-tuple-element.77.label_ref, ...), custom_call_target="tpu_custom_call" | custom-call | bytes 15730316 | tf_op jit(solution)/shard_map/products_kept/pallas_call | solution.py:411
  57.3 3.2 %collective-permute-start.21 = (s16[1040,256]{1,0:T(8,128)(2,1)S(1)}, s16[1040,256]{1,0:T(8,128)(2,1)S(1)}, u32[]{:S(2)}, u32[]{:S(2)}) collective-permute-start(s16[1040,256]{1,0:T(8,128)(2,1)S(1)} %get-tuple-element.94), channel_id=1, source_target_pairs={{0,4},{1,5},{2,6},{3,7},{4,0},{5,1},{6,2},{7,3},{8,12},{9,13},{10,... | collective-permute-start | bytes 1597448 | tf_op jit(solution)/shard_map/ppermute | solution.py:378
  63.1 7.5 %collective-permute-done.18.recv_b = s16[1040,256]{1,0:T(8,128)(2,1)S(1)} collective-permute-done((s16[1040,256]{1,0:T(8,128)(2,1)S(1)}, s16[1040,256]{1,0:T(8,128)(2,1)S(1)}, u32[]{:S(2)}, u32[]{:S(2)}) %collective-permute-start.18) | collective-permute-done | bytes 532512 | tf_op jit(solution)/shard_map/ppermute | solution.py:375
  74.1 3.4 %collective-permute-done.20.recv_b = s16[528,256]{1,0:T(8,128)(2,1)S(1)} collective-permute-done((s16[528,256]{1,0:T(8,128)(2,1)S(1)}, s16[528,256]{1,0:T(8,128)(2,1)S(1)}, u32[]{:S(2)}, u32[]{:S(2)}) %collective-permute-start.20) | collective-permute-done | bytes 270368 | tf_op jit(solution)/shard_map/ppermute | solution.py:375
  77.7 2.2 %collective-permute-start.24 = (s16[528,256]{1,0:T(8,128)(2,1)S(1)}, s16[528,256]{1,0:T(8,128)(2,1)S(1)}, u32[]{:S(2)}, u32[]{:S(2)}) collective-permute-start(s16[528,256]{1,0:T(8,128)(2,1)S(1)} %get-tuple-element.104), channel_id=1, source_target_pairs={{0,2},{1,3},{2,0},{3,1},{4,6},{5,7},{6,4},{7,5},{8,10},{9,11},{10,... | collective-permute-start | bytes 811016 | tf_op jit(solution)/shard_map/ppermute | solution.py:378
  80.0 2.3 %collective-permute-done.21.recv = s16[1040,256]{1,0:T(8,128)(2,1)S(1)} collective-permute-done((s16[1040,256]{1,0:T(8,128)(2,1)S(1)}, s16[1040,256]{1,0:T(8,128)(2,1)S(1)}, u32[]{:S(2)}, u32[]{:S(2)}) %collective-permute-start.21) | collective-permute-done | bytes 532512 | tf_op jit(solution)/shard_map/ppermute | solution.py:378
  82.6 2.1 %collective-permute-start.26 = (s16[528,256]{1,0:T(8,128)(2,1)S(1)}, s16[528,256]{1,0:T(8,128)(2,1)S(1)}, u32[]{:S(2)}, u32[]{:S(2)}) collective-permute-start(s16[528,256]{1,0:T(8,128)(2,1)S(1)} %get-tuple-element.116.own_b), channel_id=1, source_target_pairs={{0,16},{8,24},{16,0},{24,8},{1,17},{9,25},{17,1},{25,9},{2,18},{10... | collective-permute-start | bytes 811016 | tf_op jit(solution)/shard_map/ppermute | solution.py:375
  85.2 2.8 %collective-permute-done.24.recv = s16[528,256]{1,0:T(8,128)(2,1)S(1)} collective-permute-done((s16[528,256]{1,0:T(8,128)(2,1)S(1)}, s16[528,256]{1,0:T(8,128)(2,1)S(1)}, u32[]{:S(2)}, u32[]{:S(2)}) %collective-permute-start.24) | collective-permute-done | bytes 270368 | tf_op jit(solution)/shard_map/ppermute | solution.py:378
  93.7 4.0 %collective-permute-done.27.recv = s16[272,256]{1,0:T(8,128)(2,1)S(1)} collective-permute-done((s16[272,256]{1,0:T(8,128)(2,1)S(1)}, s16[272,256]{1,0:T(8,128)(2,1)S(1)}, u32[]{:S(2)}, u32[]{:S(2)}) %collective-permute-start.27) | collective-permute-done | bytes 139296 | tf_op jit(solution)/shard_map/ppermute | solution.py:378
  102.7 2.4 %collective-permute-done.31.recv = s16[272,256]{1,0:T(8,128)(2,1)S(1)} collective-permute-done((s16[272,256]{1,0:T(8,128)(2,1)S(1)}, s16[272,256]{1,0:T(8,128)(2,1)S(1)}, u32[]{:S(2)}, u32[]{:S(2)}) %collective-permute-start.31) | collective-permute-done | bytes 139296 | tf_op jit(solution)/shard_map/ppermute | solution.py:378
  105.2 1.9 %collective-permute-start.37 = (s16[272,256]{1,0:T(8,128)(2,1)S(1)}, s16[272,256]{1,0:T(8,128)(2,1)S(1)}, u32[]{:S(2)}, u32[]{:S(2)}) collective-permute-start(s16[272,256]{1,0:T(8,128)(2,1)S(1)} %finish.3.refs_0_), channel_id=1, source_target_pairs={{0,24},{8,16},{16,8},{24,0},{1,25},{9,17},{17,9},{25,1},{2,26},{10... | collective-permute-start | bytes 417800 | tf_op jit(solution)/shard_map/ppermute | solution.py:375
  111.4 3.6 %collective-permute-done.36.refs_2_ = s16[272,256]{1,0:T(8,128)(2,1)S(1)} collective-permute-done((s16[272,256]{1,0:T(8,128)(2,1)S(1)}, s16[272,256]{1,0:T(8,128)(2,1)S(1)}, u32[]{:S(2)}, u32[]{:S(2)}) %collective-permute-start.36) | collective-permute-done | bytes 139296 | tf_op jit(solution)/shard_map/ppermute | solution.py:375
  115.0 1.9 %collective-permute-done.35.refs_1_ = s16[272,256]{1,0:T(8,128)(2,1)S(1)} collective-permute-done((s16[272,256]{1,0:T(8,128)(2,1)S(1)}, s16[272,256]{1,0:T(8,128)(2,1)S(1)}, u32[]{:S(2)}, u32[]{:S(2)}) %collective-permute-start.35) | collective-permute-done | bytes 139296 | tf_op jit(solution)/shard_map/ppermute | solution.py:375
  (80 shorter events, 38.3 us)
Async XLA Ops:
  0.0 12.8 %collective-permute-start.1 = (bf16[48,256,256]{2,1,0:T(8,128)(2,1)}, bf16[48,256,256]{2,1,0:T(8,128)(2,1)}, u32[]{:S(2)}, u32[]{:S(2)}) collective-permute-start(bf16[48,256,256]{2,1,0:T(8,128)(2,1)} %own_tiles.1), channel_id=1, source_target_pairs={{0,1},{1,0},{2,3},{3,2},{4,5},{5,4},{6,7},{7,6},{8,9},{9,8},{10,11... | collective-permute-start | bytes 18874376 | tf_op jit(solution)/shard_map/ppermute | solution.py:372
  2.4 18.6 %collective-permute-start.2 = (bf16[512,256]{1,0:T(8,128)(2,1)S(1)}, bf16[512,256]{1,0:T(8,128)(2,1)S(1)}, u32[]{:S(2)}, u32[]{:S(2)}) collective-permute-start(bf16[512,256]{1,0:T(8,128)(2,1)S(1)} %get-tuple-element.130.refs_0_), channel_id=1, source_target_pairs={{0,8},{8,0},{16,24},{24,16},{1,9},{9,1},{17,25},{25,17},{2,10},{10... | collective-permute-start | bytes 786440 | tf_op jit(solution)/shard_map/ppermute | solution.py:375
  5.5 15.6 %collective-permute-start.3 = (bf16[512,256]{1,0:T(8,128)(2,1)S(1)}, bf16[512,256]{1,0:T(8,128)(2,1)S(1)}, u32[]{:S(2)}, u32[]{:S(2)}) collective-permute-start(bf16[512,256]{1,0:T(8,128)(2,1)S(1)} %get-tuple-element.129.refs_0_), channel_id=1, source_target_pairs={{0,16},{8,24},{16,0},{24,8},{1,17},{9,25},{17,1},{25,9},{2,18},{10... | collective-permute-start | bytes 786440 | tf_op jit(solution)/shard_map/ppermute | solution.py:375
  7.0 14.1 %collective-permute-start.6 = (bf16[512,256]{1,0:T(8,128)(2,1)S(1)}, bf16[512,256]{1,0:T(8,128)(2,1)S(1)}, u32[]{:S(2)}, u32[]{:S(2)}) collective-permute-start(bf16[512,256]{1,0:T(8,128)(2,1)S(1)} %get-tuple-element.72), channel_id=1, source_target_pairs={{0,24},{8,16},{16,8},{24,0},{1,25},{9,17},{17,9},{25,1},{2,26},{10... | collective-permute-start | bytes 786440 | tf_op jit(solution)/shard_map/ppermute | solution.py:375
  10.1 14.5 %collective-permute-start.5 = (bf16[512,256]{1,0:T(8,128)(2,1)S(1)}, bf16[512,256]{1,0:T(8,128)(2,1)S(1)}, u32[]{:S(2)}, u32[]{:S(2)}) collective-permute-start(bf16[512,256]{1,0:T(8,128)(2,1)S(1)} %get-tuple-element.72), channel_id=1, source_target_pairs={{0,16},{8,24},{16,0},{24,8},{1,17},{9,25},{17,1},{25,9},{2,18},{10... | collective-permute-start | bytes 786440 | tf_op jit(solution)/shard_map/ppermute | solution.py:375
  12.8 11.9 %collective-permute-start.4 = (bf16[512,256]{1,0:T(8,128)(2,1)S(1)}, bf16[512,256]{1,0:T(8,128)(2,1)S(1)}, u32[]{:S(2)}, u32[]{:S(2)}) collective-permute-start(bf16[512,256]{1,0:T(8,128)(2,1)S(1)} %get-tuple-element.72), channel_id=1, source_target_pairs={{0,8},{8,0},{16,24},{24,16},{1,9},{9,1},{17,25},{25,17},{2,10},{10... | collective-permute-start | bytes 786440 | tf_op jit(solution)/shard_map/ppermute | solution.py:375
  24.8 14.3 %collective-permute-start.9 = (bf16[1024,256]{1,0:T(8,128)(2,1)S(1)}, bf16[1024,256]{1,0:T(8,128)(2,1)S(1)}, u32[]{:S(2)}, u32[]{:S(2)}) collective-permute-start(bf16[1024,256]{1,0:T(8,128)(2,1)S(1)} %join.3.refs_0_), channel_id=1, source_target_pairs={{0,16},{8,24},{16,0},{24,8},{1,17},{9,25},{17,1},{25,9},{2,18},{10... | collective-permute-start | bytes 1572872 | tf_op jit(solution)/shard_map/ppermute | solution.py:375
  26.4 14.0 %collective-permute-start.12 = (bf16[1024,256]{1,0:T(8,128)(2,1)S(1)}, bf16[1024,256]{1,0:T(8,128)(2,1)S(1)}, u32[]{:S(2)}, u32[]{:S(2)}) collective-permute-start(bf16[1024,256]{1,0:T(8,128)(2,1)S(1)} %join.4.refs_0_), channel_id=1, source_target_pairs={{0,8},{8,0},{16,24},{24,16},{1,9},{9,1},{17,25},{25,17},{2,10},{10... | collective-permute-start | bytes 1572872 | tf_op jit(solution)/shard_map/ppermute | solution.py:375
  30.8 26.0 %collective-permute-start.14 = (s16[2064,256]{1,0:T(8,128)(2,1)S(1)}, s16[2064,256]{1,0:T(8,128)(2,1)S(1)}, u32[]{:S(2)}, u32[]{:S(2)}) collective-permute-start(s16[2064,256]{1,0:T(8,128)(2,1)S(1)} %get-tuple-element.78), channel_id=1, source_target_pairs={{0,2},{1,3},{2,0},{3,1},{4,6},{5,7},{6,4},{7,5},{8,10},{9,11},{10,... | collective-permute-start | bytes 3170312 | tf_op jit(solution)/shard_map/ppermute | solution.py:378
  44.2 16.3 %collective-permute-start.16 = (s16[1040,256]{1,0:T(8,128)(2,1)S(1)}, s16[1040,256]{1,0:T(8,128)(2,1)S(1)}, u32[]{:S(2)}, u32[]{:S(2)}) collective-permute-start(s16[1040,256]{1,0:T(8,128)(2,1)S(1)} %get-tuple-element.96), channel_id=1, source_target_pairs={{0,16},{8,24},{16,0},{24,8},{1,17},{9,25},{17,1},{25,9},{2,18},{10... | collective-permute-start | bytes 1597448 | tf_op jit(solution)/shard_map/ppermute | solution.py:375
  45.3 15.2 %collective-permute-start.15 = (s16[1040,256]{1,0:T(8,128)(2,1)S(1)}, s16[1040,256]{1,0:T(8,128)(2,1)S(1)}, u32[]{:S(2)}, u32[]{:S(2)}) collective-permute-start(s16[1040,256]{1,0:T(8,128)(2,1)S(1)} %get-tuple-element.85), channel_id=1, source_target_pairs={{0,8},{8,0},{16,24},{24,16},{1,9},{9,1},{17,25},{25,17},{2,10},{10... | collective-permute-start | bytes 1597448 | tf_op jit(solution)/shard_map/ppermute | solution.py:375
  51.2 19.4 %collective-permute-start.18 = (s16[1040,256]{1,0:T(8,128)(2,1)S(1)}, s16[1040,256]{1,0:T(8,128)(2,1)S(1)}, u32[]{:S(2)}, u32[]{:S(2)}) collective-permute-start(s16[1040,256]{1,0:T(8,128)(2,1)S(1)} %get-tuple-element.99), channel_id=1, source_target_pairs={{0,16},{8,24},{16,0},{24,8},{1,17},{9,25},{17,1},{25,9},{2,18},{10... | collective-permute-start | bytes 1597448 | tf_op jit(solution)/shard_map/ppermute | solution.py:375
  52.0 19.6 %collective-permute-start.17 = (s16[1040,256]{1,0:T(8,128)(2,1)S(1)}, s16[1040,256]{1,0:T(8,128)(2,1)S(1)}, u32[]{:S(2)}, u32[]{:S(2)}) collective-permute-start(s16[1040,256]{1,0:T(8,128)(2,1)S(1)} %get-tuple-element.90), channel_id=1, source_target_pairs={{0,8},{8,0},{16,24},{24,16},{1,9},{9,1},{17,25},{25,17},{2,10},{10... | collective-permute-start | bytes 1597448 | tf_op jit(solution)/shard_map/ppermute | solution.py:375
  57.3 25.0 %collective-permute-start.21 = (s16[1040,256]{1,0:T(8,128)(2,1)S(1)}, s16[1040,256]{1,0:T(8,128)(2,1)S(1)}, u32[]{:S(2)}, u32[]{:S(2)}) collective-permute-start(s16[1040,256]{1,0:T(8,128)(2,1)S(1)} %get-tuple-element.94), channel_id=1, source_target_pairs={{0,4},{1,5},{2,6},{3,7},{4,0},{5,1},{6,2},{7,3},{8,12},{9,13},{10,... | collective-permute-start | bytes 1597448 | tf_op jit(solution)/shard_map/ppermute | solution.py:378
  61.0 16.4 %collective-permute-start.20 = (s16[528,256]{1,0:T(8,128)(2,1)S(1)}, s16[528,256]{1,0:T(8,128)(2,1)S(1)}, u32[]{:S(2)}, u32[]{:S(2)}) collective-permute-start(s16[528,256]{1,0:T(8,128)(2,1)S(1)} %get-tuple-element.102), channel_id=1, source_target_pairs={{0,8},{8,0},{16,24},{24,16},{1,9},{9,1},{17,25},{25,17},{2,10},{10... | collective-permute-start | bytes 811016 | tf_op jit(solution)/shard_map/ppermute | solution.py:375
  62.8 14.7 %collective-permute-start.19 = (s16[528,256]{1,0:T(8,128)(2,1)S(1)}, s16[528,256]{1,0:T(8,128)(2,1)S(1)}, u32[]{:S(2)}, u32[]{:S(2)}) collective-permute-start(s16[528,256]{1,0:T(8,128)(2,1)S(1)} %get-tuple-element.97), channel_id=1, source_target_pairs={{0,16},{8,24},{16,0},{24,8},{1,17},{9,25},{17,1},{25,9},{2,18},{10... | collective-permute-start | bytes 811016 | tf_op jit(solution)/shard_map/ppermute | solution.py:375
  72.2 12.6 %collective-permute-start.23 = (s16[528,256]{1,0:T(8,128)(2,1)S(1)}, s16[528,256]{1,0:T(8,128)(2,1)S(1)}, u32[]{:S(2)}, u32[]{:S(2)}) collective-permute-start(s16[528,256]{1,0:T(8,128)(2,1)S(1)} %get-tuple-element.109), channel_id=1, source_target_pairs={{0,8},{8,0},{16,24},{24,16},{1,9},{9,1},{17,25},{25,17},{2,10},{10... | collective-permute-start | bytes 811016 | tf_op jit(solution)/shard_map/ppermute | solution.py:375
  72.8 12.0 %collective-permute-start.22 = (s16[528,256]{1,0:T(8,128)(2,1)S(1)}, s16[528,256]{1,0:T(8,128)(2,1)S(1)}, u32[]{:S(2)}, u32[]{:S(2)}) collective-permute-start(s16[528,256]{1,0:T(8,128)(2,1)S(1)} %get-tuple-element.100), channel_id=1, source_target_pairs={{0,16},{8,24},{16,0},{24,8},{1,17},{9,25},{17,1},{25,9},{2,18},{10... | collective-permute-start | bytes 811016 | tf_op jit(solution)/shard_map/ppermute | solution.py:375
  77.7 10.3 %collective-permute-start.24 = (s16[528,256]{1,0:T(8,128)(2,1)S(1)}, s16[528,256]{1,0:T(8,128)(2,1)S(1)}, u32[]{:S(2)}, u32[]{:S(2)}) collective-permute-start(s16[528,256]{1,0:T(8,128)(2,1)S(1)} %get-tuple-element.104), channel_id=1, source_target_pairs={{0,2},{1,3},{2,0},{3,1},{4,6},{5,7},{6,4},{7,5},{8,10},{9,11},{10,... | collective-permute-start | bytes 811016 | tf_op jit(solution)/shard_map/ppermute | solution.py:378
  85.1 12.7 %collective-permute-start.28 = (s16[528,256]{1,0:T(8,128)(2,1)S(1)}, s16[528,256]{1,0:T(8,128)(2,1)S(1)}, u32[]{:S(2)}, u32[]{:S(2)}) collective-permute-start(s16[528,256]{1,0:T(8,128)(2,1)S(1)} %get-tuple-element.111), channel_id=1, source_target_pairs={{0,2},{1,3},{2,0},{3,1},{4,6},{5,7},{6,4},{7,5},{8,10},{9,11},{10,... | collective-permute-start | bytes 811016 | tf_op jit(solution)/shard_map/ppermute | solution.py:378
  88.2 9.5 %collective-permute-start.27 = (s16[272,256]{1,0:T(8,128)(2,1)S(1)}, s16[272,256]{1,0:T(8,128)(2,1)S(1)}, u32[]{:S(2)}, u32[]{:S(2)}) collective-permute-start(s16[272,256]{1,0:T(8,128)(2,1)S(1)} %get-tuple-element.114), channel_id=1, source_target_pairs={{0,4},{1,5},{2,6},{3,7},{4,0},{5,1},{6,2},{7,3},{8,12},{9,13},{10,... | collective-permute-start | bytes 417800 | tf_op jit(solution)/shard_map/ppermute | solution.py:378
  98.1 10.8 %collective-permute-start.34 = (s16[272,256]{1,0:T(8,128)(2,1)S(1)}, s16[272,256]{1,0:T(8,128)(2,1)S(1)}, u32[]{:S(2)}, u32[]{:S(2)}) collective-permute-start(s16[272,256]{1,0:T(8,128)(2,1)S(1)} %finish.2.refs_0_), channel_id=1, source_target_pairs={{0,24},{8,16},{16,8},{24,0},{1,25},{9,17},{17,9},{25,1},{2,26},{10... | collective-permute-start | bytes 417800 | tf_op jit(solution)/shard_map/ppermute | solution.py:375
  99.8 10.5 %collective-permute-start.33 = (s16[272,256]{1,0:T(8,128)(2,1)S(1)}, s16[272,256]{1,0:T(8,128)(2,1)S(1)}, u32[]{:S(2)}, u32[]{:S(2)}) collective-permute-start(s16[272,256]{1,0:T(8,128)(2,1)S(1)} %finish.2.refs_0_), channel_id=1, source_target_pairs={{0,16},{8,24},{16,0},{24,8},{1,17},{9,25},{17,1},{25,9},{2,18},{10... | collective-permute-start | bytes 417800 | tf_op jit(solution)/shard_map/ppermute | solution.py:375
  101.0 9.3 %collective-permute-start.32 = (s16[272,256]{1,0:T(8,128)(2,1)S(1)}, s16[272,256]{1,0:T(8,128)(2,1)S(1)}, u32[]{:S(2)}, u32[]{:S(2)}) collective-permute-start(s16[272,256]{1,0:T(8,128)(2,1)S(1)} %finish.2.refs_0_), channel_id=1, source_target_pairs={{0,8},{8,0},{16,24},{24,16},{1,9},{9,1},{17,25},{25,17},{2,10},{10... | collective-permute-start | bytes 417800 | tf_op jit(solution)/shard_map/ppermute | solution.py:375
  (15 other events, 106.6 us)

commit v4 on v3

--- a/solution.py
+++ b/solution.py
@@ -203,11 +203,13 @@
         copy(own_tiles, 0, i).wait()
 
 
-def join_kernel(order, *refs):
+def join_kernel(first, order, *refs):
     *parts, out = refs
-    rows = parts[0].shape[0]
-    for i, part in enumerate(parts):
-        out[pl.ds(i * rows, rows), :] = part[...]
+    at, width = 0, out.shape[1]
+    for part in parts:
+        column = first if part.shape[1] > width else 0
+        out[pl.ds(at, part.shape[0]), :] = part[:, pl.ds(column, width)]
+        at += part.shape[0]
 
 
 def add_products(count, first, order_ref, slot_ref, label_ref, tiles, stack, sums):
@@ -387,9 +389,9 @@
 
     mines = [own_half(panel, j) for j in range(chunks)]
     ways = [None, (1, 2), (2, 1)]
-    firsts = [None] + [to_grp(mines[j], ways[j][0]) for j in range(1, chunks)]
-    mine, sib_index = lax.optimization_barrier((mines[0], sib_index))
-    near = [to_grp(mine, 1), to_grp(mine, 2), to_grp(mines[0], 3)]
+    from_x, from_y = [to_grp(jnp.concatenate([mines[0], mines[d]], axis=1), d) for d in (1, 2)]
+    firsts = [None, from_x, from_y]
+    near = [from_x, from_y, to_grp(mines[0], 3)]
 
     half, quarter = sums // 2, sums // 4
     plain = shape((side, CHUNK), jnp.float32)
@@ -431,7 +433,12 @@
     part = shard // 2
 
     def join(j):
-        (joined,) = call(join_kernel, "join", [shape((3 * rows // 2, CHUNK), panel.dtype)], *near)
+        (joined,) = call(
+            functools.partial(join_kernel, 0),
+            "join",
+            [shape((3 * rows // 2, CHUNK), panel.dtype)],
+            *near,
+        )
         tiles_of = [(d, range((d - 1) * part, d * part)) for d in (1, 2, 3)]
         fill = places(0, tiles_of, 0) + places(1, tiles_of, part)
         return fill, [joined, to_core(joined)]
@@ -439,7 +446,11 @@
     def pair(j):
         way, other = ways[j]
         (joined,) = call(
-            join_kernel, "join", [shape((rows, CHUNK), panel.dtype)], mines[j], firsts[j]
+            functools.partial(join_kernel, CHUNK),
+            "join",
+            [shape((rows, CHUNK), panel.dtype)],
+            mines[j],
+            firsts[j],
         )
         second = to_grp(joined, other)
         in_first = [(way, range(part, 2 * part))]

time: 119 us -> 117 us (0.983)
  starting transfers between devices: 39.7 us -> 35.8 us
  waiting for transfers between devices: 46.2 us -> 50 us
  Pallas kernels: 29.8 us -> 28.3 us
    ppermute x25 -> x23, starting transfers between devices: 31.5 us -> 26.5 us  [to_grp(): return lax.ppermute(v, 'grp', [(i, i ^ d) for i in range(4)])]
    ppermute x25 -> x23, waiting for transfers between devices: 30.7 us -> 33.1 us  [to_grp(): return lax.ppermute(v, 'grp', [(i, i ^ d) for i in range(4)])]
    ppermute x7, waiting for transfers between devices: 3.95 us -> 5.47 us  [to_core(): return lax.ppermute(v, 'wide', [(i, i ^ 1) for i in range(wide_count)])]
    pallas_call x24, Pallas kernels: 29.8 us -> 28.3 us  [call(): pl.pallas_call(body, in_specs=more.pop('in_specs', in_any(1) + in_smem(sm...]
  transfers between devices with their start and end apart: 38 -> 36, of which waited for: 17 -> 21; matrix products, arithmetic and copies ran while one was open for 2% -> 1% of each run, Pallas kernels for 24% -> 23%
where the time goes in v4:
time: 117 us; the launch traced here: 116 us
  waiting for transfers between devices  50 us (43%)
  starting transfers between devices  35.8 us (31%)
  Pallas kernels  28.3 us (24%)
  local copies, waits for them, and re-layouts  1.18 us (1%)
    ppermute x23, waiting for transfers between devices, to_grp(): return lax.ppermute(v, 'grp', [(i, i ^ d) for i in range(4)])  33.1 us
    pallas_call x24, Pallas kernels, call(): pl.pallas_call(body, in_specs=more.pop('in_specs', in_any(1) + in_smem(sm...  28.3 us
    ppermute x23, starting transfers between devices, to_grp(): return lax.ppermute(v, 'grp', [(i, i ^ d) for i in range(4)])  26.5 us
    ppermute x6, waiting for transfers between devices, to_line(): return lax.ppermute(v, 'wide', [(i, i ^ 2 << b) for i in range(wide_count)])  11.5 us
    ppermute x6, starting transfers between devices, to_line(): return lax.ppermute(v, 'wide', [(i, i ^ 2 << b) for i in range(wide_count)])  8.14 us
    ppermute x7, waiting for transfers between devices, to_core(): return lax.ppermute(v, 'wide', [(i, i ^ 1) for i in range(wide_count)])  5.47 us
  transfers between devices with their start and end apart: 36, of which 21 were waited for; matrix products, arithmetic and copies ran while one was open for 1% of the time, Pallas kernels for 23%

profile of v4, /device:TPU:0, one launch (start us, length us, event | category | flops | bytes accessed | tf_op | source)
XLA Modules:
  0.0 115.9 jit_solution(5885745699757499025)
XLA Ops:
  1.8 2.6 %collective-permute-start.2 = (bf16[512,512]{1,0:T(8,128)(2,1)S(1)}, bf16[512,512]{1,0:T(8,128)(2,1)S(1)}, u32[]{:S(2)}, u32[]{:S(2)}) collective-permute-start(bf16[512,512]{1,0:T(8,128)(2,1)S(1)} %get-tuple-element.129), channel_id=1, source_target_pairs={{0,8},{8,0},{16,24},{24,16},{1,9},{9,1},{17,25},{25,17},{2,10},{10... | collective-permute-start | bytes 1572872 | tf_op jit(solution)/shard_map/ppermute | solution.py:377
  6.0 4.3 %collective-permute-done.sib_ref = s32[128]{0:T(128)S(1)} collective-permute-done((s32[128]{0:T(128)S(1)}, s32[128]{0:T(128)S(1)}, u32[]{:S(2)}, u32[]{:S(2)}) %collective-permute-start) | collective-permute-done | bytes 544 | tf_op jit(solution)/shard_map/ppermute | solution.py:374
  10.7 6.7 %hold.1 = (s32[3]{0:T(128)S(1)}, s32[104]{0:T(128)S(1)}, s32[104]{0:T(128)S(1)}, s32[104]{0:T(128)S(1)}, s32[208]{0:T(256)S(1)}, /*index=5*/s32[208]{0:T(256)S(1)}, bf16[104,256,256]{2,1,0:T(8,128)(2,1)S(1)}) custom-call(s32[1]{0:T(128)} %constant.8.clone.1.order, s32[128]{0:T(128)S(1)} %pad_add_fusion.own_ref, s32[128]{0:T(128)S(1)} %collective-permute-done.sib_ref, ...), custom_call_target="tpu_custom_call" | custom-call | bytes 12583936 | tf_op jit(solution)/shard_map/hold/pallas_call | solution.py:413
  17.5 6.5 %collective-permute-done.3.refs_1_ = bf16[512,512]{1,0:T(8,128)(2,1)S(1)} collective-permute-done((bf16[512,512]{1,0:T(8,128)(2,1)S(1)}, bf16[512,512]{1,0:T(8,128)(2,1)S(1)}, u32[]{:S(2)}, u32[]{:S(2)}) %collective-permute-start.3) | collective-permute-done | bytes 524320 | tf_op jit(solution)/shard_map/ppermute | solution.py:377
  26.5 2.7 %products_sent.3 = (s16[2064,256]{1,0:T(8,128)(2,1)S(1)}, bf16[16,256,256]{2,1,0:T(8,128)(2,1)S(1)}) custom-call(s32[1]{0:T(128)} %constant.8.clone.1.order, s32[3]{0:T(128)S(1)} %get-tuple-element.70.count_ref, s32[208]{0:T(256)S(1)} %get-tuple-element.71.order_ref, s32[104]{0:T(128)S(1)} %get-tuple-element.72.slot_ref, ...), custom_call_target="tpu_custom_call" | custom-call | bytes 16778892 | tf_op jit(solution)/shard_map/products_sent/pallas_call | solution.py:413
  29.2 2.6 %collective-permute-start.12 = (s16[2064,256]{1,0:T(8,128)(2,1)S(1)}, s16[2064,256]{1,0:T(8,128)(2,1)S(1)}, u32[]{:S(2)}, u32[]{:S(2)}) collective-permute-start(s16[2064,256]{1,0:T(8,128)(2,1)S(1)} %get-tuple-element.74), channel_id=1, source_target_pairs={{0,2},{1,3},{2,0},{3,1},{4,6},{5,7},{6,4},{7,5},{8,10},{9,11},{10,... | collective-permute-start | bytes 3170312 | tf_op jit(solution)/shard_map/ppermute | solution.py:380
  31.8 2.3 %products_kept.3.kept = f32[9,256,256]{2,1,0:T(8,128)S(1)} custom-call(s32[1]{0:T(128)} %constant.8.clone.1.order, s32[3]{0:T(128)S(1)} %get-tuple-element.70.count_ref, s32[208]{0:T(256)S(1)} %get-tuple-element.71.order_ref, s32[104]{0:T(128)S(1)} %get-tuple-element.72.slot_ref, s32[104]{0:T(128)S(1)} %get-tuple-element.73.label_ref, ...), custom_call_target="tpu_custom_call" | custom-call | bytes 15730316 | tf_op jit(solution)/shard_map/products_kept/pallas_call | solution.py:413
  34.1 4.5 %collective-permute-done.7.refs_2_ = bf16[1024,256]{1,0:T(8,128)(2,1)S(1)} collective-permute-done((bf16[1024,256]{1,0:T(8,128)(2,1)S(1)}, bf16[1024,256]{1,0:T(8,128)(2,1)S(1)}, u32[]{:S(2)}, u32[]{:S(2)}) %collective-permute-start.7) | collective-permute-done | bytes 524320 | tf_op jit(solution)/shard_map/ppermute | solution.py:377
  40.4 2.2 %products_sent.4 = (s16[1040,256]{1,0:T(8,128)(2,1)S(1)}, s16[1040,256]{1,0:T(8,128)(2,1)S(1)}, bf16[16,256,256]{2,1,0:T(8,128)(2,1)S(1)}) custom-call(s32[1]{0:T(128)} %constant.8.clone.1.order, s32[3]{0:T(128)S(1)} %get-tuple-element.70.count_ref, s32[208]{0:T(256)S(1)} %get-tuple-element.78.order_ref, s32[104]{0:T(128)S(1)} %get-tuple-element.79.slot_ref, ...), custom_call_target="tpu_custom_call" | custom-call | bytes 17303180 | tf_op jit(solution)/shard_map/products_sent/pallas_call | solution.py:413
  42.6 3.5 %collective-permute-start.14 = (s16[1040,256]{1,0:T(8,128)(2,1)S(1)}, s16[1040,256]{1,0:T(8,128)(2,1)S(1)}, u32[]{:S(2)}, u32[]{:S(2)}) collective-permute-start(s16[1040,256]{1,0:T(8,128)(2,1)S(1)} %get-tuple-element.92), channel_id=1, source_target_pairs={{0,16},{8,24},{16,0},{24,8},{1,17},{9,25},{17,1},{25,9},{2,18},{10... | collective-permute-start | bytes 1597448 | tf_op jit(solution)/shard_map/ppermute | solution.py:377
  46.2 2.7 %products_kept.4.kept = f32[9,256,256]{2,1,0:T(8,128)S(1)} custom-call(s32[1]{0:T(128)} %constant.8.clone.1.order, s32[3]{0:T(128)S(1)} %get-tuple-element.70.count_ref, s32[208]{0:T(256)S(1)} %get-tuple-element.78.order_ref, s32[104]{0:T(128)S(1)} %get-tuple-element.79.slot_ref, s32[104]{0:T(128)S(1)} %get-tuple-element.73.label_ref, ...), custom_call_target="tpu_custom_call" | custom-call | bytes 15730316 | tf_op jit(solution)/shard_map/products_kept/pallas_call | solution.py:413
  48.9 2.2 %products_sent.5 = (s16[1040,256]{1,0:T(8,128)(2,1)S(1)}, s16[1040,256]{1,0:T(8,128)(2,1)S(1)}, bf16[16,256,256]{2,1,0:T(8,128)(2,1)S(1)}) custom-call(s32[1]{0:T(128)} %constant.8.clone.1.order, s32[3]{0:T(128)S(1)} %get-tuple-element.70.count_ref, s32[208]{0:T(256)S(1)} %get-tuple-element.78.order_ref, s32[104]{0:T(128)S(1)} %get-tuple-element.79.slot_ref, ...), custom_call_target="tpu_custom_call" | custom-call | bytes 17303180 | tf_op jit(solution)/shard_map/products_sent/pallas_call | solution.py:413
  51.1 2.3 %collective-permute-start.16 = (s16[1040,256]{1,0:T(8,128)(2,1)S(1)}, s16[1040,256]{1,0:T(8,128)(2,1)S(1)}, u32[]{:S(2)}, u32[]{:S(2)}) collective-permute-start(s16[1040,256]{1,0:T(8,128)(2,1)S(1)} %get-tuple-element.95), channel_id=1, source_target_pairs={{0,16},{8,24},{16,0},{24,8},{1,17},{9,25},{17,1},{25,9},{2,18},{10... | collective-permute-start | bytes 1597448 | tf_op jit(solution)/shard_map/ppermute | solution.py:377
  54.3 2.9 %products_kept.5.kept = f32[9,256,256]{2,1,0:T(8,128)S(1)} custom-call(s32[1]{0:T(128)} %constant.8.clone.1.order, s32[3]{0:T(128)S(1)} %get-tuple-element.70.count_ref, s32[208]{0:T(256)S(1)} %get-tuple-element.78.order_ref, s32[104]{0:T(128)S(1)} %get-tuple-element.79.slot_ref, s32[104]{0:T(128)S(1)} %get-tuple-element.73.label_ref, ...), custom_call_target="tpu_custom_call" | custom-call | bytes 15730316 | tf_op jit(solution)/shard_map/products_kept/pallas_call | solution.py:413
  57.7 3.2 %collective-permute-start.19 = (s16[1040,256]{1,0:T(8,128)(2,1)S(1)}, s16[1040,256]{1,0:T(8,128)(2,1)S(1)}, u32[]{:S(2)}, u32[]{:S(2)}) collective-permute-start(s16[1040,256]{1,0:T(8,128)(2,1)S(1)} %get-tuple-element.90), channel_id=1, source_target_pairs={{0,4},{1,5},{2,6},{3,7},{4,0},{5,1},{6,2},{7,3},{8,12},{9,13},{10,... | collective-permute-start | bytes 1597448 | tf_op jit(solution)/shard_map/ppermute | solution.py:380
  63.0 7.6 %collective-permute-done.16.recv_b = s16[1040,256]{1,0:T(8,128)(2,1)S(1)} collective-permute-done((s16[1040,256]{1,0:T(8,128)(2,1)S(1)}, s16[1040,256]{1,0:T(8,128)(2,1)S(1)}, u32[]{:S(2)}, u32[]{:S(2)}) %collective-permute-start.16) | collective-permute-done | bytes 532512 | tf_op jit(solution)/shard_map/ppermute | solution.py:377
  70.6 2.0 %collective-permute-done.15.recv_a = s16[1040,256]{1,0:T(8,128)(2,1)S(1)} collective-permute-done((s16[1040,256]{1,0:T(8,128)(2,1)S(1)}, s16[1040,256]{1,0:T(8,128)(2,1)S(1)}, u32[]{:S(2)}, u32[]{:S(2)}) %collective-permute-start.15) | collective-permute-done | bytes 532512 | tf_op jit(solution)/shard_map/ppermute | solution.py:377
  74.0 4.4 %collective-permute-done.18.recv_b = s16[528,256]{1,0:T(8,128)(2,1)S(1)} collective-permute-done((s16[528,256]{1,0:T(8,128)(2,1)S(1)}, s16[528,256]{1,0:T(8,128)(2,1)S(1)}, u32[]{:S(2)}, u32[]{:S(2)}) %collective-permute-start.18) | collective-permute-done | bytes 270368 | tf_op jit(solution)/shard_map/ppermute | solution.py:377
  84.8 3.3 %collective-permute-done.22.recv = s16[528,256]{1,0:T(8,128)(2,1)S(1)} collective-permute-done((s16[528,256]{1,0:T(8,128)(2,1)S(1)}, s16[528,256]{1,0:T(8,128)(2,1)S(1)}, u32[]{:S(2)}, u32[]{:S(2)}) %collective-permute-start.22) | collective-permute-done | bytes 270368 | tf_op jit(solution)/shard_map/ppermute | solution.py:380
  88.4 2.4 %collective-permute-done.24.recv_b = s16[528,256]{1,0:T(8,128)(2,1)S(1)} collective-permute-done((s16[528,256]{1,0:T(8,128)(2,1)S(1)}, s16[528,256]{1,0:T(8,128)(2,1)S(1)}, u32[]{:S(2)}, u32[]{:S(2)}) %collective-permute-start.24) | collective-permute-done | bytes 270368 | tf_op jit(solution)/shard_map/ppermute | solution.py:377
  94.3 3.0 %collective-permute-done.25.recv = s16[272,256]{1,0:T(8,128)(2,1)S(1)} collective-permute-done((s16[272,256]{1,0:T(8,128)(2,1)S(1)}, s16[272,256]{1,0:T(8,128)(2,1)S(1)}, u32[]{:S(2)}, u32[]{:S(2)}) %collective-permute-start.25) | collective-permute-done | bytes 139296 | tf_op jit(solution)/shard_map/ppermute | solution.py:380
  102.7 3.1 %collective-permute-done.29.recv = s16[272,256]{1,0:T(8,128)(2,1)S(1)} collective-permute-done((s16[272,256]{1,0:T(8,128)(2,1)S(1)}, s16[272,256]{1,0:T(8,128)(2,1)S(1)}, u32[]{:S(2)}, u32[]{:S(2)}) %collective-permute-start.29) | collective-permute-done | bytes 139296 | tf_op jit(solution)/shard_map/ppermute | solution.py:380
  106.1 2.3 %collective-permute-start.34 = (s16[272,256]{1,0:T(8,128)(2,1)S(1)}, s16[272,256]{1,0:T(8,128)(2,1)S(1)}, u32[]{:S(2)}, u32[]{:S(2)}) collective-permute-start(s16[272,256]{1,0:T(8,128)(2,1)S(1)} %finish.3.refs_0_), channel_id=1, source_target_pairs={{0,16},{8,24},{16,0},{24,8},{1,17},{9,25},{17,1},{25,9},{2,18},{10... | collective-permute-start | bytes 417800 | tf_op jit(solution)/shard_map/ppermute | solution.py:377
  110.5 3.0 %collective-permute-done.35.refs_3_ = s16[272,256]{1,0:T(8,128)(2,1)S(1)} collective-permute-done((s16[272,256]{1,0:T(8,128)(2,1)S(1)}, s16[272,256]{1,0:T(8,128)(2,1)S(1)}, u32[]{:S(2)}, u32[]{:S(2)}) %collective-permute-start.35) | collective-permute-done | bytes 139296 | tf_op jit(solution)/shard_map/ppermute | solution.py:377
  (83 shorter events, 33.1 us)
Async XLA Ops:
  0.0 10.6 %collective-permute-start.1 = (bf16[48,256,256]{2,1,0:T(8,128)(2,1)}, bf16[48,256,256]{2,1,0:T(8,128)(2,1)}, u32[]{:S(2)}, u32[]{:S(2)}) collective-permute-start(bf16[48,256,256]{2,1,0:T(8,128)(2,1)} %own_tiles.1), channel_id=1, source_target_pairs={{0,1},{1,0},{2,3},{3,2},{4,5},{5,4},{6,7},{7,6},{8,9},{9,8},{10,11... | collective-permute-start | bytes 18874376 | tf_op jit(solution)/shard_map/ppermute | solution.py:374
  1.8 15.6 %collective-permute-start.2 = (bf16[512,512]{1,0:T(8,128)(2,1)S(1)}, bf16[512,512]{1,0:T(8,128)(2,1)S(1)}, u32[]{:S(2)}, u32[]{:S(2)}) collective-permute-start(bf16[512,512]{1,0:T(8,128)(2,1)S(1)} %get-tuple-element.129), channel_id=1, source_target_pairs={{0,8},{8,0},{16,24},{24,16},{1,9},{9,1},{17,25},{25,17},{2,10},{10... | collective-permute-start | bytes 1572872 | tf_op jit(solution)/shard_map/ppermute | solution.py:377
  4.4 19.6 %collective-permute-start.3 = (bf16[512,512]{1,0:T(8,128)(2,1)S(1)}, bf16[512,512]{1,0:T(8,128)(2,1)S(1)}, u32[]{:S(2)}, u32[]{:S(2)}) collective-permute-start(bf16[512,512]{1,0:T(8,128)(2,1)S(1)} %get-tuple-element.128), channel_id=1, source_target_pairs={{0,16},{8,24},{16,0},{24,8},{1,17},{9,25},{17,1},{25,9},{2,18},{10... | collective-permute-start | bytes 1572872 | tf_op jit(solution)/shard_map/ppermute | solution.py:377
  5.9 18.2 %collective-permute-start.4 = (bf16[512,256]{1,0:T(8,128)(2,1)S(1)}, bf16[512,256]{1,0:T(8,128)(2,1)S(1)}, u32[]{:S(2)}, u32[]{:S(2)}) collective-permute-start(bf16[512,256]{1,0:T(8,128)(2,1)S(1)} %get-tuple-element.126), channel_id=1, source_target_pairs={{0,24},{8,16},{16,8},{24,0},{1,25},{9,17},{17,9},{25,1},{2,26},{10... | collective-permute-start | bytes 786440 | tf_op jit(solution)/shard_map/ppermute | solution.py:377
  24.2 14.3 %collective-permute-start.7 = (bf16[1024,256]{1,0:T(8,128)(2,1)S(1)}, bf16[1024,256]{1,0:T(8,128)(2,1)S(1)}, u32[]{:S(2)}, u32[]{:S(2)}) collective-permute-start(bf16[1024,256]{1,0:T(8,128)(2,1)S(1)} %join.3.refs_0_), channel_id=1, source_target_pairs={{0,16},{8,24},{16,0},{24,8},{1,17},{9,25},{17,1},{25,9},{2,18},{10... | collective-permute-start | bytes 1572872 | tf_op jit(solution)/shard_map/ppermute | solution.py:377
  25.8 14.0 %collective-permute-start.10 = (bf16[1024,256]{1,0:T(8,128)(2,1)S(1)}, bf16[1024,256]{1,0:T(8,128)(2,1)S(1)}, u32[]{:S(2)}, u32[]{:S(2)}) collective-permute-start(bf16[1024,256]{1,0:T(8,128)(2,1)S(1)} %join.4.refs_0_), channel_id=1, source_target_pairs={{0,8},{8,0},{16,24},{24,16},{1,9},{9,1},{17,25},{25,17},{2,10},{10... | collective-permute-start | bytes 1572872 | tf_op jit(solution)/shard_map/ppermute | solution.py:377
  29.2 28.0 %collective-permute-start.12 = (s16[2064,256]{1,0:T(8,128)(2,1)S(1)}, s16[2064,256]{1,0:T(8,128)(2,1)S(1)}, u32[]{:S(2)}, u32[]{:S(2)}) collective-permute-start(s16[2064,256]{1,0:T(8,128)(2,1)S(1)} %get-tuple-element.74), channel_id=1, source_target_pairs={{0,2},{1,3},{2,0},{3,1},{4,6},{5,7},{6,4},{7,5},{8,10},{9,11},{10,... | collective-permute-start | bytes 3170312 | tf_op jit(solution)/shard_map/ppermute | solution.py:380
  38.5 10.3 %collective-permute-start.9 = (bf16[1024,256]{1,0:T(8,128)(2,1)S(1)}, bf16[1024,256]{1,0:T(8,128)(2,1)S(1)}, u32[]{:S(2)}, u32[]{:S(2)}) collective-permute-start(bf16[1024,256]{1,0:T(8,128)(2,1)S(1)} %join.4.refs_0_), channel_id=1, source_target_pairs={{0,1},{1,0},{2,3},{3,2},{4,5},{5,4},{6,7},{7,6},{8,9},{9,8},{10,11... | collective-permute-start | bytes 1572872 | tf_op jit(solution)/shard_map/ppermute | solution.py:374
  39.8 9.1 %collective-permute-start.11 = (bf16[1024,256]{1,0:T(8,128)(2,1)S(1)}, bf16[1024,256]{1,0:T(8,128)(2,1)S(1)}, u32[]{:S(2)}, u32[]{:S(2)}) collective-permute-start(bf16[1024,256]{1,0:T(8,128)(2,1)S(1)} %collective-permute-done.10.refs_2_), channel_id=1, source_target_pairs={{0,1},{1,0},{2,3},{3,2},{4,5},{5,4},{6,7},{7,6},{8,9},{9,8},{10,11... | collective-permute-start | bytes 1572872 | tf_op jit(solution)/shard_map/ppermute | solution.py:374
  42.6 18.3 %collective-permute-start.14 = (s16[1040,256]{1,0:T(8,128)(2,1)S(1)}, s16[1040,256]{1,0:T(8,128)(2,1)S(1)}, u32[]{:S(2)}, u32[]{:S(2)}) collective-permute-start(s16[1040,256]{1,0:T(8,128)(2,1)S(1)} %get-tuple-element.92), channel_id=1, source_target_pairs={{0,16},{8,24},{16,0},{24,8},{1,17},{9,25},{17,1},{25,9},{2,18},{10... | collective-permute-start | bytes 1597448 | tf_op jit(solution)/shard_map/ppermute | solution.py:377
  46.2 15.0 %collective-permute-start.13 = (s16[1040,256]{1,0:T(8,128)(2,1)S(1)}, s16[1040,256]{1,0:T(8,128)(2,1)S(1)}, u32[]{:S(2)}, u32[]{:S(2)}) collective-permute-start(s16[1040,256]{1,0:T(8,128)(2,1)S(1)} %get-tuple-element.81), channel_id=1, source_target_pairs={{0,8},{8,0},{16,24},{24,16},{1,9},{9,1},{17,25},{25,17},{2,10},{10... | collective-permute-start | bytes 1597448 | tf_op jit(solution)/shard_map/ppermute | solution.py:377
  51.1 19.5 %collective-permute-start.16 = (s16[1040,256]{1,0:T(8,128)(2,1)S(1)}, s16[1040,256]{1,0:T(8,128)(2,1)S(1)}, u32[]{:S(2)}, u32[]{:S(2)}) collective-permute-start(s16[1040,256]{1,0:T(8,128)(2,1)S(1)} %get-tuple-element.95), channel_id=1, source_target_pairs={{0,16},{8,24},{16,0},{24,8},{1,17},{9,25},{17,1},{25,9},{2,18},{10... | collective-permute-start | bytes 1597448 | tf_op jit(solution)/shard_map/ppermute | solution.py:377
  53.3 19.3 %collective-permute-start.15 = (s16[1040,256]{1,0:T(8,128)(2,1)S(1)}, s16[1040,256]{1,0:T(8,128)(2,1)S(1)}, u32[]{:S(2)}, u32[]{:S(2)}) collective-permute-start(s16[1040,256]{1,0:T(8,128)(2,1)S(1)} %get-tuple-element.86), channel_id=1, source_target_pairs={{0,8},{8,0},{16,24},{24,16},{1,9},{9,1},{17,25},{25,17},{2,10},{10... | collective-permute-start | bytes 1597448 | tf_op jit(solution)/shard_map/ppermute | solution.py:377
  57.7 24.4 %collective-permute-start.19 = (s16[1040,256]{1,0:T(8,128)(2,1)S(1)}, s16[1040,256]{1,0:T(8,128)(2,1)S(1)}, u32[]{:S(2)}, u32[]{:S(2)}) collective-permute-start(s16[1040,256]{1,0:T(8,128)(2,1)S(1)} %get-tuple-element.90), channel_id=1, source_target_pairs={{0,4},{1,5},{2,6},{3,7},{4,0},{5,1},{6,2},{7,3},{8,12},{9,13},{10,... | collective-permute-start | bytes 1597448 | tf_op jit(solution)/shard_map/ppermute | solution.py:380
  61.8 16.6 %collective-permute-start.18 = (s16[528,256]{1,0:T(8,128)(2,1)S(1)}, s16[528,256]{1,0:T(8,128)(2,1)S(1)}, u32[]{:S(2)}, u32[]{:S(2)}) collective-permute-start(s16[528,256]{1,0:T(8,128)(2,1)S(1)} %get-tuple-element.98), channel_id=1, source_target_pairs={{0,8},{8,0},{16,24},{24,16},{1,9},{9,1},{17,25},{25,17},{2,10},{10... | collective-permute-start | bytes 811016 | tf_op jit(solution)/shard_map/ppermute | solution.py:377
  62.1 16.3 %collective-permute-start.17 = (s16[528,256]{1,0:T(8,128)(2,1)S(1)}, s16[528,256]{1,0:T(8,128)(2,1)S(1)}, u32[]{:S(2)}, u32[]{:S(2)}) collective-permute-start(s16[528,256]{1,0:T(8,128)(2,1)S(1)} %get-tuple-element.93), channel_id=1, source_target_pairs={{0,16},{8,24},{16,0},{24,8},{1,17},{9,25},{17,1},{25,9},{2,18},{10... | collective-permute-start | bytes 811016 | tf_op jit(solution)/shard_map/ppermute | solution.py:377
  73.2 10.6 %collective-permute-start.21 = (s16[528,256]{1,0:T(8,128)(2,1)S(1)}, s16[528,256]{1,0:T(8,128)(2,1)S(1)}, u32[]{:S(2)}, u32[]{:S(2)}) collective-permute-start(s16[528,256]{1,0:T(8,128)(2,1)S(1)} %get-tuple-element.105), channel_id=1, source_target_pairs={{0,8},{8,0},{16,24},{24,16},{1,9},{9,1},{17,25},{25,17},{2,10},{10... | collective-permute-start | bytes 811016 | tf_op jit(solution)/shard_map/ppermute | solution.py:377
  73.2 10.6 %collective-permute-start.20 = (s16[528,256]{1,0:T(8,128)(2,1)S(1)}, s16[528,256]{1,0:T(8,128)(2,1)S(1)}, u32[]{:S(2)}, u32[]{:S(2)}) collective-permute-start(s16[528,256]{1,0:T(8,128)(2,1)S(1)} %get-tuple-element.96), channel_id=1, source_target_pairs={{0,16},{8,24},{16,0},{24,8},{1,17},{9,25},{17,1},{25,9},{2,18},{10... | collective-permute-start | bytes 811016 | tf_op jit(solution)/shard_map/ppermute | solution.py:377
  78.7 9.4 %collective-permute-start.22 = (s16[528,256]{1,0:T(8,128)(2,1)S(1)}, s16[528,256]{1,0:T(8,128)(2,1)S(1)}, u32[]{:S(2)}, u32[]{:S(2)}) collective-permute-start(s16[528,256]{1,0:T(8,128)(2,1)S(1)} %get-tuple-element.100), channel_id=1, source_target_pairs={{0,2},{1,3},{2,0},{3,1},{4,6},{5,7},{6,4},{7,5},{8,10},{9,11},{10,... | collective-permute-start | bytes 811016 | tf_op jit(solution)/shard_map/ppermute | solution.py:380
  84.1 13.3 %collective-permute-start.26 = (s16[528,256]{1,0:T(8,128)(2,1)S(1)}, s16[528,256]{1,0:T(8,128)(2,1)S(1)}, u32[]{:S(2)}, u32[]{:S(2)}) collective-permute-start(s16[528,256]{1,0:T(8,128)(2,1)S(1)} %get-tuple-element.107), channel_id=1, source_target_pairs={{0,2},{1,3},{2,0},{3,1},{4,6},{5,7},{6,4},{7,5},{8,10},{9,11},{10,... | collective-permute-start | bytes 811016 | tf_op jit(solution)/shard_map/ppermute | solution.py:380
  88.3 9.0 %collective-permute-start.25 = (s16[272,256]{1,0:T(8,128)(2,1)S(1)}, s16[272,256]{1,0:T(8,128)(2,1)S(1)}, u32[]{:S(2)}, u32[]{:S(2)}) collective-permute-start(s16[272,256]{1,0:T(8,128)(2,1)S(1)} %get-tuple-element.110), channel_id=1, source_target_pairs={{0,4},{1,5},{2,6},{3,7},{4,0},{5,1},{6,2},{7,3},{8,12},{9,13},{10,... | collective-permute-start | bytes 417800 | tf_op jit(solution)/shard_map/ppermute | solution.py:380
  91.3 9.4 %collective-permute-start.28 = (s16[528,256]{1,0:T(8,128)(2,1)S(1)}, s16[528,256]{1,0:T(8,128)(2,1)S(1)}, u32[]{:S(2)}, u32[]{:S(2)}) collective-permute-start(s16[528,256]{1,0:T(8,128)(2,1)S(1)} %get-tuple-element.120.refs_1_), channel_id=1, source_target_pairs={{0,8},{8,0},{16,24},{24,16},{1,9},{9,1},{17,25},{25,17},{2,10},{10... | collective-permute-start | bytes 811016 | tf_op jit(solution)/shard_map/ppermute | solution.py:377
  97.7 10.7 %collective-permute-start.32 = (s16[272,256]{1,0:T(8,128)(2,1)S(1)}, s16[272,256]{1,0:T(8,128)(2,1)S(1)}, u32[]{:S(2)}, u32[]{:S(2)}) collective-permute-start(s16[272,256]{1,0:T(8,128)(2,1)S(1)} %finish.2.refs_0_), channel_id=1, source_target_pairs={{0,24},{8,16},{16,8},{24,0},{1,25},{9,17},{17,9},{25,1},{2,26},{10... | collective-permute-start | bytes 417800 | tf_op jit(solution)/shard_map/ppermute | solution.py:377
  98.7 10.7 %collective-permute-start.31 = (s16[272,256]{1,0:T(8,128)(2,1)S(1)}, s16[272,256]{1,0:T(8,128)(2,1)S(1)}, u32[]{:S(2)}, u32[]{:S(2)}) collective-permute-start(s16[272,256]{1,0:T(8,128)(2,1)S(1)} %finish.2.refs_0_), channel_id=1, source_target_pairs={{0,16},{8,24},{16,0},{24,8},{1,17},{9,25},{17,1},{25,9},{2,18},{10... | collective-permute-start | bytes 417800 | tf_op jit(solution)/shard_map/ppermute | solution.py:377
  (16 other events, 106.6 us)

commit v5 on v4

--- a/solution.py
+++ b/solution.py
@@ -589,8 +589,8 @@
     own_a, own_b = call(
         swap_kernel, "swap", pair_of, own_a, own_b, to_grp(own_a, 1), to_grp(own_b, 2)
     )
+    sent[2], keep[2] = line(2)
     done_1 = finish(1)
-    sent[2], keep[2] = line(2)
     result = spread(0, [own_a, own_b, to_grp(own_a, 2), to_grp(own_b, 1)], None)
     done_2 = finish(2)
     result = spread(1, gathered(done_1), result)

time: 117 us -> 116 us (level)
  starting transfers between devices: 35.8 us -> 29.6 us
  waiting for transfers between devices: 50 us -> 53 us
  Pallas kernels: 28.3 us -> 31.2 us
    ppermute x6, starting transfers between devices: 8.14 us -> 2.18 us  [to_line(): return lax.ppermute(v, 'wide', [(i, i ^ 2 << b) for i in range(wide_count)])]
    ppermute x23, starting transfers between devices: 26.5 us -> 23.4 us  [to_grp(): return lax.ppermute(v, 'grp', [(i, i ^ d) for i in range(4)])]
    pallas_call x24, Pallas kernels: 28.3 us -> 31.2 us  [call(): pl.pallas_call(body, in_specs=more.pop('in_specs', in_any(1) + in_smem(sm...]
    ppermute x7, starting transfers between devices: 1.12 us -> 4.02 us  [to_core(): return lax.ppermute(v, 'wide', [(i, i ^ 1) for i in range(wide_count)])]
    ppermute x6, waiting for transfers between devices: 11.5 us -> 14 us  [to_line(): return lax.ppermute(v, 'wide', [(i, i ^ 2 << b) for i in range(wide_count)])]
  transfers between devices with their start and end apart: 36 -> 36, of which waited for: 21 -> 22; matrix products, arithmetic and copies ran while one was open for 1% -> 1% of each run, Pallas kernels for 23% -> 26%
where the time goes in v5:
time: 116 us
  waiting for transfers between devices  53 us (46%)
  Pallas kernels  31.2 us (27%)
  starting transfers between devices  29.6 us (26%)
  local copies, waits for them, and re-layouts  1.18 us (1%)
    ppermute x23, waiting for transfers between devices, to_grp(): return lax.ppermute(v, 'grp', [(i, i ^ d) for i in range(4)])  33.5 us
    pallas_call x24, Pallas kernels, call(): pl.pallas_call(body, in_specs=more.pop('in_specs', in_any(1) + in_smem(sm...  31.2 us
    ppermute x23, starting transfers between devices, to_grp(): return lax.ppermute(v, 'grp', [(i, i ^ d) for i in range(4)])  23.4 us
    ppermute x6, waiting for transfers between devices, to_line(): return lax.ppermute(v, 'wide', [(i, i ^ 2 << b) for i in range(wide_count)])  14 us
    ppermute x7, waiting for transfers between devices, to_core(): return lax.ppermute(v, 'wide', [(i, i ^ 1) for i in range(wide_count)])  5.47 us
    ppermute x7, starting transfers between devices, to_core(): return lax.ppermute(v, 'wide', [(i, i ^ 1) for i in range(wide_count)])  4.02 us
  transfers between devices with their start and end apart: 36, of which 22 were waited for; matrix products, arithmetic and copies ran while one was open for 1% of the time, Pallas kernels for 26%

profile of v5, /device:TPU:0, one launch (start us, length us, event | category | flops | bytes accessed | tf_op | source)
XLA Modules:
  0.0 115.7 jit_solution(18390095686336852215)
XLA Ops:
  1.8 2.6 %collective-permute-start.2 = (bf16[512,512]{1,0:T(8,128)(2,1)S(1)}, bf16[512,512]{1,0:T(8,128)(2,1)S(1)}, u32[]{:S(2)}, u32[]{:S(2)}) collective-permute-start(bf16[512,512]{1,0:T(8,128)(2,1)S(1)} %get-tuple-element.129), channel_id=1, source_target_pairs={{0,8},{8,0},{16,24},{24,16},{1,9},{9,1},{17,25},{25,17},{2,10},{10... | collective-permute-start | bytes 1572872 | tf_op jit(solution)/shard_map/ppermute | solution.py:377
  6.0 4.3 %collective-permute-done.sib_ref = s32[128]{0:T(128)S(1)} collective-permute-done((s32[128]{0:T(128)S(1)}, s32[128]{0:T(128)S(1)}, u32[]{:S(2)}, u32[]{:S(2)}) %collective-permute-start) | collective-permute-done | bytes 544 | tf_op jit(solution)/shard_map/ppermute | solution.py:374
  10.7 6.7 %hold.1 = (s32[3]{0:T(128)S(1)}, s32[104]{0:T(128)S(1)}, s32[104]{0:T(128)S(1)}, s32[104]{0:T(128)S(1)}, s32[208]{0:T(256)S(1)}, /*index=5*/s32[208]{0:T(256)S(1)}, bf16[104,256,256]{2,1,0:T(8,128)(2,1)S(1)}) custom-call(s32[1]{0:T(128)} %constant.8.clone.1.order, s32[128]{0:T(128)S(1)} %pad_add_fusion.own_ref, s32[128]{0:T(128)S(1)} %collective-permute-done.sib_ref, ...), custom_call_target="tpu_custom_call" | custom-call | bytes 12583936 | tf_op jit(solution)/shard_map/hold/pallas_call | solution.py:413
  17.5 6.5 %collective-permute-done.3.refs_1_ = bf16[512,512]{1,0:T(8,128)(2,1)S(1)} collective-permute-done((bf16[512,512]{1,0:T(8,128)(2,1)S(1)}, bf16[512,512]{1,0:T(8,128)(2,1)S(1)}, u32[]{:S(2)}, u32[]{:S(2)}) %collective-permute-start.3) | collective-permute-done | bytes 524320 | tf_op jit(solution)/shard_map/ppermute | solution.py:377
  26.5 3.7 %products_sent.3 = (s16[2064,256]{1,0:T(8,128)(2,1)S(1)}, bf16[16,256,256]{2,1,0:T(8,128)(2,1)S(1)}) custom-call(s32[1]{0:T(128)} %constant.8.clone.1.order, s32[3]{0:T(128)S(1)} %get-tuple-element.70.count_ref, s32[208]{0:T(256)S(1)} %get-tuple-element.71.order_ref, s32[104]{0:T(128)S(1)} %get-tuple-element.72.slot_ref, ...), custom_call_target="tpu_custom_call" | custom-call | bytes 16778892 | tf_op jit(solution)/shard_map/products_sent/pallas_call | solution.py:413
  30.3 2.9 %collective-permute-start.6 = (bf16[1024,256]{1,0:T(8,128)(2,1)S(1)}, bf16[1024,256]{1,0:T(8,128)(2,1)S(1)}, u32[]{:S(2)}, u32[]{:S(2)}) collective-permute-start(bf16[1024,256]{1,0:T(8,128)(2,1)S(1)} %join.3.refs_0_), channel_id=1, source_target_pairs={{0,1},{1,0},{2,3},{3,2},{4,5},{5,4},{6,7},{7,6},{8,9},{9,8},{10,11... | collective-permute-start | bytes 1572872 | tf_op jit(solution)/shard_map/ppermute | solution.py:374
  33.2 2.3 %products_kept.3.kept = f32[9,256,256]{2,1,0:T(8,128)S(1)} custom-call(s32[1]{0:T(128)} %constant.8.clone.1.order, s32[3]{0:T(128)S(1)} %get-tuple-element.70.count_ref, s32[208]{0:T(256)S(1)} %get-tuple-element.71.order_ref, s32[104]{0:T(128)S(1)} %get-tuple-element.72.slot_ref, s32[104]{0:T(128)S(1)} %get-tuple-element.73.label_ref, ...), custom_call_target="tpu_custom_call" | custom-call | bytes 15730316 | tf_op jit(solution)/shard_map/products_kept/pallas_call | solution.py:413
  35.4 3.1 %collective-permute-done.7.refs_2_ = bf16[1024,256]{1,0:T(8,128)(2,1)S(1)} collective-permute-done((bf16[1024,256]{1,0:T(8,128)(2,1)S(1)}, bf16[1024,256]{1,0:T(8,128)(2,1)S(1)}, u32[]{:S(2)}, u32[]{:S(2)}) %collective-permute-start.7) | collective-permute-done | bytes 524320 | tf_op jit(solution)/shard_map/ppermute | solution.py:377
  40.4 3.1 %products_sent.4 = (s16[1040,256]{1,0:T(8,128)(2,1)S(1)}, s16[1040,256]{1,0:T(8,128)(2,1)S(1)}, bf16[16,256,256]{2,1,0:T(8,128)(2,1)S(1)}) custom-call(s32[1]{0:T(128)} %constant.8.clone.1.order, s32[3]{0:T(128)S(1)} %get-tuple-element.70.count_ref, s32[208]{0:T(256)S(1)} %get-tuple-element.78.order_ref, s32[104]{0:T(128)S(1)} %get-tuple-element.79.slot_ref, ...), custom_call_target="tpu_custom_call" | custom-call | bytes 17303180 | tf_op jit(solution)/shard_map/products_sent/pallas_call | solution.py:413
  43.6 2.1 %collective-permute-start.14 = (s16[1040,256]{1,0:T(8,128)(2,1)S(1)}, s16[1040,256]{1,0:T(8,128)(2,1)S(1)}, u32[]{:S(2)}, u32[]{:S(2)}) collective-permute-start(s16[1040,256]{1,0:T(8,128)(2,1)S(1)} %get-tuple-element.92), channel_id=1, source_target_pairs={{0,16},{8,24},{16,0},{24,8},{1,17},{9,25},{17,1},{25,9},{2,18},{10... | collective-permute-start | bytes 1597448 | tf_op jit(solution)/shard_map/ppermute | solution.py:377
  45.7 2.7 %products_kept.4.kept = f32[9,256,256]{2,1,0:T(8,128)S(1)} custom-call(s32[1]{0:T(128)} %constant.8.clone.1.order, s32[3]{0:T(128)S(1)} %get-tuple-element.70.count_ref, s32[208]{0:T(256)S(1)} %get-tuple-element.78.order_ref, s32[104]{0:T(128)S(1)} %get-tuple-element.79.slot_ref, s32[104]{0:T(128)S(1)} %get-tuple-element.73.label_ref, ...), custom_call_target="tpu_custom_call" | custom-call | bytes 15730316 | tf_op jit(solution)/shard_map/products_kept/pallas_call | solution.py:413
  48.5 3.2 %products_sent.5 = (s16[1040,256]{1,0:T(8,128)(2,1)S(1)}, s16[1040,256]{1,0:T(8,128)(2,1)S(1)}, bf16[16,256,256]{2,1,0:T(8,128)(2,1)S(1)}) custom-call(s32[1]{0:T(128)} %constant.8.clone.1.order, s32[3]{0:T(128)S(1)} %get-tuple-element.70.count_ref, s32[208]{0:T(256)S(1)} %get-tuple-element.78.order_ref, s32[104]{0:T(128)S(1)} %get-tuple-element.79.slot_ref, ...), custom_call_target="tpu_custom_call" | custom-call | bytes 17303180 | tf_op jit(solution)/shard_map/products_sent/pallas_call | solution.py:413
  53.8 2.9 %products_kept.5.kept = f32[9,256,256]{2,1,0:T(8,128)S(1)} custom-call(s32[1]{0:T(128)} %constant.8.clone.1.order, s32[3]{0:T(128)S(1)} %get-tuple-element.70.count_ref, s32[208]{0:T(256)S(1)} %get-tuple-element.78.order_ref, s32[104]{0:T(128)S(1)} %get-tuple-element.79.slot_ref, s32[104]{0:T(128)S(1)} %get-tuple-element.73.label_ref, ...), custom_call_target="tpu_custom_call" | custom-call | bytes 15730316 | tf_op jit(solution)/shard_map/products_kept/pallas_call | solution.py:413
  58.7 2.0 %collective-permute-done.13.recv_a = s16[1040,256]{1,0:T(8,128)(2,1)S(1)} collective-permute-done((s16[1040,256]{1,0:T(8,128)(2,1)S(1)}, s16[1040,256]{1,0:T(8,128)(2,1)S(1)}, u32[]{:S(2)}, u32[]{:S(2)}) %collective-permute-start.13) | collective-permute-done | bytes 532512 | tf_op jit(solution)/shard_map/ppermute | solution.py:377
  62.6 7.5 %collective-permute-done.16.recv_b = s16[1040,256]{1,0:T(8,128)(2,1)S(1)} collective-permute-done((s16[1040,256]{1,0:T(8,128)(2,1)S(1)}, s16[1040,256]{1,0:T(8,128)(2,1)S(1)}, u32[]{:S(2)}, u32[]{:S(2)}) %collective-permute-start.16) | collective-permute-done | bytes 532512 | tf_op jit(solution)/shard_map/ppermute | solution.py:377
  70.1 2.0 %collective-permute-done.15.recv_a = s16[1040,256]{1,0:T(8,128)(2,1)S(1)} collective-permute-done((s16[1040,256]{1,0:T(8,128)(2,1)S(1)}, s16[1040,256]{1,0:T(8,128)(2,1)S(1)}, u32[]{:S(2)}, u32[]{:S(2)}) %collective-permute-start.15) | collective-permute-done | bytes 532512 | tf_op jit(solution)/shard_map/ppermute | solution.py:377
  74.0 3.9 %collective-permute-done.18.recv_b = s16[528,256]{1,0:T(8,128)(2,1)S(1)} collective-permute-done((s16[528,256]{1,0:T(8,128)(2,1)S(1)}, s16[528,256]{1,0:T(8,128)(2,1)S(1)}, u32[]{:S(2)}, u32[]{:S(2)}) %collective-permute-start.18) | collective-permute-done | bytes 270368 | tf_op jit(solution)/shard_map/ppermute | solution.py:377
  78.8 4.8 %collective-permute-done.19.recv = s16[1040,256]{1,0:T(8,128)(2,1)S(1)} collective-permute-done((s16[1040,256]{1,0:T(8,128)(2,1)S(1)}, s16[1040,256]{1,0:T(8,128)(2,1)S(1)}, u32[]{:S(2)}, u32[]{:S(2)}) %collective-permute-start.19) | collective-permute-done | bytes 532512 | tf_op jit(solution)/shard_map/ppermute | solution.py:380
  85.7 3.7 %collective-permute-done.22.recv = s16[528,256]{1,0:T(8,128)(2,1)S(1)} collective-permute-done((s16[528,256]{1,0:T(8,128)(2,1)S(1)}, s16[528,256]{1,0:T(8,128)(2,1)S(1)}, u32[]{:S(2)}, u32[]{:S(2)}) %collective-permute-start.22) | collective-permute-done | bytes 270368 | tf_op jit(solution)/shard_map/ppermute | solution.py:380
  89.8 2.4 %collective-permute-done.24.recv_b = s16[528,256]{1,0:T(8,128)(2,1)S(1)} collective-permute-done((s16[528,256]{1,0:T(8,128)(2,1)S(1)}, s16[528,256]{1,0:T(8,128)(2,1)S(1)}, u32[]{:S(2)}, u32[]{:S(2)}) %collective-permute-start.24) | collective-permute-done | bytes 270368 | tf_op jit(solution)/shard_map/ppermute | solution.py:377
  94.7 1.9 %collective-permute-done.25.recv = s16[528,256]{1,0:T(8,128)(2,1)S(1)} collective-permute-done((s16[528,256]{1,0:T(8,128)(2,1)S(1)}, s16[528,256]{1,0:T(8,128)(2,1)S(1)}, u32[]{:S(2)}, u32[]{:S(2)}) %collective-permute-start.25) | collective-permute-done | bytes 270368 | tf_op jit(solution)/shard_map/ppermute | solution.py:380
  96.9 2.1 %collective-permute-done.26.recv = s16[272,256]{1,0:T(8,128)(2,1)S(1)} collective-permute-done((s16[272,256]{1,0:T(8,128)(2,1)S(1)}, s16[272,256]{1,0:T(8,128)(2,1)S(1)}, u32[]{:S(2)}, u32[]{:S(2)}) %collective-permute-start.26) | collective-permute-done | bytes 139296 | tf_op jit(solution)/shard_map/ppermute | solution.py:380
  105.7 1.8 %collective-permute-start.34 = (s16[272,256]{1,0:T(8,128)(2,1)S(1)}, s16[272,256]{1,0:T(8,128)(2,1)S(1)}, u32[]{:S(2)}, u32[]{:S(2)}) collective-permute-start(s16[272,256]{1,0:T(8,128)(2,1)S(1)} %finish.3.refs_0_), channel_id=1, source_target_pairs={{0,16},{8,24},{16,0},{24,8},{1,17},{9,25},{17,1},{25,9},{2,18},{10... | collective-permute-start | bytes 417800 | tf_op jit(solution)/shard_map/ppermute | solution.py:377
  109.9 2.9 %collective-permute-done.35.refs_3_ = s16[272,256]{1,0:T(8,128)(2,1)S(1)} collective-permute-done((s16[272,256]{1,0:T(8,128)(2,1)S(1)}, s16[272,256]{1,0:T(8,128)(2,1)S(1)}, u32[]{:S(2)}, u32[]{:S(2)}) %collective-permute-start.35) | collective-permute-done | bytes 139296 | tf_op jit(solution)/shard_map/ppermute | solution.py:377
  (83 shorter events, 33.9 us)
Async XLA Ops:
  0.0 10.6 %collective-permute-start.1 = (bf16[48,256,256]{2,1,0:T(8,128)(2,1)}, bf16[48,256,256]{2,1,0:T(8,128)(2,1)}, u32[]{:S(2)}, u32[]{:S(2)}) collective-permute-start(bf16[48,256,256]{2,1,0:T(8,128)(2,1)} %own_tiles.1), channel_id=1, source_target_pairs={{0,1},{1,0},{2,3},{3,2},{4,5},{5,4},{6,7},{7,6},{8,9},{9,8},{10,11... | collective-permute-start | bytes 18874376 | tf_op jit(solution)/shard_map/ppermute | solution.py:374
  1.8 15.6 %collective-permute-start.2 = (bf16[512,512]{1,0:T(8,128)(2,1)S(1)}, bf16[512,512]{1,0:T(8,128)(2,1)S(1)}, u32[]{:S(2)}, u32[]{:S(2)}) collective-permute-start(bf16[512,512]{1,0:T(8,128)(2,1)S(1)} %get-tuple-element.129), channel_id=1, source_target_pairs={{0,8},{8,0},{16,24},{24,16},{1,9},{9,1},{17,25},{25,17},{2,10},{10... | collective-permute-start | bytes 1572872 | tf_op jit(solution)/shard_map/ppermute | solution.py:377
  4.4 19.6 %collective-permute-start.3 = (bf16[512,512]{1,0:T(8,128)(2,1)S(1)}, bf16[512,512]{1,0:T(8,128)(2,1)S(1)}, u32[]{:S(2)}, u32[]{:S(2)}) collective-permute-start(bf16[512,512]{1,0:T(8,128)(2,1)S(1)} %get-tuple-element.128), channel_id=1, source_target_pairs={{0,16},{8,24},{16,0},{24,8},{1,17},{9,25},{17,1},{25,9},{2,18},{10... | collective-permute-start | bytes 1572872 | tf_op jit(solution)/shard_map/ppermute | solution.py:377
  5.9 18.2 %collective-permute-start.4 = (bf16[512,256]{1,0:T(8,128)(2,1)S(1)}, bf16[512,256]{1,0:T(8,128)(2,1)S(1)}, u32[]{:S(2)}, u32[]{:S(2)}) collective-permute-start(bf16[512,256]{1,0:T(8,128)(2,1)S(1)} %get-tuple-element.126), channel_id=1, source_target_pairs={{0,24},{8,16},{16,8},{24,0},{1,25},{9,17},{17,9},{25,1},{2,26},{10... | collective-permute-start | bytes 786440 | tf_op jit(solution)/shard_map/ppermute | solution.py:377
  24.2 14.3 %collective-permute-start.7 = (bf16[1024,256]{1,0:T(8,128)(2,1)S(1)}, bf16[1024,256]{1,0:T(8,128)(2,1)S(1)}, u32[]{:S(2)}, u32[]{:S(2)}) collective-permute-start(bf16[1024,256]{1,0:T(8,128)(2,1)S(1)} %join.3.refs_0_), channel_id=1, source_target_pairs={{0,16},{8,24},{16,0},{24,8},{1,17},{9,25},{17,1},{25,9},{2,18},{10... | collective-permute-start | bytes 1572872 | tf_op jit(solution)/shard_map/ppermute | solution.py:377
  25.8 14.0 %collective-permute-start.10 = (bf16[1024,256]{1,0:T(8,128)(2,1)S(1)}, bf16[1024,256]{1,0:T(8,128)(2,1)S(1)}, u32[]{:S(2)}, u32[]{:S(2)}) collective-permute-start(bf16[1024,256]{1,0:T(8,128)(2,1)S(1)} %join.4.refs_0_), channel_id=1, source_target_pairs={{0,8},{8,0},{16,24},{24,16},{1,9},{9,1},{17,25},{25,17},{2,10},{10... | collective-permute-start | bytes 1572872 | tf_op jit(solution)/shard_map/ppermute | solution.py:377
  30.2 26.5 %collective-permute-start.12 = (s16[2064,256]{1,0:T(8,128)(2,1)S(1)}, s16[2064,256]{1,0:T(8,128)(2,1)S(1)}, u32[]{:S(2)}, u32[]{:S(2)}) collective-permute-start(s16[2064,256]{1,0:T(8,128)(2,1)S(1)} %get-tuple-element.74), channel_id=1, source_target_pairs={{0,2},{1,3},{2,0},{3,1},{4,6},{5,7},{6,4},{7,5},{8,10},{9,11},{10,... | collective-permute-start | bytes 3170312 | tf_op jit(solution)/shard_map/ppermute | solution.py:380
  30.3 9.5 %collective-permute-start.6 = (bf16[1024,256]{1,0:T(8,128)(2,1)S(1)}, bf16[1024,256]{1,0:T(8,128)(2,1)S(1)}, u32[]{:S(2)}, u32[]{:S(2)}) collective-permute-start(bf16[1024,256]{1,0:T(8,128)(2,1)S(1)} %join.3.refs_0_), channel_id=1, source_target_pairs={{0,1},{1,0},{2,3},{3,2},{4,5},{5,4},{6,7},{7,6},{8,9},{9,8},{10,11... | collective-permute-start | bytes 1572872 | tf_op jit(solution)/shard_map/ppermute | solution.py:374
  38.5 9.9 %collective-permute-start.9 = (bf16[1024,256]{1,0:T(8,128)(2,1)S(1)}, bf16[1024,256]{1,0:T(8,128)(2,1)S(1)}, u32[]{:S(2)}, u32[]{:S(2)}) collective-permute-start(bf16[1024,256]{1,0:T(8,128)(2,1)S(1)} %join.4.refs_0_), channel_id=1, source_target_pairs={{0,1},{1,0},{2,3},{3,2},{4,5},{5,4},{6,7},{7,6},{8,9},{9,8},{10,11... | collective-permute-start | bytes 1572872 | tf_op jit(solution)/shard_map/ppermute | solution.py:374
  39.8 8.7 %collective-permute-start.11 = (bf16[1024,256]{1,0:T(8,128)(2,1)S(1)}, bf16[1024,256]{1,0:T(8,128)(2,1)S(1)}, u32[]{:S(2)}, u32[]{:S(2)}) collective-permute-start(bf16[1024,256]{1,0:T(8,128)(2,1)S(1)} %collective-permute-done.10.refs_2_), channel_id=1, source_target_pairs={{0,1},{1,0},{2,3},{3,2},{4,5},{5,4},{6,7},{7,6},{8,9},{9,8},{10,11... | collective-permute-start | bytes 1572872 | tf_op jit(solution)/shard_map/ppermute | solution.py:374
  43.6 15.1 %collective-permute-start.14 = (s16[1040,256]{1,0:T(8,128)(2,1)S(1)}, s16[1040,256]{1,0:T(8,128)(2,1)S(1)}, u32[]{:S(2)}, u32[]{:S(2)}) collective-permute-start(s16[1040,256]{1,0:T(8,128)(2,1)S(1)} %get-tuple-element.92), channel_id=1, source_target_pairs={{0,16},{8,24},{16,0},{24,8},{1,17},{9,25},{17,1},{25,9},{2,18},{10... | collective-permute-start | bytes 1597448 | tf_op jit(solution)/shard_map/ppermute | solution.py:377
  45.7 15.0 %collective-permute-start.13 = (s16[1040,256]{1,0:T(8,128)(2,1)S(1)}, s16[1040,256]{1,0:T(8,128)(2,1)S(1)}, u32[]{:S(2)}, u32[]{:S(2)}) collective-permute-start(s16[1040,256]{1,0:T(8,128)(2,1)S(1)} %get-tuple-element.81), channel_id=1, source_target_pairs={{0,8},{8,0},{16,24},{24,16},{1,9},{9,1},{17,25},{25,17},{2,10},{10... | collective-permute-start | bytes 1597448 | tf_op jit(solution)/shard_map/ppermute | solution.py:377
  51.7 18.4 %collective-permute-start.16 = (s16[1040,256]{1,0:T(8,128)(2,1)S(1)}, s16[1040,256]{1,0:T(8,128)(2,1)S(1)}, u32[]{:S(2)}, u32[]{:S(2)}) collective-permute-start(s16[1040,256]{1,0:T(8,128)(2,1)S(1)} %get-tuple-element.95), channel_id=1, source_target_pairs={{0,16},{8,24},{16,0},{24,8},{1,17},{9,25},{17,1},{25,9},{2,18},{10... | collective-permute-start | bytes 1597448 | tf_op jit(solution)/shard_map/ppermute | solution.py:377
  53.4 18.8 %collective-permute-start.15 = (s16[1040,256]{1,0:T(8,128)(2,1)S(1)}, s16[1040,256]{1,0:T(8,128)(2,1)S(1)}, u32[]{:S(2)}, u32[]{:S(2)}) collective-permute-start(s16[1040,256]{1,0:T(8,128)(2,1)S(1)} %get-tuple-element.86), channel_id=1, source_target_pairs={{0,8},{8,0},{16,24},{24,16},{1,9},{9,1},{17,25},{25,17},{2,10},{10... | collective-permute-start | bytes 1597448 | tf_op jit(solution)/shard_map/ppermute | solution.py:377
  57.2 26.4 %collective-permute-start.19 = (s16[1040,256]{1,0:T(8,128)(2,1)S(1)}, s16[1040,256]{1,0:T(8,128)(2,1)S(1)}, u32[]{:S(2)}, u32[]{:S(2)}) collective-permute-start(s16[1040,256]{1,0:T(8,128)(2,1)S(1)} %get-tuple-element.90), channel_id=1, source_target_pairs={{0,4},{1,5},{2,6},{3,7},{4,0},{5,1},{6,2},{7,3},{8,12},{9,13},{10,... | collective-permute-start | bytes 1597448 | tf_op jit(solution)/shard_map/ppermute | solution.py:380
  61.3 16.6 %collective-permute-start.18 = (s16[528,256]{1,0:T(8,128)(2,1)S(1)}, s16[528,256]{1,0:T(8,128)(2,1)S(1)}, u32[]{:S(2)}, u32[]{:S(2)}) collective-permute-start(s16[528,256]{1,0:T(8,128)(2,1)S(1)} %get-tuple-element.98), channel_id=1, source_target_pairs={{0,8},{8,0},{16,24},{24,16},{1,9},{9,1},{17,25},{25,17},{2,10},{10... | collective-permute-start | bytes 811016 | tf_op jit(solution)/shard_map/ppermute | solution.py:377
  61.4 16.5 %collective-permute-start.17 = (s16[528,256]{1,0:T(8,128)(2,1)S(1)}, s16[528,256]{1,0:T(8,128)(2,1)S(1)}, u32[]{:S(2)}, u32[]{:S(2)}) collective-permute-start(s16[528,256]{1,0:T(8,128)(2,1)S(1)} %get-tuple-element.93), channel_id=1, source_target_pairs={{0,16},{8,24},{16,0},{24,8},{1,17},{9,25},{17,1},{25,9},{2,18},{10... | collective-permute-start | bytes 811016 | tf_op jit(solution)/shard_map/ppermute | solution.py:377
  72.7 12.4 %collective-permute-start.21 = (s16[528,256]{1,0:T(8,128)(2,1)S(1)}, s16[528,256]{1,0:T(8,128)(2,1)S(1)}, u32[]{:S(2)}, u32[]{:S(2)}) collective-permute-start(s16[528,256]{1,0:T(8,128)(2,1)S(1)} %get-tuple-element.105), channel_id=1, source_target_pairs={{0,8},{8,0},{16,24},{24,16},{1,9},{9,1},{17,25},{25,17},{2,10},{10... | collective-permute-start | bytes 811016 | tf_op jit(solution)/shard_map/ppermute | solution.py:377
  72.8 12.3 %collective-permute-start.20 = (s16[528,256]{1,0:T(8,128)(2,1)S(1)}, s16[528,256]{1,0:T(8,128)(2,1)S(1)}, u32[]{:S(2)}, u32[]{:S(2)}) collective-permute-start(s16[528,256]{1,0:T(8,128)(2,1)S(1)} %get-tuple-element.96), channel_id=1, source_target_pairs={{0,16},{8,24},{16,0},{24,8},{1,17},{9,25},{17,1},{25,9},{2,18},{10... | collective-permute-start | bytes 811016 | tf_op jit(solution)/shard_map/ppermute | solution.py:377
  78.2 11.2 %collective-permute-start.22 = (s16[528,256]{1,0:T(8,128)(2,1)S(1)}, s16[528,256]{1,0:T(8,128)(2,1)S(1)}, u32[]{:S(2)}, u32[]{:S(2)}) collective-permute-start(s16[528,256]{1,0:T(8,128)(2,1)S(1)} %get-tuple-element.100), channel_id=1, source_target_pairs={{0,2},{1,3},{2,0},{3,1},{4,6},{5,7},{6,4},{7,5},{8,10},{9,11},{10,... | collective-permute-start | bytes 811016 | tf_op jit(solution)/shard_map/ppermute | solution.py:380
  85.4 11.3 %collective-permute-start.25 = (s16[528,256]{1,0:T(8,128)(2,1)S(1)}, s16[528,256]{1,0:T(8,128)(2,1)S(1)}, u32[]{:S(2)}, u32[]{:S(2)}) collective-permute-start(s16[528,256]{1,0:T(8,128)(2,1)S(1)} %get-tuple-element.107), channel_id=1, source_target_pairs={{0,2},{1,3},{2,0},{3,1},{4,6},{5,7},{6,4},{7,5},{8,10},{9,11},{10,... | collective-permute-start | bytes 811016 | tf_op jit(solution)/shard_map/ppermute | solution.py:380
  89.5 9.4 %collective-permute-start.26 = (s16[272,256]{1,0:T(8,128)(2,1)S(1)}, s16[272,256]{1,0:T(8,128)(2,1)S(1)}, u32[]{:S(2)}, u32[]{:S(2)}) collective-permute-start(s16[272,256]{1,0:T(8,128)(2,1)S(1)} %get-tuple-element.110), channel_id=1, source_target_pairs={{0,4},{1,5},{2,6},{3,7},{4,0},{5,1},{6,2},{7,3},{8,12},{9,13},{10,... | collective-permute-start | bytes 417800 | tf_op jit(solution)/shard_map/ppermute | solution.py:380
  93.0 9.6 %collective-permute-start.27 = (s16[528,256]{1,0:T(8,128)(2,1)S(1)}, s16[528,256]{1,0:T(8,128)(2,1)S(1)}, u32[]{:S(2)}, u32[]{:S(2)}) collective-permute-start(s16[528,256]{1,0:T(8,128)(2,1)S(1)} %get-tuple-element.113.refs_0_), channel_id=1, source_target_pairs={{0,16},{8,24},{16,0},{24,8},{1,17},{9,25},{17,1},{25,9},{2,18},{10... | collective-permute-start | bytes 811016 | tf_op jit(solution)/shard_map/ppermute | solution.py:377
  100.0 8.9 %collective-permute-start.31 = (s16[272,256]{1,0:T(8,128)(2,1)S(1)}, s16[272,256]{1,0:T(8,128)(2,1)S(1)}, u32[]{:S(2)}, u32[]{:S(2)}) collective-permute-start(s16[272,256]{1,0:T(8,128)(2,1)S(1)} %finish.2.refs_0_), channel_id=1, source_target_pairs={{0,16},{8,24},{16,0},{24,8},{1,17},{9,25},{17,1},{25,9},{2,18},{10... | collective-permute-start | bytes 417800 | tf_op jit(solution)/shard_map/ppermute | solution.py:377
  (16 other events, 107.2 us)

commit v6 on v5

--- a/solution.py
+++ b/solution.py
@@ -477,16 +477,18 @@
             extra=[pltpu.VMEM((half + 1, side, CHUNK), jnp.float32)],
             mib=24,
         )
-        (kept,) = call(
-            functools.partial(kept_kernel, which),
-            "products_kept",
-            [stack_of(half + 1, plain)],
-            *lists,
-            held,
-            stacked,
-            smem=4,
-            mib=24,
-        )
+        def kept():
+            return call(
+                functools.partial(kept_kernel, which),
+                "products_kept",
+                [stack_of(half + 1, plain)],
+                *lists,
+                held,
+                stacked,
+                smem=4,
+                mib=24,
+            )[0]
+
         return *sends, kept
 
     def gathered(done):
@@ -528,23 +530,25 @@
     slots, orders = {1: in_plane, 2: in_line}, {1: plane_order, 2: line_order}
     pairs = {j: pair(j) for j in (1, 2)}
 
-    send, keep_0 = products(0, 2, [coded(half)], *join(0))
+    send, kept = products(0, 2, [coded(half)], *join(0))
+    keep_0 = kept()
     sent_0 = send
     sent, keep = {}, {}
     for j in (1, 2):
         fill, (*parts, second) = pairs[j]
         second = lax.optimization_barrier((second, keep_0))[0]
         parts += [second, to_core(second)]
-        send_a, send_b, keep[j] = products(j, 1, [coded(quarter)] * 2, fill, parts)
+        send_a, send_b, kept = products(j, 1, [coded(quarter)] * 2, fill, parts)
         sent[j] = send_a, send_b
-
-    sent_0, keep_0 = call(
-        line_kernel,
-        "line",
-        [coded(quarter), stack_of(quarter, plain)],
-        to_line(sent_0, 0),
-        keep_0,
-    )
+        if j == 2:
+            sent_0, keep_0 = call(
+                line_kernel,
+                "line",
+                [coded(quarter), stack_of(quarter, plain)],
+                to_line(sent_0, 0),
+                keep_0,
+            )
+        keep[j] = kept()
 
     def plane(j):
         return call(

time: 116 us -> 115 us (level)
  starting transfers between devices: 29.6 us -> 34 us
  waiting for transfers between devices: 53 us -> 48.6 us
    ppermute x6, starting transfers between devices: 2.18 us -> 6.9 us  [to_line(): return lax.ppermute(v, 'wide', [(i, i ^ 2 << b) for i in range(wide_count)])]
    ppermute x6, waiting for transfers between devices: 14 us -> 11.3 us  [to_line(): return lax.ppermute(v, 'wide', [(i, i ^ 2 << b) for i in range(wide_count)])]
    ppermute x7, starting transfers between devices: 4.02 us -> 1.96 us  [to_core(): return lax.ppermute(v, 'wide', [(i, i ^ 1) for i in range(wide_count)])]
    ppermute x23, starting transfers between devices: 23.4 us -> 25.1 us  [to_grp(): return lax.ppermute(v, 'grp', [(i, i ^ d) for i in range(4)])]
    ppermute x23, waiting for transfers between devices: 33.5 us -> 31.9 us  [to_grp(): return lax.ppermute(v, 'grp', [(i, i ^ d) for i in range(4)])]
  transfers between devices with their start and end apart: 36 -> 36, of which waited for: 22 -> 21; matrix products, arithmetic and copies ran while one was open for 1% -> 1% of each run, Pallas kernels for 26% -> 26%
where the time goes in v6:
time: 115 us
  waiting for transfers between devices  48.6 us (42%)
  starting transfers between devices  34 us (30%)
  Pallas kernels  30.8 us (27%)
  local copies, waits for them, and re-layouts  1.18 us (1%)
    ppermute x23, waiting for transfers between devices, to_grp(): return lax.ppermute(v, 'grp', [(i, i ^ d) for i in range(4)])  31.9 us
    pallas_call x24, Pallas kernels, call(): pl.pallas_call(body, in_specs=more.pop('in_specs', in_any(1) + in_smem(sm...  30.8 us
    ppermute x23, starting transfers between devices, to_grp(): return lax.ppermute(v, 'grp', [(i, i ^ d) for i in range(4)])  25.1 us
    ppermute x6, waiting for transfers between devices, to_line(): return lax.ppermute(v, 'wide', [(i, i ^ 2 << b) for i in range(wide_count)])  11.3 us
    ppermute x6, starting transfers between devices, to_line(): return lax.ppermute(v, 'wide', [(i, i ^ 2 << b) for i in range(wide_count)])  6.9 us
    ppermute x7, waiting for transfers between devices, to_core(): return lax.ppermute(v, 'wide', [(i, i ^ 1) for i in range(wide_count)])  5.47 us
  transfers between devices with their start and end apart: 36, of which 21 were waited for; matrix products, arithmetic and copies ran while one was open for 1% of the time, Pallas kernels for 26%

profile of v6, /device:TPU:0, one launch (start us, length us, event | category | flops | bytes accessed | tf_op | source)
XLA Modules:
  0.0 115.2 jit_solution(3866954070124086357)
XLA Ops:
  1.8 2.6 %collective-permute-start.2 = (bf16[512,512]{1,0:T(8,128)(2,1)S(1)}, bf16[512,512]{1,0:T(8,128)(2,1)S(1)}, u32[]{:S(2)}, u32[]{:S(2)}) collective-permute-start(bf16[512,512]{1,0:T(8,128)(2,1)S(1)} %get-tuple-element.129), channel_id=1, source_target_pairs={{0,8},{8,0},{16,24},{24,16},{1,9},{9,1},{17,25},{25,17},{2,10},{10... | collective-permute-start | bytes 1572872 | tf_op jit(solution)/shard_map/ppermute | solution.py:377
  6.0 4.3 %collective-permute-done.sib_ref = s32[128]{0:T(128)S(1)} collective-permute-done((s32[128]{0:T(128)S(1)}, s32[128]{0:T(128)S(1)}, u32[]{:S(2)}, u32[]{:S(2)}) %collective-permute-start) | collective-permute-done | bytes 544 | tf_op jit(solution)/shard_map/ppermute | solution.py:374
  10.7 6.8 %hold.1 = (s32[3]{0:T(128)S(1)}, s32[104]{0:T(128)S(1)}, s32[104]{0:T(128)S(1)}, s32[104]{0:T(128)S(1)}, s32[208]{0:T(256)S(1)}, /*index=5*/s32[208]{0:T(256)S(1)}, bf16[104,256,256]{2,1,0:T(8,128)(2,1)S(1)}) custom-call(s32[1]{0:T(128)} %constant.8.clone.1.order, s32[128]{0:T(128)S(1)} %pad_add_fusion.own_ref, s32[128]{0:T(128)S(1)} %collective-permute-done.sib_ref, ...), custom_call_target="tpu_custom_call" | custom-call | bytes 12583936 | tf_op jit(solution)/shard_map/hold/pallas_call | solution.py:413
  17.5 6.5 %collective-permute-done.3.refs_1_ = bf16[512,512]{1,0:T(8,128)(2,1)S(1)} collective-permute-done((bf16[512,512]{1,0:T(8,128)(2,1)S(1)}, bf16[512,512]{1,0:T(8,128)(2,1)S(1)}, u32[]{:S(2)}, u32[]{:S(2)}) %collective-permute-start.3) | collective-permute-done | bytes 524320 | tf_op jit(solution)/shard_map/ppermute | solution.py:377
  26.5 2.2 %products_sent.3 = (s16[2064,256]{1,0:T(8,128)(2,1)S(1)}, bf16[16,256,256]{2,1,0:T(8,128)(2,1)S(1)}) custom-call(s32[1]{0:T(128)} %constant.8.clone.1.order, s32[3]{0:T(128)S(1)} %get-tuple-element.70.count_ref, s32[208]{0:T(256)S(1)} %get-tuple-element.71.order_ref, s32[104]{0:T(128)S(1)} %get-tuple-element.72.slot_ref, ...), custom_call_target="tpu_custom_call" | custom-call | bytes 16778892 | tf_op jit(solution)/shard_map/products_sent/pallas_call | solution.py:413
  28.7 1.6 %collective-permute-start.12 = (s16[2064,256]{1,0:T(8,128)(2,1)S(1)}, s16[2064,256]{1,0:T(8,128)(2,1)S(1)}, u32[]{:S(2)}, u32[]{:S(2)}) collective-permute-start(s16[2064,256]{1,0:T(8,128)(2,1)S(1)} %get-tuple-element.74), channel_id=1, source_target_pairs={{0,2},{1,3},{2,0},{3,1},{4,6},{5,7},{6,4},{7,5},{8,10},{9,11},{10,... | collective-permute-start | bytes 3170312 | tf_op jit(solution)/shard_map/ppermute | solution.py:380
  31.2 3.3 %products_kept.3.kept = f32[9,256,256]{2,1,0:T(8,128)S(1)} custom-call(s32[1]{0:T(128)} %constant.8.clone.1.order, s32[3]{0:T(128)S(1)} %get-tuple-element.70.count_ref, s32[208]{0:T(256)S(1)} %get-tuple-element.71.order_ref, s32[104]{0:T(128)S(1)} %get-tuple-element.72.slot_ref, s32[104]{0:T(128)S(1)} %get-tuple-element.73.label_ref, ...), custom_call_target="tpu_custom_call" | custom-call | bytes 15730316 | tf_op jit(solution)/shard_map/products_kept/pallas_call | solution.py:413
  34.4 4.1 %collective-permute-done.7.refs_2_ = bf16[1024,256]{1,0:T(8,128)(2,1)S(1)} collective-permute-done((bf16[1024,256]{1,0:T(8,128)(2,1)S(1)}, bf16[1024,256]{1,0:T(8,128)(2,1)S(1)}, u32[]{:S(2)}, u32[]{:S(2)}) %collective-permute-start.7) | collective-permute-done | bytes 524320 | tf_op jit(solution)/shard_map/ppermute | solution.py:377
  40.4 3.1 %products_sent.4 = (s16[1040,256]{1,0:T(8,128)(2,1)S(1)}, s16[1040,256]{1,0:T(8,128)(2,1)S(1)}, bf16[16,256,256]{2,1,0:T(8,128)(2,1)S(1)}) custom-call(s32[1]{0:T(128)} %constant.8.clone.1.order, s32[3]{0:T(128)S(1)} %get-tuple-element.70.count_ref, s32[208]{0:T(256)S(1)} %get-tuple-element.78.order_ref, s32[104]{0:T(128)S(1)} %get-tuple-element.79.slot_ref, ...), custom_call_target="tpu_custom_call" | custom-call | bytes 17303180 | tf_op jit(solution)/shard_map/products_sent/pallas_call | solution.py:413
  45.7 2.7 %products_kept.4.kept = f32[9,256,256]{2,1,0:T(8,128)S(1)} custom-call(s32[1]{0:T(128)} %constant.8.clone.1.order, s32[3]{0:T(128)S(1)} %get-tuple-element.70.count_ref, s32[208]{0:T(256)S(1)} %get-tuple-element.78.order_ref, s32[104]{0:T(128)S(1)} %get-tuple-element.79.slot_ref, s32[104]{0:T(128)S(1)} %get-tuple-element.73.label_ref, ...), custom_call_target="tpu_custom_call" | custom-call | bytes 15730316 | tf_op jit(solution)/shard_map/products_kept/pallas_call | solution.py:413
  48.5 3.2 %products_sent.5 = (s16[1040,256]{1,0:T(8,128)(2,1)S(1)}, s16[1040,256]{1,0:T(8,128)(2,1)S(1)}, bf16[16,256,256]{2,1,0:T(8,128)(2,1)S(1)}) custom-call(s32[1]{0:T(128)} %constant.8.clone.1.order, s32[3]{0:T(128)S(1)} %get-tuple-element.70.count_ref, s32[208]{0:T(256)S(1)} %get-tuple-element.78.order_ref, s32[104]{0:T(128)S(1)} %get-tuple-element.79.slot_ref, ...), custom_call_target="tpu_custom_call" | custom-call | bytes 17303180 | tf_op jit(solution)/shard_map/products_sent/pallas_call | solution.py:413
  52.7 2.1 %collective-permute-done.12.recv = s16[2064,256]{1,0:T(8,128)(2,1)S(1)} collective-permute-done((s16[2064,256]{1,0:T(8,128)(2,1)S(1)}, s16[2064,256]{1,0:T(8,128)(2,1)S(1)}, u32[]{:S(2)}, u32[]{:S(2)}) %collective-permute-start.12) | collective-permute-done | bytes 1056800 | tf_op jit(solution)/shard_map/ppermute | solution.py:380
  55.3 3.0 %collective-permute-start.19 = (s16[1040,256]{1,0:T(8,128)(2,1)S(1)}, s16[1040,256]{1,0:T(8,128)(2,1)S(1)}, u32[]{:S(2)}, u32[]{:S(2)}) collective-permute-start(s16[1040,256]{1,0:T(8,128)(2,1)S(1)} %get-tuple-element.88), channel_id=1, source_target_pairs={{0,4},{1,5},{2,6},{3,7},{4,0},{5,1},{6,2},{7,3},{8,12},{9,13},{10,... | collective-permute-start | bytes 1597448 | tf_op jit(solution)/shard_map/ppermute | solution.py:380
  58.3 2.9 %products_kept.5.kept = f32[9,256,256]{2,1,0:T(8,128)S(1)} custom-call(s32[1]{0:T(128)} %constant.8.clone.1.order, s32[3]{0:T(128)S(1)} %get-tuple-element.70.count_ref, s32[208]{0:T(256)S(1)} %get-tuple-element.78.order_ref, s32[104]{0:T(128)S(1)} %get-tuple-element.79.slot_ref, s32[104]{0:T(128)S(1)} %get-tuple-element.73.label_ref, ...), custom_call_target="tpu_custom_call" | custom-call | bytes 15730316 | tf_op jit(solution)/shard_map/products_kept/pallas_call | solution.py:413
  62.9 7.1 %collective-permute-done.16.recv_b = s16[1040,256]{1,0:T(8,128)(2,1)S(1)} collective-permute-done((s16[1040,256]{1,0:T(8,128)(2,1)S(1)}, s16[1040,256]{1,0:T(8,128)(2,1)S(1)}, u32[]{:S(2)}, u32[]{:S(2)}) %collective-permute-start.16) | collective-permute-done | bytes 532512 | tf_op jit(solution)/shard_map/ppermute | solution.py:377
  73.4 3.4 %collective-permute-done.18.recv_b = s16[528,256]{1,0:T(8,128)(2,1)S(1)} collective-permute-done((s16[528,256]{1,0:T(8,128)(2,1)S(1)}, s16[528,256]{1,0:T(8,128)(2,1)S(1)}, u32[]{:S(2)}, u32[]{:S(2)}) %collective-permute-start.18) | collective-permute-done | bytes 270368 | tf_op jit(solution)/shard_map/ppermute | solution.py:377
  78.7 3.3 %collective-permute-done.19.recv = s16[1040,256]{1,0:T(8,128)(2,1)S(1)} collective-permute-done((s16[1040,256]{1,0:T(8,128)(2,1)S(1)}, s16[1040,256]{1,0:T(8,128)(2,1)S(1)}, u32[]{:S(2)}, u32[]{:S(2)}) %collective-permute-start.19) | collective-permute-done | bytes 532512 | tf_op jit(solution)/shard_map/ppermute | solution.py:380
  82.4 2.1 %collective-permute-start.24 = (s16[528,256]{1,0:T(8,128)(2,1)S(1)}, s16[528,256]{1,0:T(8,128)(2,1)S(1)}, u32[]{:S(2)}, u32[]{:S(2)}) collective-permute-start(s16[528,256]{1,0:T(8,128)(2,1)S(1)} %get-tuple-element.112.own_b), channel_id=1, source_target_pairs={{0,16},{8,24},{16,0},{24,8},{1,17},{9,25},{17,1},{25,9},{2,18},{10... | collective-permute-start | bytes 811016 | tf_op jit(solution)/shard_map/ppermute | solution.py:377
  84.9 3.0 %collective-permute-done.22.recv = s16[528,256]{1,0:T(8,128)(2,1)S(1)} collective-permute-done((s16[528,256]{1,0:T(8,128)(2,1)S(1)}, s16[528,256]{1,0:T(8,128)(2,1)S(1)}, u32[]{:S(2)}, u32[]{:S(2)}) %collective-permute-start.22) | collective-permute-done | bytes 270368 | tf_op jit(solution)/shard_map/ppermute | solution.py:380
  88.5 2.2 %collective-permute-done.24.recv_b = s16[528,256]{1,0:T(8,128)(2,1)S(1)} collective-permute-done((s16[528,256]{1,0:T(8,128)(2,1)S(1)}, s16[528,256]{1,0:T(8,128)(2,1)S(1)}, u32[]{:S(2)}, u32[]{:S(2)}) %collective-permute-start.24) | collective-permute-done | bytes 270368 | tf_op jit(solution)/shard_map/ppermute | solution.py:377
  94.4 1.7 %collective-permute-done.25.recv = s16[528,256]{1,0:T(8,128)(2,1)S(1)} collective-permute-done((s16[528,256]{1,0:T(8,128)(2,1)S(1)}, s16[528,256]{1,0:T(8,128)(2,1)S(1)}, u32[]{:S(2)}, u32[]{:S(2)}) %collective-permute-start.25) | collective-permute-done | bytes 270368 | tf_op jit(solution)/shard_map/ppermute | solution.py:380
  99.2 3.7 %collective-permute-start.31 = (s16[272,256]{1,0:T(8,128)(2,1)S(1)}, s16[272,256]{1,0:T(8,128)(2,1)S(1)}, u32[]{:S(2)}, u32[]{:S(2)}) collective-permute-start(s16[272,256]{1,0:T(8,128)(2,1)S(1)} %finish.2.refs_0_), channel_id=1, source_target_pairs={{0,16},{8,24},{16,0},{24,8},{1,17},{9,25},{17,1},{25,9},{2,18},{10... | collective-permute-start | bytes 417800 | tf_op jit(solution)/shard_map/ppermute | solution.py:377
  105.6 2.0 %collective-permute-start.34 = (s16[272,256]{1,0:T(8,128)(2,1)S(1)}, s16[272,256]{1,0:T(8,128)(2,1)S(1)}, u32[]{:S(2)}, u32[]{:S(2)}) collective-permute-start(s16[272,256]{1,0:T(8,128)(2,1)S(1)} %finish.3.refs_0_), channel_id=1, source_target_pairs={{0,16},{8,24},{16,0},{24,8},{1,17},{9,25},{17,1},{25,9},{2,18},{10... | collective-permute-start | bytes 417800 | tf_op jit(solution)/shard_map/ppermute | solution.py:377
  109.0 2.6 %collective-permute-done.35.refs_3_ = s16[272,256]{1,0:T(8,128)(2,1)S(1)} collective-permute-done((s16[272,256]{1,0:T(8,128)(2,1)S(1)}, s16[272,256]{1,0:T(8,128)(2,1)S(1)}, u32[]{:S(2)}, u32[]{:S(2)}) %collective-permute-start.35) | collective-permute-done | bytes 139296 | tf_op jit(solution)/shard_map/ppermute | solution.py:377
  (83 shorter events, 35.1 us)
Async XLA Ops:
  0.0 10.6 %collective-permute-start.1 = (bf16[48,256,256]{2,1,0:T(8,128)(2,1)}, bf16[48,256,256]{2,1,0:T(8,128)(2,1)}, u32[]{:S(2)}, u32[]{:S(2)}) collective-permute-start(bf16[48,256,256]{2,1,0:T(8,128)(2,1)} %own_tiles.1), channel_id=1, source_target_pairs={{0,1},{1,0},{2,3},{3,2},{4,5},{5,4},{6,7},{7,6},{8,9},{9,8},{10,11... | collective-permute-start | bytes 18874376 | tf_op jit(solution)/shard_map/ppermute | solution.py:374
  1.8 15.7 %collective-permute-start.2 = (bf16[512,512]{1,0:T(8,128)(2,1)S(1)}, bf16[512,512]{1,0:T(8,128)(2,1)S(1)}, u32[]{:S(2)}, u32[]{:S(2)}) collective-permute-start(bf16[512,512]{1,0:T(8,128)(2,1)S(1)} %get-tuple-element.129), channel_id=1, source_target_pairs={{0,8},{8,0},{16,24},{24,16},{1,9},{9,1},{17,25},{25,17},{2,10},{10... | collective-permute-start | bytes 1572872 | tf_op jit(solution)/shard_map/ppermute | solution.py:377
  4.4 19.6 %collective-permute-start.3 = (bf16[512,512]{1,0:T(8,128)(2,1)S(1)}, bf16[512,512]{1,0:T(8,128)(2,1)S(1)}, u32[]{:S(2)}, u32[]{:S(2)}) collective-permute-start(bf16[512,512]{1,0:T(8,128)(2,1)S(1)} %get-tuple-element.128), channel_id=1, source_target_pairs={{0,16},{8,24},{16,0},{24,8},{1,17},{9,25},{17,1},{25,9},{2,18},{10... | collective-permute-start | bytes 1572872 | tf_op jit(solution)/shard_map/ppermute | solution.py:377
  5.9 18.2 %collective-permute-start.4 = (bf16[512,256]{1,0:T(8,128)(2,1)S(1)}, bf16[512,256]{1,0:T(8,128)(2,1)S(1)}, u32[]{:S(2)}, u32[]{:S(2)}) collective-permute-start(bf16[512,256]{1,0:T(8,128)(2,1)S(1)} %get-tuple-element.126), channel_id=1, source_target_pairs={{0,24},{8,16},{16,8},{24,0},{1,25},{9,17},{17,9},{25,1},{2,26},{10... | collective-permute-start | bytes 786440 | tf_op jit(solution)/shard_map/ppermute | solution.py:377
  24.2 14.3 %collective-permute-start.7 = (bf16[1024,256]{1,0:T(8,128)(2,1)S(1)}, bf16[1024,256]{1,0:T(8,128)(2,1)S(1)}, u32[]{:S(2)}, u32[]{:S(2)}) collective-permute-start(bf16[1024,256]{1,0:T(8,128)(2,1)S(1)} %join.3.refs_0_), channel_id=1, source_target_pairs={{0,16},{8,24},{16,0},{24,8},{1,17},{9,25},{17,1},{25,9},{2,18},{10... | collective-permute-start | bytes 1572872 | tf_op jit(solution)/shard_map/ppermute | solution.py:377
  25.8 14.0 %collective-permute-start.10 = (bf16[1024,256]{1,0:T(8,128)(2,1)S(1)}, bf16[1024,256]{1,0:T(8,128)(2,1)S(1)}, u32[]{:S(2)}, u32[]{:S(2)}) collective-permute-start(bf16[1024,256]{1,0:T(8,128)(2,1)S(1)} %join.4.refs_0_), channel_id=1, source_target_pairs={{0,8},{8,0},{16,24},{24,16},{1,9},{9,1},{17,25},{25,17},{2,10},{10... | collective-permute-start | bytes 1572872 | tf_op jit(solution)/shard_map/ppermute | solution.py:377
  28.7 26.1 %collective-permute-start.12 = (s16[2064,256]{1,0:T(8,128)(2,1)S(1)}, s16[2064,256]{1,0:T(8,128)(2,1)S(1)}, u32[]{:S(2)}, u32[]{:S(2)}) collective-permute-start(s16[2064,256]{1,0:T(8,128)(2,1)S(1)} %get-tuple-element.74), channel_id=1, source_target_pairs={{0,2},{1,3},{2,0},{3,1},{4,6},{5,7},{6,4},{7,5},{8,10},{9,11},{10,... | collective-permute-start | bytes 3170312 | tf_op jit(solution)/shard_map/ppermute | solution.py:380
  30.3 9.5 %collective-permute-start.6 = (bf16[1024,256]{1,0:T(8,128)(2,1)S(1)}, bf16[1024,256]{1,0:T(8,128)(2,1)S(1)}, u32[]{:S(2)}, u32[]{:S(2)}) collective-permute-start(bf16[1024,256]{1,0:T(8,128)(2,1)S(1)} %join.3.refs_0_), channel_id=1, source_target_pairs={{0,1},{1,0},{2,3},{3,2},{4,5},{5,4},{6,7},{7,6},{8,9},{9,8},{10,11... | collective-permute-start | bytes 1572872 | tf_op jit(solution)/shard_map/ppermute | solution.py:374
  38.5 9.9 %collective-permute-start.9 = (bf16[1024,256]{1,0:T(8,128)(2,1)S(1)}, bf16[1024,256]{1,0:T(8,128)(2,1)S(1)}, u32[]{:S(2)}, u32[]{:S(2)}) collective-permute-start(bf16[1024,256]{1,0:T(8,128)(2,1)S(1)} %join.4.refs_0_), channel_id=1, source_target_pairs={{0,1},{1,0},{2,3},{3,2},{4,5},{5,4},{6,7},{7,6},{8,9},{9,8},{10,11... | collective-permute-start | bytes 1572872 | tf_op jit(solution)/shard_map/ppermute | solution.py:374
  43.6 17.6 %collective-permute-start.14 = (s16[1040,256]{1,0:T(8,128)(2,1)S(1)}, s16[1040,256]{1,0:T(8,128)(2,1)S(1)}, u32[]{:S(2)}, u32[]{:S(2)}) collective-permute-start(s16[1040,256]{1,0:T(8,128)(2,1)S(1)} %get-tuple-element.92), channel_id=1, source_target_pairs={{0,16},{8,24},{16,0},{24,8},{1,17},{9,25},{17,1},{25,9},{2,18},{10... | collective-permute-start | bytes 1597448 | tf_op jit(solution)/shard_map/ppermute | solution.py:377
  44.7 16.5 %collective-permute-start.13 = (s16[1040,256]{1,0:T(8,128)(2,1)S(1)}, s16[1040,256]{1,0:T(8,128)(2,1)S(1)}, u32[]{:S(2)}, u32[]{:S(2)}) collective-permute-start(s16[1040,256]{1,0:T(8,128)(2,1)S(1)} %get-tuple-element.81), channel_id=1, source_target_pairs={{0,8},{8,0},{16,24},{24,16},{1,9},{9,1},{17,25},{25,17},{2,10},{10... | collective-permute-start | bytes 1597448 | tf_op jit(solution)/shard_map/ppermute | solution.py:377
  51.7 18.4 %collective-permute-start.16 = (s16[1040,256]{1,0:T(8,128)(2,1)S(1)}, s16[1040,256]{1,0:T(8,128)(2,1)S(1)}, u32[]{:S(2)}, u32[]{:S(2)}) collective-permute-start(s16[1040,256]{1,0:T(8,128)(2,1)S(1)} %get-tuple-element.95), channel_id=1, source_target_pairs={{0,16},{8,24},{16,0},{24,8},{1,17},{9,25},{17,1},{25,9},{2,18},{10... | collective-permute-start | bytes 1597448 | tf_op jit(solution)/shard_map/ppermute | solution.py:377
  51.7 19.3 %collective-permute-start.15 = (s16[1040,256]{1,0:T(8,128)(2,1)S(1)}, s16[1040,256]{1,0:T(8,128)(2,1)S(1)}, u32[]{:S(2)}, u32[]{:S(2)}) collective-permute-start(s16[1040,256]{1,0:T(8,128)(2,1)S(1)} %get-tuple-element.86), channel_id=1, source_target_pairs={{0,8},{8,0},{16,24},{24,16},{1,9},{9,1},{17,25},{25,17},{2,10},{10... | collective-permute-start | bytes 1597448 | tf_op jit(solution)/shard_map/ppermute | solution.py:377
  55.3 26.8 %collective-permute-start.19 = (s16[1040,256]{1,0:T(8,128)(2,1)S(1)}, s16[1040,256]{1,0:T(8,128)(2,1)S(1)}, u32[]{:S(2)}, u32[]{:S(2)}) collective-permute-start(s16[1040,256]{1,0:T(8,128)(2,1)S(1)} %get-tuple-element.88), channel_id=1, source_target_pairs={{0,4},{1,5},{2,6},{3,7},{4,0},{5,1},{6,2},{7,3},{8,12},{9,13},{10,... | collective-permute-start | bytes 1597448 | tf_op jit(solution)/shard_map/ppermute | solution.py:380
  61.8 15.0 %collective-permute-start.18 = (s16[528,256]{1,0:T(8,128)(2,1)S(1)}, s16[528,256]{1,0:T(8,128)(2,1)S(1)}, u32[]{:S(2)}, u32[]{:S(2)}) collective-permute-start(s16[528,256]{1,0:T(8,128)(2,1)S(1)} %get-tuple-element.98), channel_id=1, source_target_pairs={{0,8},{8,0},{16,24},{24,16},{1,9},{9,1},{17,25},{25,17},{2,10},{10... | collective-permute-start | bytes 811016 | tf_op jit(solution)/shard_map/ppermute | solution.py:377
  61.9 15.0 %collective-permute-start.17 = (s16[528,256]{1,0:T(8,128)(2,1)S(1)}, s16[528,256]{1,0:T(8,128)(2,1)S(1)}, u32[]{:S(2)}, u32[]{:S(2)}) collective-permute-start(s16[528,256]{1,0:T(8,128)(2,1)S(1)} %get-tuple-element.93), channel_id=1, source_target_pairs={{0,16},{8,24},{16,0},{24,8},{1,17},{9,25},{17,1},{25,9},{2,18},{10... | collective-permute-start | bytes 811016 | tf_op jit(solution)/shard_map/ppermute | solution.py:377
  71.6 13.0 %collective-permute-start.21 = (s16[528,256]{1,0:T(8,128)(2,1)S(1)}, s16[528,256]{1,0:T(8,128)(2,1)S(1)}, u32[]{:S(2)}, u32[]{:S(2)}) collective-permute-start(s16[528,256]{1,0:T(8,128)(2,1)S(1)} %get-tuple-element.105), channel_id=1, source_target_pairs={{0,8},{8,0},{16,24},{24,16},{1,9},{9,1},{17,25},{25,17},{2,10},{10... | collective-permute-start | bytes 811016 | tf_op jit(solution)/shard_map/ppermute | solution.py:377
  72.8 11.8 %collective-permute-start.20 = (s16[528,256]{1,0:T(8,128)(2,1)S(1)}, s16[528,256]{1,0:T(8,128)(2,1)S(1)}, u32[]{:S(2)}, u32[]{:S(2)}) collective-permute-start(s16[528,256]{1,0:T(8,128)(2,1)S(1)} %get-tuple-element.96), channel_id=1, source_target_pairs={{0,16},{8,24},{16,0},{24,8},{1,17},{9,25},{17,1},{25,9},{2,18},{10... | collective-permute-start | bytes 811016 | tf_op jit(solution)/shard_map/ppermute | solution.py:377
  77.1 10.8 %collective-permute-start.22 = (s16[528,256]{1,0:T(8,128)(2,1)S(1)}, s16[528,256]{1,0:T(8,128)(2,1)S(1)}, u32[]{:S(2)}, u32[]{:S(2)}) collective-permute-start(s16[528,256]{1,0:T(8,128)(2,1)S(1)} %get-tuple-element.100), channel_id=1, source_target_pairs={{0,2},{1,3},{2,0},{3,1},{4,6},{5,7},{6,4},{7,5},{8,10},{9,11},{10,... | collective-permute-start | bytes 811016 | tf_op jit(solution)/shard_map/ppermute | solution.py:380
  84.8 11.2 %collective-permute-start.25 = (s16[528,256]{1,0:T(8,128)(2,1)S(1)}, s16[528,256]{1,0:T(8,128)(2,1)S(1)}, u32[]{:S(2)}, u32[]{:S(2)}) collective-permute-start(s16[528,256]{1,0:T(8,128)(2,1)S(1)} %get-tuple-element.107), channel_id=1, source_target_pairs={{0,2},{1,3},{2,0},{3,1},{4,6},{5,7},{6,4},{7,5},{8,10},{9,11},{10,... | collective-permute-start | bytes 811016 | tf_op jit(solution)/shard_map/ppermute | solution.py:380
  88.0 9.5 %collective-permute-start.26 = (s16[272,256]{1,0:T(8,128)(2,1)S(1)}, s16[272,256]{1,0:T(8,128)(2,1)S(1)}, u32[]{:S(2)}, u32[]{:S(2)}) collective-permute-start(s16[272,256]{1,0:T(8,128)(2,1)S(1)} %get-tuple-element.110), channel_id=1, source_target_pairs={{0,4},{1,5},{2,6},{3,7},{4,0},{5,1},{6,2},{7,3},{8,12},{9,13},{10,... | collective-permute-start | bytes 417800 | tf_op jit(solution)/shard_map/ppermute | solution.py:380
  92.7 10.3 %collective-permute-start.28 = (s16[528,256]{1,0:T(8,128)(2,1)S(1)}, s16[528,256]{1,0:T(8,128)(2,1)S(1)}, u32[]{:S(2)}, u32[]{:S(2)}) collective-permute-start(s16[528,256]{1,0:T(8,128)(2,1)S(1)} %get-tuple-element.120.refs_1_), channel_id=1, source_target_pairs={{0,8},{8,0},{16,24},{24,16},{1,9},{9,1},{17,25},{25,17},{2,10},{10... | collective-permute-start | bytes 811016 | tf_op jit(solution)/shard_map/ppermute | solution.py:377
  93.0 9.9 %collective-permute-start.27 = (s16[528,256]{1,0:T(8,128)(2,1)S(1)}, s16[528,256]{1,0:T(8,128)(2,1)S(1)}, u32[]{:S(2)}, u32[]{:S(2)}) collective-permute-start(s16[528,256]{1,0:T(8,128)(2,1)S(1)} %get-tuple-element.113.refs_0_), channel_id=1, source_target_pairs={{0,16},{8,24},{16,0},{24,8},{1,17},{9,25},{17,1},{25,9},{2,18},{10... | collective-permute-start | bytes 811016 | tf_op jit(solution)/shard_map/ppermute | solution.py:377
  97.6 10.0 %collective-permute-start.32 = (s16[272,256]{1,0:T(8,128)(2,1)S(1)}, s16[272,256]{1,0:T(8,128)(2,1)S(1)}, u32[]{:S(2)}, u32[]{:S(2)}) collective-permute-start(s16[272,256]{1,0:T(8,128)(2,1)S(1)} %finish.2.refs_0_), channel_id=1, source_target_pairs={{0,24},{8,16},{16,8},{24,0},{1,25},{9,17},{17,9},{25,1},{2,26},{10... | collective-permute-start | bytes 417800 | tf_op jit(solution)/shard_map/ppermute | solution.py:377
  (16 other events, 102.6 us)

commit v7 on v6

--- a/solution.py
+++ b/solution.py
@@ -548,7 +548,8 @@
                 to_line(sent_0, 0),
                 keep_0,
             )
-        keep[j] = kept()
+        else:
+            keep[j] = kept()
 
     def plane(j):
         return call(
@@ -571,6 +572,7 @@
         )
 
     *sent[1], keep[1] = plane(1)
+    keep[2] = kept()
     *sent[2], keep[2] = plane(2)
     sent[1], keep[1] = owner(1)
     pair_of = [coded(2)] * 2

time: 115 us -> 115 us (level)
  waiting for transfers between devices: 48.6 us -> 44.8 us
  Pallas kernels: 30.8 us -> 32.7 us
  starting transfers between devices: 34 us -> 35.9 us
    ppermute x6, waiting for transfers between devices: 11.3 us -> 7.6 us  [to_line(): return lax.ppermute(v, 'wide', [(i, i ^ 2 << b) for i in range(wide_count)])]
    ppermute x23, starting transfers between devices: 25.1 us -> 27.6 us  [to_grp(): return lax.ppermute(v, 'grp', [(i, i ^ d) for i in range(4)])]
    pallas_call x24, Pallas kernels: 30.8 us -> 32.7 us  [call(): pl.pallas_call(body, in_specs=more.pop('in_specs', in_any(1) + in_smem(sm...]
  transfers between devices with their start and end apart: 36 -> 36, of which waited for: 21 -> 21; matrix products, arithmetic and copies ran while one was open for 1% -> 1% of each run, Pallas kernels for 26% -> 27%
where the time goes in v7:
time: 115 us
  waiting for transfers between devices  44.8 us (39%)
  starting transfers between devices  35.9 us (31%)
  Pallas kernels  32.7 us (28%)
  local copies, waits for them, and re-layouts  1.18 us (1%)
    pallas_call x24, Pallas kernels, call(): pl.pallas_call(body, in_specs=more.pop('in_specs', in_any(1) + in_smem(sm...  32.7 us
    ppermute x23, waiting for transfers between devices, to_grp(): return lax.ppermute(v, 'grp', [(i, i ^ d) for i in range(4)])  31.7 us
    ppermute x23, starting transfers between devices, to_grp(): return lax.ppermute(v, 'grp', [(i, i ^ d) for i in range(4)])  27.6 us
    ppermute x6, waiting for transfers between devices, to_line(): return lax.ppermute(v, 'wide', [(i, i ^ 2 << b) for i in range(wide_count)])  7.6 us
    ppermute x6, starting transfers between devices, to_line(): return lax.ppermute(v, 'wide', [(i, i ^ 2 << b) for i in range(wide_count)])  7.16 us
    ppermute x7, waiting for transfers between devices, to_core(): return lax.ppermute(v, 'wide', [(i, i ^ 1) for i in range(wide_count)])  5.47 us
  transfers between devices with their start and end apart: 36, of which 21 were waited for; matrix products, arithmetic and copies ran while one was open for 1% of the time, Pallas kernels for 27%

profile of v7, /device:TPU:0, one launch (start us, length us, event | category | flops | bytes accessed | tf_op | source)
XLA Modules:
  0.0 115.1 jit_solution(16272791718558074367)
XLA Ops:
  1.8 2.6 %collective-permute-start.2 = (bf16[512,512]{1,0:T(8,128)(2,1)S(1)}, bf16[512,512]{1,0:T(8,128)(2,1)S(1)}, u32[]{:S(2)}, u32[]{:S(2)}) collective-permute-start(bf16[512,512]{1,0:T(8,128)(2,1)S(1)} %get-tuple-element.129), channel_id=1, source_target_pairs={{0,8},{8,0},{16,24},{24,16},{1,9},{9,1},{17,25},{25,17},{2,10},{10... | collective-permute-start | bytes 1572872 | tf_op jit(solution)/shard_map/ppermute | solution.py:377
  6.0 4.3 %collective-permute-done.sib_ref = s32[128]{0:T(128)S(1)} collective-permute-done((s32[128]{0:T(128)S(1)}, s32[128]{0:T(128)S(1)}, u32[]{:S(2)}, u32[]{:S(2)}) %collective-permute-start) | collective-permute-done | bytes 544 | tf_op jit(solution)/shard_map/ppermute | solution.py:374
  10.7 6.7 %hold.1 = (s32[3]{0:T(128)S(1)}, s32[104]{0:T(128)S(1)}, s32[104]{0:T(128)S(1)}, s32[104]{0:T(128)S(1)}, s32[208]{0:T(256)S(1)}, /*index=5*/s32[208]{0:T(256)S(1)}, bf16[104,256,256]{2,1,0:T(8,128)(2,1)S(1)}) custom-call(s32[1]{0:T(128)} %constant.8.clone.1.order, s32[128]{0:T(128)S(1)} %pad_add_fusion.own_ref, s32[128]{0:T(128)S(1)} %collective-permute-done.sib_ref, ...), custom_call_target="tpu_custom_call" | custom-call | bytes 12583936 | tf_op jit(solution)/shard_map/hold/pallas_call | solution.py:413
  17.5 6.5 %collective-permute-done.3.refs_1_ = bf16[512,512]{1,0:T(8,128)(2,1)S(1)} collective-permute-done((bf16[512,512]{1,0:T(8,128)(2,1)S(1)}, bf16[512,512]{1,0:T(8,128)(2,1)S(1)}, u32[]{:S(2)}, u32[]{:S(2)}) %collective-permute-start.3) | collective-permute-done | bytes 524320 | tf_op jit(solution)/shard_map/ppermute | solution.py:377
  26.5 3.2 %products_sent.3 = (s16[2064,256]{1,0:T(8,128)(2,1)S(1)}, bf16[16,256,256]{2,1,0:T(8,128)(2,1)S(1)}) custom-call(s32[1]{0:T(128)} %constant.8.clone.1.order, s32[3]{0:T(128)S(1)} %get-tuple-element.70.count_ref, s32[208]{0:T(256)S(1)} %get-tuple-element.71.order_ref, s32[104]{0:T(128)S(1)} %get-tuple-element.72.slot_ref, ...), custom_call_target="tpu_custom_call" | custom-call | bytes 16778892 | tf_op jit(solution)/shard_map/products_sent/pallas_call | solution.py:413
  29.7 2.1 %collective-permute-start.12 = (s16[2064,256]{1,0:T(8,128)(2,1)S(1)}, s16[2064,256]{1,0:T(8,128)(2,1)S(1)}, u32[]{:S(2)}, u32[]{:S(2)}) collective-permute-start(s16[2064,256]{1,0:T(8,128)(2,1)S(1)} %get-tuple-element.74), channel_id=1, source_target_pairs={{0,2},{1,3},{2,0},{3,1},{4,6},{5,7},{6,4},{7,5},{8,10},{9,11},{10,... | collective-permute-start | bytes 3170312 | tf_op jit(solution)/shard_map/ppermute | solution.py:380
  31.8 3.3 %products_kept.3.kept = f32[9,256,256]{2,1,0:T(8,128)S(1)} custom-call(s32[1]{0:T(128)} %constant.8.clone.1.order, s32[3]{0:T(128)S(1)} %get-tuple-element.70.count_ref, s32[208]{0:T(256)S(1)} %get-tuple-element.71.order_ref, s32[104]{0:T(128)S(1)} %get-tuple-element.72.slot_ref, s32[104]{0:T(128)S(1)} %get-tuple-element.73.label_ref, ...), custom_call_target="tpu_custom_call" | custom-call | bytes 15730316 | tf_op jit(solution)/shard_map/products_kept/pallas_call | solution.py:413
  35.1 3.5 %collective-permute-done.7.refs_2_ = bf16[1024,256]{1,0:T(8,128)(2,1)S(1)} collective-permute-done((bf16[1024,256]{1,0:T(8,128)(2,1)S(1)}, bf16[1024,256]{1,0:T(8,128)(2,1)S(1)}, u32[]{:S(2)}, u32[]{:S(2)}) %collective-permute-start.7) | collective-permute-done | bytes 524320 | tf_op jit(solution)/shard_map/ppermute | solution.py:377
  40.4 3.1 %products_sent.4 = (s16[1040,256]{1,0:T(8,128)(2,1)S(1)}, s16[1040,256]{1,0:T(8,128)(2,1)S(1)}, bf16[16,256,256]{2,1,0:T(8,128)(2,1)S(1)}) custom-call(s32[1]{0:T(128)} %constant.8.clone.1.order, s32[3]{0:T(128)S(1)} %get-tuple-element.70.count_ref, s32[208]{0:T(256)S(1)} %get-tuple-element.78.order_ref, s32[104]{0:T(128)S(1)} %get-tuple-element.79.slot_ref, ...), custom_call_target="tpu_custom_call" | custom-call | bytes 17303180 | tf_op jit(solution)/shard_map/products_sent/pallas_call | solution.py:413
  45.3 3.2 %products_kept.4.kept = f32[9,256,256]{2,1,0:T(8,128)S(1)} custom-call(s32[1]{0:T(128)} %constant.8.clone.1.order, s32[3]{0:T(128)S(1)} %get-tuple-element.70.count_ref, s32[208]{0:T(256)S(1)} %get-tuple-element.78.order_ref, s32[104]{0:T(128)S(1)} %get-tuple-element.79.slot_ref, s32[104]{0:T(128)S(1)} %get-tuple-element.73.label_ref, ...), custom_call_target="tpu_custom_call" | custom-call | bytes 15730316 | tf_op jit(solution)/shard_map/products_kept/pallas_call | solution.py:413
  48.5 3.1 %products_sent.5 = (s16[1040,256]{1,0:T(8,128)(2,1)S(1)}, s16[1040,256]{1,0:T(8,128)(2,1)S(1)}, bf16[16,256,256]{2,1,0:T(8,128)(2,1)S(1)}) custom-call(s32[1]{0:T(128)} %constant.8.clone.1.order, s32[3]{0:T(128)S(1)} %get-tuple-element.70.count_ref, s32[208]{0:T(256)S(1)} %get-tuple-element.78.order_ref, s32[104]{0:T(128)S(1)} %get-tuple-element.79.slot_ref, ...), custom_call_target="tpu_custom_call" | custom-call | bytes 17303180 | tf_op jit(solution)/shard_map/products_sent/pallas_call | solution.py:413
  52.8 2.2 %collective-permute-done.12.recv = s16[2064,256]{1,0:T(8,128)(2,1)S(1)} collective-permute-done((s16[2064,256]{1,0:T(8,128)(2,1)S(1)}, s16[2064,256]{1,0:T(8,128)(2,1)S(1)}, u32[]{:S(2)}, u32[]{:S(2)}) %collective-permute-start.12) | collective-permute-done | bytes 1056800 | tf_op jit(solution)/shard_map/ppermute | solution.py:380
  55.5 2.3 %collective-permute-start.19 = (s16[1040,256]{1,0:T(8,128)(2,1)S(1)}, s16[1040,256]{1,0:T(8,128)(2,1)S(1)}, u32[]{:S(2)}, u32[]{:S(2)}) collective-permute-start(s16[1040,256]{1,0:T(8,128)(2,1)S(1)} %get-tuple-element.88), channel_id=1, source_target_pairs={{0,4},{1,5},{2,6},{3,7},{4,0},{5,1},{6,2},{7,3},{8,12},{9,13},{10,... | collective-permute-start | bytes 1597448 | tf_op jit(solution)/shard_map/ppermute | solution.py:380
  62.0 3.4 %products_kept.5.kept = f32[9,256,256]{2,1,0:T(8,128)S(1)} custom-call(s32[1]{0:T(128)} %constant.8.clone.1.order, s32[3]{0:T(128)S(1)} %get-tuple-element.70.count_ref, s32[208]{0:T(256)S(1)} %get-tuple-element.78.order_ref, s32[104]{0:T(128)S(1)} %get-tuple-element.79.slot_ref, s32[104]{0:T(128)S(1)} %get-tuple-element.73.label_ref, ...), custom_call_target="tpu_custom_call" | custom-call | bytes 15730316 | tf_op jit(solution)/shard_map/products_kept/pallas_call | solution.py:413
  65.3 4.8 %collective-permute-done.16.recv_b = s16[1040,256]{1,0:T(8,128)(2,1)S(1)} collective-permute-done((s16[1040,256]{1,0:T(8,128)(2,1)S(1)}, s16[1040,256]{1,0:T(8,128)(2,1)S(1)}, u32[]{:S(2)}, u32[]{:S(2)}) %collective-permute-start.16) | collective-permute-done | bytes 532512 | tf_op jit(solution)/shard_map/ppermute | solution.py:377
  73.4 4.1 %collective-permute-done.18.recv_b = s16[528,256]{1,0:T(8,128)(2,1)S(1)} collective-permute-done((s16[528,256]{1,0:T(8,128)(2,1)S(1)}, s16[528,256]{1,0:T(8,128)(2,1)S(1)}, u32[]{:S(2)}, u32[]{:S(2)}) %collective-permute-start.18) | collective-permute-done | bytes 270368 | tf_op jit(solution)/shard_map/ppermute | solution.py:377
  78.7 2.3 %collective-permute-done.19.recv = s16[1040,256]{1,0:T(8,128)(2,1)S(1)} collective-permute-done((s16[1040,256]{1,0:T(8,128)(2,1)S(1)}, s16[1040,256]{1,0:T(8,128)(2,1)S(1)}, u32[]{:S(2)}, u32[]{:S(2)}) %collective-permute-start.19) | collective-permute-done | bytes 532512 | tf_op jit(solution)/shard_map/ppermute | solution.py:380
  81.3 2.5 %collective-permute-start.24 = (s16[528,256]{1,0:T(8,128)(2,1)S(1)}, s16[528,256]{1,0:T(8,128)(2,1)S(1)}, u32[]{:S(2)}, u32[]{:S(2)}) collective-permute-start(s16[528,256]{1,0:T(8,128)(2,1)S(1)} %get-tuple-element.112.own_b), channel_id=1, source_target_pairs={{0,16},{8,24},{16,0},{24,8},{1,17},{9,25},{17,1},{25,9},{2,18},{10... | collective-permute-start | bytes 811016 | tf_op jit(solution)/shard_map/ppermute | solution.py:377
  88.4 2.1 %collective-permute-done.24.recv_b = s16[528,256]{1,0:T(8,128)(2,1)S(1)} collective-permute-done((s16[528,256]{1,0:T(8,128)(2,1)S(1)}, s16[528,256]{1,0:T(8,128)(2,1)S(1)}, u32[]{:S(2)}, u32[]{:S(2)}) %collective-permute-start.24) | collective-permute-done | bytes 270368 | tf_op jit(solution)/shard_map/ppermute | solution.py:377
  92.3 1.6 %collective-permute-start.28 = (s16[528,256]{1,0:T(8,128)(2,1)S(1)}, s16[528,256]{1,0:T(8,128)(2,1)S(1)}, u32[]{:S(2)}, u32[]{:S(2)}) collective-permute-start(s16[528,256]{1,0:T(8,128)(2,1)S(1)} %get-tuple-element.120.refs_1_), channel_id=1, source_target_pairs={{0,8},{8,0},{16,24},{24,16},{1,9},{9,1},{17,25},{25,17},{2,10},{10... | collective-permute-start | bytes 811016 | tf_op jit(solution)/shard_map/ppermute | solution.py:377
  94.3 2.2 %collective-permute-done.25.recv = s16[528,256]{1,0:T(8,128)(2,1)S(1)} collective-permute-done((s16[528,256]{1,0:T(8,128)(2,1)S(1)}, s16[528,256]{1,0:T(8,128)(2,1)S(1)}, u32[]{:S(2)}, u32[]{:S(2)}) %collective-permute-start.25) | collective-permute-done | bytes 270368 | tf_op jit(solution)/shard_map/ppermute | solution.py:380
  96.9 6.0 %collective-permute-start.32 = (s16[272,256]{1,0:T(8,128)(2,1)S(1)}, s16[272,256]{1,0:T(8,128)(2,1)S(1)}, u32[]{:S(2)}, u32[]{:S(2)}) collective-permute-start(s16[272,256]{1,0:T(8,128)(2,1)S(1)} %finish.2.refs_0_), channel_id=1, source_target_pairs={{0,24},{8,16},{16,8},{24,0},{1,25},{9,17},{17,9},{25,1},{2,26},{10... | collective-permute-start | bytes 417800 | tf_op jit(solution)/shard_map/ppermute | solution.py:377
  104.7 2.9 %collective-permute-start.35 = (s16[272,256]{1,0:T(8,128)(2,1)S(1)}, s16[272,256]{1,0:T(8,128)(2,1)S(1)}, u32[]{:S(2)}, u32[]{:S(2)}) collective-permute-start(s16[272,256]{1,0:T(8,128)(2,1)S(1)} %finish.3.refs_0_), channel_id=1, source_target_pairs={{0,24},{8,16},{16,8},{24,0},{1,25},{9,17},{17,9},{25,1},{2,26},{10... | collective-permute-start | bytes 417800 | tf_op jit(solution)/shard_map/ppermute | solution.py:377
  108.3 2.6 %collective-permute-done.31.refs_2_ = s16[272,256]{1,0:T(8,128)(2,1)S(1)} collective-permute-done((s16[272,256]{1,0:T(8,128)(2,1)S(1)}, s16[272,256]{1,0:T(8,128)(2,1)S(1)}, u32[]{:S(2)}, u32[]{:S(2)}) %collective-permute-start.31) | collective-permute-done | bytes 139296 | tf_op jit(solution)/shard_map/ppermute | solution.py:377
  (83 shorter events, 34.1 us)
Async XLA Ops:
  0.0 10.6 %collective-permute-start.1 = (bf16[48,256,256]{2,1,0:T(8,128)(2,1)}, bf16[48,256,256]{2,1,0:T(8,128)(2,1)}, u32[]{:S(2)}, u32[]{:S(2)}) collective-permute-start(bf16[48,256,256]{2,1,0:T(8,128)(2,1)} %own_tiles.1), channel_id=1, source_target_pairs={{0,1},{1,0},{2,3},{3,2},{4,5},{5,4},{6,7},{7,6},{8,9},{9,8},{10,11... | collective-permute-start | bytes 18874376 | tf_op jit(solution)/shard_map/ppermute | solution.py:374
  1.8 15.6 %collective-permute-start.2 = (bf16[512,512]{1,0:T(8,128)(2,1)S(1)}, bf16[512,512]{1,0:T(8,128)(2,1)S(1)}, u32[]{:S(2)}, u32[]{:S(2)}) collective-permute-start(bf16[512,512]{1,0:T(8,128)(2,1)S(1)} %get-tuple-element.129), channel_id=1, source_target_pairs={{0,8},{8,0},{16,24},{24,16},{1,9},{9,1},{17,25},{25,17},{2,10},{10... | collective-permute-start | bytes 1572872 | tf_op jit(solution)/shard_map/ppermute | solution.py:377
  4.4 19.6 %collective-permute-start.3 = (bf16[512,512]{1,0:T(8,128)(2,1)S(1)}, bf16[512,512]{1,0:T(8,128)(2,1)S(1)}, u32[]{:S(2)}, u32[]{:S(2)}) collective-permute-start(bf16[512,512]{1,0:T(8,128)(2,1)S(1)} %get-tuple-element.128), channel_id=1, source_target_pairs={{0,16},{8,24},{16,0},{24,8},{1,17},{9,25},{17,1},{25,9},{2,18},{10... | collective-permute-start | bytes 1572872 | tf_op jit(solution)/shard_map/ppermute | solution.py:377
  5.9 18.2 %collective-permute-start.4 = (bf16[512,256]{1,0:T(8,128)(2,1)S(1)}, bf16[512,256]{1,0:T(8,128)(2,1)S(1)}, u32[]{:S(2)}, u32[]{:S(2)}) collective-permute-start(bf16[512,256]{1,0:T(8,128)(2,1)S(1)} %get-tuple-element.126), channel_id=1, source_target_pairs={{0,24},{8,16},{16,8},{24,0},{1,25},{9,17},{17,9},{25,1},{2,26},{10... | collective-permute-start | bytes 786440 | tf_op jit(solution)/shard_map/ppermute | solution.py:377
  24.2 14.3 %collective-permute-start.7 = (bf16[1024,256]{1,0:T(8,128)(2,1)S(1)}, bf16[1024,256]{1,0:T(8,128)(2,1)S(1)}, u32[]{:S(2)}, u32[]{:S(2)}) collective-permute-start(bf16[1024,256]{1,0:T(8,128)(2,1)S(1)} %join.3.refs_0_), channel_id=1, source_target_pairs={{0,16},{8,24},{16,0},{24,8},{1,17},{9,25},{17,1},{25,9},{2,18},{10... | collective-permute-start | bytes 1572872 | tf_op jit(solution)/shard_map/ppermute | solution.py:377
  25.8 14.0 %collective-permute-start.10 = (bf16[1024,256]{1,0:T(8,128)(2,1)S(1)}, bf16[1024,256]{1,0:T(8,128)(2,1)S(1)}, u32[]{:S(2)}, u32[]{:S(2)}) collective-permute-start(bf16[1024,256]{1,0:T(8,128)(2,1)S(1)} %join.4.refs_0_), channel_id=1, source_target_pairs={{0,8},{8,0},{16,24},{24,16},{1,9},{9,1},{17,25},{25,17},{2,10},{10... | collective-permute-start | bytes 1572872 | tf_op jit(solution)/shard_map/ppermute | solution.py:377
  29.7 25.3 %collective-permute-start.12 = (s16[2064,256]{1,0:T(8,128)(2,1)S(1)}, s16[2064,256]{1,0:T(8,128)(2,1)S(1)}, u32[]{:S(2)}, u32[]{:S(2)}) collective-permute-start(s16[2064,256]{1,0:T(8,128)(2,1)S(1)} %get-tuple-element.74), channel_id=1, source_target_pairs={{0,2},{1,3},{2,0},{3,1},{4,6},{5,7},{6,4},{7,5},{8,10},{9,11},{10,... | collective-permute-start | bytes 3170312 | tf_op jit(solution)/shard_map/ppermute | solution.py:380
  38.5 9.9 %collective-permute-start.9 = (bf16[1024,256]{1,0:T(8,128)(2,1)S(1)}, bf16[1024,256]{1,0:T(8,128)(2,1)S(1)}, u32[]{:S(2)}, u32[]{:S(2)}) collective-permute-start(bf16[1024,256]{1,0:T(8,128)(2,1)S(1)} %join.4.refs_0_), channel_id=1, source_target_pairs={{0,1},{1,0},{2,3},{3,2},{4,5},{5,4},{6,7},{7,6},{8,9},{9,8},{10,11... | collective-permute-start | bytes 1572872 | tf_op jit(solution)/shard_map/ppermute | solution.py:374
  43.6 15.1 %collective-permute-start.14 = (s16[1040,256]{1,0:T(8,128)(2,1)S(1)}, s16[1040,256]{1,0:T(8,128)(2,1)S(1)}, u32[]{:S(2)}, u32[]{:S(2)}) collective-permute-start(s16[1040,256]{1,0:T(8,128)(2,1)S(1)} %get-tuple-element.90), channel_id=1, source_target_pairs={{0,16},{8,24},{16,0},{24,8},{1,17},{9,25},{17,1},{25,9},{2,18},{10... | collective-permute-start | bytes 1597448 | tf_op jit(solution)/shard_map/ppermute | solution.py:377
  45.2 15.0 %collective-permute-start.13 = (s16[1040,256]{1,0:T(8,128)(2,1)S(1)}, s16[1040,256]{1,0:T(8,128)(2,1)S(1)}, u32[]{:S(2)}, u32[]{:S(2)}) collective-permute-start(s16[1040,256]{1,0:T(8,128)(2,1)S(1)} %get-tuple-element.81), channel_id=1, source_target_pairs={{0,8},{8,0},{16,24},{24,16},{1,9},{9,1},{17,25},{25,17},{2,10},{10... | collective-permute-start | bytes 1597448 | tf_op jit(solution)/shard_map/ppermute | solution.py:377
  51.6 18.5 %collective-permute-start.16 = (s16[1040,256]{1,0:T(8,128)(2,1)S(1)}, s16[1040,256]{1,0:T(8,128)(2,1)S(1)}, u32[]{:S(2)}, u32[]{:S(2)}) collective-permute-start(s16[1040,256]{1,0:T(8,128)(2,1)S(1)} %get-tuple-element.95), channel_id=1, source_target_pairs={{0,16},{8,24},{16,0},{24,8},{1,17},{9,25},{17,1},{25,9},{2,18},{10... | collective-permute-start | bytes 1597448 | tf_op jit(solution)/shard_map/ppermute | solution.py:377
  51.9 19.8 %collective-permute-start.15 = (s16[1040,256]{1,0:T(8,128)(2,1)S(1)}, s16[1040,256]{1,0:T(8,128)(2,1)S(1)}, u32[]{:S(2)}, u32[]{:S(2)}) collective-permute-start(s16[1040,256]{1,0:T(8,128)(2,1)S(1)} %get-tuple-element.86), channel_id=1, source_target_pairs={{0,8},{8,0},{16,24},{24,16},{1,9},{9,1},{17,25},{25,17},{2,10},{10... | collective-permute-start | bytes 1597448 | tf_op jit(solution)/shard_map/ppermute | solution.py:377
  55.5 25.5 %collective-permute-start.19 = (s16[1040,256]{1,0:T(8,128)(2,1)S(1)}, s16[1040,256]{1,0:T(8,128)(2,1)S(1)}, u32[]{:S(2)}, u32[]{:S(2)}) collective-permute-start(s16[1040,256]{1,0:T(8,128)(2,1)S(1)} %get-tuple-element.88), channel_id=1, source_target_pairs={{0,4},{1,5},{2,6},{3,7},{4,0},{5,1},{6,2},{7,3},{8,12},{9,13},{10,... | collective-permute-start | bytes 1597448 | tf_op jit(solution)/shard_map/ppermute | solution.py:380
  60.8 16.6 %collective-permute-start.18 = (s16[528,256]{1,0:T(8,128)(2,1)S(1)}, s16[528,256]{1,0:T(8,128)(2,1)S(1)}, u32[]{:S(2)}, u32[]{:S(2)}) collective-permute-start(s16[528,256]{1,0:T(8,128)(2,1)S(1)} %get-tuple-element.98), channel_id=1, source_target_pairs={{0,8},{8,0},{16,24},{24,16},{1,9},{9,1},{17,25},{25,17},{2,10},{10... | collective-permute-start | bytes 811016 | tf_op jit(solution)/shard_map/ppermute | solution.py:377
  60.9 16.6 %collective-permute-start.17 = (s16[528,256]{1,0:T(8,128)(2,1)S(1)}, s16[528,256]{1,0:T(8,128)(2,1)S(1)}, u32[]{:S(2)}, u32[]{:S(2)}) collective-permute-start(s16[528,256]{1,0:T(8,128)(2,1)S(1)} %get-tuple-element.91), channel_id=1, source_target_pairs={{0,16},{8,24},{16,0},{24,8},{1,17},{9,25},{17,1},{25,9},{2,18},{10... | collective-permute-start | bytes 811016 | tf_op jit(solution)/shard_map/ppermute | solution.py:377
  72.2 13.2 %collective-permute-start.21 = (s16[528,256]{1,0:T(8,128)(2,1)S(1)}, s16[528,256]{1,0:T(8,128)(2,1)S(1)}, u32[]{:S(2)}, u32[]{:S(2)}) collective-permute-start(s16[528,256]{1,0:T(8,128)(2,1)S(1)} %get-tuple-element.105), channel_id=1, source_target_pairs={{0,8},{8,0},{16,24},{24,16},{1,9},{9,1},{17,25},{25,17},{2,10},{10... | collective-permute-start | bytes 811016 | tf_op jit(solution)/shard_map/ppermute | solution.py:377
  72.3 13.1 %collective-permute-start.20 = (s16[528,256]{1,0:T(8,128)(2,1)S(1)}, s16[528,256]{1,0:T(8,128)(2,1)S(1)}, u32[]{:S(2)}, u32[]{:S(2)}) collective-permute-start(s16[528,256]{1,0:T(8,128)(2,1)S(1)} %get-tuple-element.96), channel_id=1, source_target_pairs={{0,16},{8,24},{16,0},{24,8},{1,17},{9,25},{17,1},{25,9},{2,18},{10... | collective-permute-start | bytes 811016 | tf_op jit(solution)/shard_map/ppermute | solution.py:377
  77.7 9.0 %collective-permute-start.22 = (s16[528,256]{1,0:T(8,128)(2,1)S(1)}, s16[528,256]{1,0:T(8,128)(2,1)S(1)}, u32[]{:S(2)}, u32[]{:S(2)}) collective-permute-start(s16[528,256]{1,0:T(8,128)(2,1)S(1)} %get-tuple-element.100), channel_id=1, source_target_pairs={{0,2},{1,3},{2,0},{3,1},{4,6},{5,7},{6,4},{7,5},{8,10},{9,11},{10,... | collective-permute-start | bytes 811016 | tf_op jit(solution)/shard_map/ppermute | solution.py:380
  81.3 9.2 %collective-permute-start.24 = (s16[528,256]{1,0:T(8,128)(2,1)S(1)}, s16[528,256]{1,0:T(8,128)(2,1)S(1)}, u32[]{:S(2)}, u32[]{:S(2)}) collective-permute-start(s16[528,256]{1,0:T(8,128)(2,1)S(1)} %get-tuple-element.112.own_b), channel_id=1, source_target_pairs={{0,16},{8,24},{16,0},{24,8},{1,17},{9,25},{17,1},{25,9},{2,18},{10... | collective-permute-start | bytes 811016 | tf_op jit(solution)/shard_map/ppermute | solution.py:377
  85.7 10.9 %collective-permute-start.25 = (s16[528,256]{1,0:T(8,128)(2,1)S(1)}, s16[528,256]{1,0:T(8,128)(2,1)S(1)}, u32[]{:S(2)}, u32[]{:S(2)}) collective-permute-start(s16[528,256]{1,0:T(8,128)(2,1)S(1)} %get-tuple-element.107), channel_id=1, source_target_pairs={{0,2},{1,3},{2,0},{3,1},{4,6},{5,7},{6,4},{7,5},{8,10},{9,11},{10,... | collective-permute-start | bytes 811016 | tf_op jit(solution)/shard_map/ppermute | solution.py:380
  86.9 9.9 %collective-permute-start.26 = (s16[272,256]{1,0:T(8,128)(2,1)S(1)}, s16[272,256]{1,0:T(8,128)(2,1)S(1)}, u32[]{:S(2)}, u32[]{:S(2)}) collective-permute-start(s16[272,256]{1,0:T(8,128)(2,1)S(1)} %get-tuple-element.110), channel_id=1, source_target_pairs={{0,4},{1,5},{2,6},{3,7},{4,0},{5,1},{6,2},{7,3},{8,12},{9,13},{10,... | collective-permute-start | bytes 417800 | tf_op jit(solution)/shard_map/ppermute | solution.py:380
  92.3 10.6 %collective-permute-start.28 = (s16[528,256]{1,0:T(8,128)(2,1)S(1)}, s16[528,256]{1,0:T(8,128)(2,1)S(1)}, u32[]{:S(2)}, u32[]{:S(2)}) collective-permute-start(s16[528,256]{1,0:T(8,128)(2,1)S(1)} %get-tuple-element.120.refs_1_), channel_id=1, source_target_pairs={{0,8},{8,0},{16,24},{24,16},{1,9},{9,1},{17,25},{25,17},{2,10},{10... | collective-permute-start | bytes 811016 | tf_op jit(solution)/shard_map/ppermute | solution.py:377
  94.0 9.6 %collective-permute-start.27 = (s16[528,256]{1,0:T(8,128)(2,1)S(1)}, s16[528,256]{1,0:T(8,128)(2,1)S(1)}, u32[]{:S(2)}, u32[]{:S(2)}) collective-permute-start(s16[528,256]{1,0:T(8,128)(2,1)S(1)} %get-tuple-element.113.refs_0_), channel_id=1, source_target_pairs={{0,16},{8,24},{16,0},{24,8},{1,17},{9,25},{17,1},{25,9},{2,18},{10... | collective-permute-start | bytes 811016 | tf_op jit(solution)/shard_map/ppermute | solution.py:377
  96.9 10.8 %collective-permute-start.32 = (s16[272,256]{1,0:T(8,128)(2,1)S(1)}, s16[272,256]{1,0:T(8,128)(2,1)S(1)}, u32[]{:S(2)}, u32[]{:S(2)}) collective-permute-start(s16[272,256]{1,0:T(8,128)(2,1)S(1)} %finish.2.refs_0_), channel_id=1, source_target_pairs={{0,24},{8,16},{16,8},{24,0},{1,25},{9,17},{17,9},{25,1},{2,26},{10... | collective-permute-start | bytes 417800 | tf_op jit(solution)/shard_map/ppermute | solution.py:377
  (16 other events, 104.6 us)
